TPU v7x, 32 devices: a whole 2x2x4 slice. The times are simulated.
32 devices in a mesh: seq: 8 (over y, x, core), tp: 4 (over z).
Axes of the slice: x: 2, y: 2, z: 4, core: 2. Of those that a mesh axis runs over, the one named last changes fastest.
Arguments:
- tokens: bfloat16 [4096, 2048], P('seq'), may hold values from -6 to 6
- w_zx: float32 [2048, 8192], P(('seq', 'tp')), may hold values from -0.125 to 0.125
- w_dt: float32 [2048, 64], P(('seq', 'tp')), may hold values from -0.26516503 to 0.26516503
- w_bc: float32 [2048, 256], P(('seq', 'tp')), may hold values from -0.125 to 0.125
- conv_x_weight: float32 [4, 4096], P(None, 'tp'), may hold values from -3 to 3
- conv_x_bias: float32 [4096], P('tp'), may hold values from -1.8 to 1.8
- conv_bc_weight: float32 [4, 256], replicated, may hold values from -3 to 3
- conv_bc_bias: float32 [256], replicated, may hold values from -1.8 to 1.8
- dt_bias: float32 [64], P('tp'), may hold values from -11 to -2
- a_log: float32 [64], P('tp'), may hold values from 0 to 2.77
- skip: float32 [64], P('tp'), may hold values from 0.5 to 2
- norm_weight: float32 [4096], P('tp'), may hold values from 0.1 to 1.9
- w_out: float32 [4096, 2048], P('tp', 'seq'), may hold values from -0.09375 to 0.09375
- lengths: int32 [8], replicated, may hold values from 1 to 2048, 4096 in all
- request_group: int32 [16], replicated, may hold values from 0 to 15
Outputs:
- mixed: bfloat16 [4096, 2048], P(('seq', 'tp'))
- request_states: float32 [16, 64, 64, 128], P('seq', 'tp')
Inputs may be any that keep to these rules, and one draw needn't show every extreme that they name: 8 prompts packed end to end in this order; the lengths sum to 4096 and the longest is exactly 2048.
All inputs are finite; a program needn't handle non-finite values.
Results may differ from a plain program's by a relative error of at most 0.011.
Values may be sent and summed in bfloat16 or wider, within the bound.
No kernel may reach another device: no remote copies, remote signals or barrier semaphores. Data moves between devices by JAX's collectives and lax.ppermute only.
A program may use at most 128 MiB of HBM per device.

v0:
```python
import functools

import jax
import jax.numpy as jnp
from jax import lax
from jax.experimental import pallas as pl
from jax.experimental.pallas import tpu as pltpu
from jax.sharding import PartitionSpec as P

GROUP = 256
HALO = 16
LANES = 128
TERMS = 32
MM = jnp.bfloat16
F32 = jnp.float32
NEGATIVE = -1e30
sds = jax.ShapeDtypeStruct
VMEM_BYTES = 20 * 1024 * 1024

epsilon = 1e-05

ANY = pl.BlockSpec(memory_space=pl.ANY)
SMEM = pl.BlockSpec(memory_space=pltpu.SMEM)
VMEM = pl.BlockSpec(memory_space=pltpu.VMEM)


def flip(x, bits):
    count = lax.axis_size("seq")
    return lax.ppermute(x, "seq", [(i, i ^ bits) for i in range(count)])


def shift(x, by):
    count = lax.axis_size("tp")
    return lax.ppermute(x, "tp", [(i, (i + by) % count) for i in range(count)])


def plane_near(block):
    chips = lax.axis_size("seq") // 2
    return {k: (block if k == 0 else flip(block, 2 * k),) for k in range(chips) if k & (k - 1) == 0}


def plane_far(blocks):
    chips = lax.axis_size("seq") // 2
    blocks = dict(blocks)

    def half(k, side):
        if len(blocks[k]) == 2:
            return blocks[k][side]
        size = blocks[k][0].shape[0] // 2
        return blocks[k][0][side * size : (side + 1) * size]

    for k in range(1, chips):
        if k not in blocks:
            low = k & -k
            high = 1 << (k.bit_length() - 1)
            first = flip(half(k ^ low, 0), 2 * low)
            second = flip(half(k ^ high, 1), 2 * high)
            blocks[k] = (first, second)
    return blocks


def call(kernel, outs, in_specs, scratch=(), flops=0, moved=0, out_specs=None, name=None):
    return pl.pallas_call(
        kernel,
        out_shape=outs,
        in_specs=in_specs,
        out_specs=[VMEM] * len(outs) if out_specs is None else out_specs,
        scratch_shapes=list(scratch),
        compiler_params=pltpu.CompilerParams(vmem_limit_bytes=VMEM_BYTES),
        cost_estimate=pl.CostEstimate(flops=flops, bytes_accessed=moved, transcendentals=0),
        name=name,
    )


def split_terms(x):
    high = x.astype(MM).astype(F32)
    rest = x - high
    mid = rest.astype(MM).astype(F32)
    return high, mid, (rest - mid).astype(MM).astype(F32)


def silu(x):
    half = 0.5 * x
    return half + half * jnp.tanh(half)


def run_all(copies):
    for copy in copies:
        copy.start()
    for copy in copies:
        copy.wait()


def starts_of(position, ints):
    start, end = jnp.zeros_like(position), 0
    for i in range(ints.prompts):
        end = end + ints.ref[3 + i]
        start = jnp.where(position >= end, end, start)
    return start


class Ints:
    def __init__(self, ref, prompts):
        self.ref, self.prompts = ref, prompts
        self.t, self.p, self.c = ref[0], ref[1], ref[2]

    def wanted(self, i):
        return self.ref[3 + self.prompts + i]


def rows_at(first, size):
    return pl.ds(pl.multiple_of(first, 16), size)


def pack_x_kernel(tp_count, ints, w_ref, bc_ref, dt_ref, *outs):
    t = ints[0]
    pair = w_ref.shape[1] // tp_count
    inner = pair // 2
    bc_width = bc_ref.shape[1]
    heads = dt_ref.shape[1] // tp_count
    low_bc = bc_ref[...].astype(MM)
    for j, out in enumerate(outs):
        owner = lax.rem(t + j, tp_count)
        at = pl.multiple_of(owner * pair, LANES)
        out[:, :inner] = w_ref[:, pl.ds(at, inner)].astype(MM)
        out[:, inner : inner + bc_width] = low_bc
        steps = jnp.zeros((dt_ref.shape[0], heads), F32)
        for u in range(tp_count):
            steps = jnp.where(owner == u, dt_ref[:, u * heads : (u + 1) * heads], steps)
        steps = jnp.concatenate(
            [steps, jnp.zeros((dt_ref.shape[0], LANES - heads), F32)], axis=1
        )
        out[:, inner + bc_width : inner + bc_width + LANES] = steps.astype(MM)
        at = pl.multiple_of(owner * pair + inner, LANES)
        out[:, inner + bc_width + LANES :] = w_ref[:, pl.ds(at, inner)].astype(MM)


def pack_z_kernel(tp_count, ints, w_ref, *outs):
    pair = w_ref.shape[1] // tp_count
    for j, out in enumerate(outs):
        at = pl.multiple_of(lax.rem(ints[0] + j, tp_count) * pair, LANES)
        out[...] = w_ref[:, pl.ds(at, pair)].astype(MM)


def assemble_x_kernel(tp_count, ints, *refs):
    pieces, out = refs[:tp_count], refs[tp_count]
    rows = pieces[0].shape[0]
    for j, piece in enumerate(pieces):
        source = lax.rem(ints[0] + tp_count - j, tp_count)
        out[rows_at(source * rows, rows), :] = piece[...]


def assemble_z_kernel(tp_count, ints, *refs):
    pieces, (mine, theirs) = refs[:tp_count], refs[tp_count:]
    rows, inner = pieces[0].shape[0], mine.shape[1]
    c = ints[2]
    for j, piece in enumerate(pieces):
        at = rows_at(lax.rem(ints[0] + tp_count - j, tp_count) * rows, rows)
        mine[at, :] = piece[:, pl.ds(pl.multiple_of(c * inner, LANES), inner)]
        theirs[at, :] = piece[:, pl.ds(pl.multiple_of((1 - c) * inner, LANES), inner)]


def merge_kernel(ints, mine, theirs, out):
    rows = mine.shape[0]
    out[rows_at(ints[2] * rows, rows), :] = mine[...]
    out[rows_at((1 - ints[2]) * rows, rows), :] = theirs[...]


def lane_row(ref, first, count):
    lane = lax.broadcasted_iota(jnp.int32, (1, LANES), 1)
    row = jnp.zeros((1, LANES), F32)
    for i in range(count):
        row = jnp.where(lane == i, ref[first + i], row)
    return row


def front_kernel(sizes, ints_ref, floats, vecs, tok_ref, *refs):
    inner, bc_width, heads, prompts, where, depth, groups, side = sizes
    ints = Ints(ints_ref, prompts)
    c = ints.c
    conv = inner + bc_width
    state = bc_width // 2
    head_width = inner // heads
    half = groups // 2
    if where:
        pieces = refs[: len(where)]
        xs_ref, bc_ref, cum_ref, step_ref, message, weights, raw, sems = refs[len(where) :]
        start_x = pl.multiple_of(c * (conv + LANES), LANES)
        copies = []
        for piece, (k, other, first) in zip(pieces, where):
            core = 1 - c if other else c
            rows = rows_at(((ints.p ^ k) * 2 + core) * depth + first, piece.shape[0])
            for source, goal, size in ((start_x, 0, inner), (inner, inner, bc_width + LANES)):
                copies.append(
                    pltpu.make_async_copy(
                        piece.at[:, pl.ds(source, size)],
                        weights.at[rows, pl.ds(goal, size)],
                        sems.at[len(copies)],
                    )
                )
        run_all(copies)
    else:
        weights, xs_ref, bc_ref, cum_ref, step_ref, message, raw = refs
    taps = 4
    lower = (
        lax.broadcasted_iota(jnp.int32, (GROUP, GROUP), 0)
        >= lax.broadcasted_iota(jnp.int32, (GROUP, GROUP), 1)
    ).astype(F32)
    within = lax.broadcasted_iota(jnp.int32, (GROUP, LANES), 0)
    base = ints.p * (groups * GROUP) + side * half * GROUP
    all_heads = 2 * heads
    bias = lane_row(floats, c * heads, heads)
    rate = -jnp.exp(lane_row(floats, all_heads + c * heads, heads))

    def project(g):
        at = (side * half + g) * GROUP
        value = jnp.dot(
            tok_ref[at : at + GROUP + HALO, :], weights[...], preferred_element_type=F32
        )
        raw[g % 2, :, :conv] = value[:, :conv].astype(MM).astype(F32)
        raw[g % 2, :, conv:] = value[:, conv:]

    def one(g):
        rows = slice(g * GROUP, (g + 1) * GROUP)
        slot = g % 2
        first = base + g * GROUP
        position = first + within
        behind = position - starts_of(position, ints)
        keeps = [(behind >= lag).astype(F32) for lag in range(1, taps)]
        dt = raw[slot, HALO : HALO + GROUP, conv:]
        dt = jnp.where(c == 0, dt, pltpu.roll(dt, LANES - heads, 1)) + bias
        step = jnp.maximum(dt, 0.0) + jnp.log1p(jnp.exp(-jnp.abs(dt)))
        cum = jnp.dot(
            lower, step * rate, precision=lax.Precision.HIGHEST, preferred_element_type=F32
        )
        cum_ref[rows, :] = cum
        step_ref[rows, :] = step
        last = cum[GROUP - 1 : GROUP, :]
        start_last = starts_of(first + (GROUP - 1), ints)
        tail = jnp.where(position >= start_last, jnp.exp(last - cum), 0.0) * step
        for block in range(0, conv, LANES):
            lanes = slice(block, block + LANES)
            if block < inner:
                here = pl.ds(pl.multiple_of(c * inner + block, LANES), LANES)
                weight, offset = vecs[0:taps, here], vecs[taps : taps + 1, here]
            else:
                here = slice(block - inner, block - inner + LANES)
                weight, offset = vecs[8 : 8 + taps, here], vecs[8 + taps : 9 + taps, here]
            total = offset + raw[slot, HALO : HALO + GROUP, lanes] * weight[taps - 1 : taps]
            for lag in range(1, taps):
                term = raw[slot, HALO - lag : HALO - lag + GROUP, lanes] * keeps[lag - 1]
                total = total + term * weight[taps - 1 - lag : taps - lag]
            value = silu(total).astype(MM)
            if block < inner:
                xs_ref[rows, lanes] = value
            else:
                bc_ref[rows, here] = value
        b_wide = bc_ref[rows, :state].astype(F32)
        for h in range(0, heads, 2):
            weighted = jnp.concatenate(
                [(b_wide * tail[:, h + i : h + i + 1]).astype(MM) for i in range(2)], axis=1
            )
            both = lax.dot_general(
                xs_ref[rows, h * head_width : (h + 2) * head_width],
                weighted,
                (((0,), (0,)), ((), ())),
                preferred_element_type=F32,
            )
            at = h * head_width
            message[g, at : at + head_width, :] = both[:head_width, :state].astype(MM)
            at = at + head_width
            message[g, at : at + head_width, :] = both[head_width:, state:].astype(MM)
        spread = jnp.broadcast_to(jnp.exp(last), (8, LANES))
        diagonal = lax.broadcasted_iota(jnp.int32, (8, LANES), 0) == lax.broadcasted_iota(
            jnp.int32, (8, LANES), 1
        )
        gates = jnp.sum(jnp.where(diagonal, spread, 0.0), axis=1, keepdims=True)
        gates = jnp.where(start_last < first, jnp.broadcast_to(gates, (8, LANES)), 0.0)
        terms = jnp.concatenate(list(split_terms(gates)) + [jnp.zeros_like(gates)], axis=0)
        message[g, inner : inner + TERMS, :] = terms.astype(MM)

    project(0)
    for g in range(half):
        if g + 1 < half:
            project(g + 1)
        one(g)


def mid_kernel(sizes, ints_ref, floats, xs_ref, bc_ref, cum_ref, step_ref, y_ref, keep_ref):
    inner, heads, prompts, groups, side = sizes
    ints = Ints(ints_ref, prompts)
    state = bc_ref.shape[1] // 2
    head_width = inner // heads
    half = groups // 2
    base = ints.p * (groups * GROUP) + side * half * GROUP
    within_i = lax.broadcasted_iota(jnp.int32, (GROUP, GROUP), 0)
    within_j = lax.broadcasted_iota(jnp.int32, (GROUP, GROUP), 1)
    lane = lax.broadcasted_iota(jnp.int32, (GROUP, LANES), 1)
    skip_at = 4 * heads + ints.c * heads

    @pl.loop(0, half)
    def _(g):
        rows = rows_at(g * GROUP, GROUP)
        first = base + g * GROUP
        start = starts_of(first + within_i, ints)
        seen = (within_j <= within_i) & (first + within_j >= start)
        scores = lax.dot_general(
            bc_ref[rows, state:],
            bc_ref[rows, :state],
            (((1,), (1,)), ((), ())),
            preferred_element_type=F32,
        )
        cum = cum_ref[rows, :]
        cum_t = cum.T
        step_t = step_ref[rows, :].T
        keep = jnp.where(start[:, :LANES] < first, jnp.exp(cum), 0.0)
        for h in range(0, heads, 2):
            lanes = slice(h * head_width, (h + 2) * head_width)
            pair = xs_ref[rows, lanes]
            first_skip, second_skip = (floats[skip_at + h + i] for i in range(2))
            total = jnp.where(lane < head_width, first_skip, second_skip) * pair.astype(F32)
            for i in range(2):
                log_decay = cum[:, h + i : h + i + 1] - cum_t[h + i : h + i + 1, :]
                decay = jnp.exp(jnp.where(seen, log_decay, NEGATIVE))
                mix = (decay * scores * step_t[h + i : h + i + 1, :]).astype(MM)
                own = jnp.where((lane < head_width) == (i == 0), pair, jnp.zeros_like(pair))
                total = total + jnp.dot(mix, own, preferred_element_type=F32)
            y_ref[rows, lanes] = total
            keep_ref[rows, lanes] = jnp.where(
                lane < head_width, keep[:, h : h + 1], keep[:, h + 1 : h + 2]
            )


def gate_kernel(where, depth, last, ints, tok_ref, *refs):
    pieces, refs = refs[: len(where)], refs[len(where) :]
    before, outs = (refs[:2], refs[2:]) if last else ((None, None), refs)
    count = outs[0].shape[0] // GROUP
    for side, (earlier, out) in enumerate(zip(before, outs)):

        @pl.loop(0, count)
        def _(g):
            rows = rows_at(g * GROUP, GROUP)
            total = earlier[rows, :] if last else 0.0
            for piece, (k, first) in zip(pieces, where):
                columns = pl.ds(
                    pl.multiple_of((ints[1] ^ k) * depth + first, LANES), piece.shape[0]
                )
                total = total + jnp.dot(
                    tok_ref[rows_at((side * count + g) * GROUP + HALO, GROUP), columns],
                    piece[...],
                    preferred_element_type=F32,
                )
            out[rows, :] = silu(total.astype(MM).astype(F32)) if last else total


def gating(sizes, ints, low_states, vecs, side, y_ref, keep_ref, gate_ref, bc_ref, out):
    inner, heads, groups = sizes
    half = groups // 2
    state = bc_ref.shape[1] // 2
    lane = lax.broadcasted_iota(jnp.int32, (GROUP, LANES), 1)
    for g in range(half):
        rows = slice(g * GROUP, (g + 1) * GROUP)
        carried = lax.dot_general(
            bc_ref[rows, state:],
            low_states[side * half + g],
            (((1,), (1,)), ((), ())),
            preferred_element_type=F32,
        )
        squares = jnp.zeros((GROUP, LANES), F32)
        for at in range(0, inner, LANES):
            lanes = slice(at, at + LANES)
            y = y_ref[rows, lanes] + carried[:, lanes] * keep_ref[rows, lanes]
            gated = y * gate_ref[rows, lanes]
            squares = squares + gated * gated
            here = pl.ds(pl.multiple_of(ints[2] * inner + at, LANES), LANES)
            out[rows, lanes] = (gated * vecs[5:6, here]).astype(MM)
        total = jnp.broadcast_to(jnp.sum(squares, axis=1, keepdims=True), (GROUP, LANES))
        out[rows, inner:] = spread_terms(total).astype(MM)


def spread_terms(total):
    lane = lax.broadcasted_iota(jnp.int32, total.shape, 1)
    high, mid, low = split_terms(total)
    return jnp.where(lane == 0, high, jnp.where(lane == 1, mid, jnp.where(lane == 2, low, 0.0)))


def added_terms(ref, at):
    value = ref[:, at:].astype(F32)
    return jnp.broadcast_to(jnp.sum(value, axis=1, keepdims=True), value.shape)


def back_kernel(sizes, ints_ref, vecs, *refs):
    inner, heads, prompts, groups, n_pieces, per = sizes
    pieces = refs[:n_pieces]
    sides = (refs[n_pieces : n_pieces + 4], refs[n_pieces + 4 : n_pieces + 8])
    theirs, low_states, asked, own_asked, parts, states, sems = refs[n_pieces + 8 :]
    ints = Ints(ints_ref, prompts)
    p, c = ints.p, ints.c
    head_width = inner // heads
    half = groups // 2
    copies = []
    for i, piece in enumerate(pieces):
        k, side = i // 2, i % 2
        at = (p ^ k) * groups + side * half
        copies.append(pltpu.make_async_copy(piece, parts.at[pl.ds(at, half)], sems.at[i]))
    run_all(copies)
    blocks = parts.shape[0]
    states[0] = jnp.zeros(states.shape[1:], F32)

    @pl.loop(0, blocks)
    def _(b):
        terms = parts[b, inner : inner + TERMS, :].astype(F32)
        gates = terms[0:8] + terms[8:16] + terms[16:24]
        for h in range(heads):
            rows = slice(h * head_width, (h + 1) * head_width)
            states[b + 1, rows, :] = gates[h : h + 1, :] * states[b, rows, :] + parts[
                b, rows, :
            ].astype(F32)

    for g in range(groups):
        low_states[g] = states[p * groups + g].astype(MM)
    for side in range(2):

        @pl.when(c != side)
        def _():
            gating((inner, heads, groups), ints_ref, low_states, vecs, side, *sides[side], theirs)

    for i in range(per):
        own_asked[i] = states[ints.wanted((p * 2 + c) * per + i) + 1]
        asked[i] = states[ints.wanted((p * 2 + 1 - c) * per + i) + 1].astype(MM)


def back_own_kernel(sizes, ints_ref, vecs, low_states, *refs):
    sides = (refs[:4], refs[4:8])
    mine = refs[8]
    for side in range(2):

        @pl.when(ints_ref[2] == side)
        def _():
            gating(sizes, ints_ref, low_states, vecs, side, *sides[side], mine)


def is_inner(t):
    return (t == 1) | (t == 2)


def block_places(t, tp_count):
    if tp_count == 4:
        inside = is_inner(t)
        first = jnp.where(inside, t ^ 1, 3 - t)
        return [first, lax.rem(t + 2, 4), jnp.where(inside, 3 - t, t ^ 1), t]
    return [lax.rem(t + j, tp_count) for j in range(1, tp_count)] + [t]


def out_kernel(sizes, ints, mine, theirs, *refs):
    inner, tp_count, chosen, where = sizes
    t, p, c = ints[0], ints[1], ints[2]
    if where:
        pieces = refs[: len(where)]
        outs = refs[len(where) : len(where) + 2 * len(chosen)]
        weights, sems = refs[len(where) + 2 * len(chosen) :]
        copies = []
        for i, (piece, (k, other, first)) in enumerate(zip(pieces, where)):
            rows, columns = piece.shape
            core = 1 - c if other else c
            at = pl.multiple_of(((p ^ k) * 2 + core) * columns, LANES)
            copies.append(
                pltpu.make_async_copy(
                    piece, weights.at[pl.ds(first, rows), pl.ds(at, columns)], sems.at[i]
                )
            )
        run_all(copies)
    else:
        weights, outs = refs[0], refs[1:]
    width = weights.shape[1]
    piece_rows = mine.shape[0] // tp_count
    own_rows = rows_at(c * inner, inner)
    other_rows = rows_at((1 - c) * inner, inner)
    for i, low, high in zip(chosen, outs[::2], outs[1::2]):
        rows = rows_at(block_places(t, tp_count)[i] * piece_rows, piece_rows)
        sums = jnp.sum(
            mine[rows, inner:].astype(F32) + theirs[rows, inner:].astype(F32), axis=1, keepdims=True
        )
        sums = spread_terms(jnp.broadcast_to(sums, (piece_rows, LANES)))
        high[:, width // 2 :] = sums.astype(high.dtype)
        for at in range(0, width, width // 4):
            lanes = slice(at, at + width // 4)
            value = jnp.dot(mine[rows, :inner], weights[own_rows, lanes], preferred_element_type=F32)
            value = value + jnp.dot(
                theirs[rows, :inner], weights[other_rows, lanes], preferred_element_type=F32
            )
            out, first = (low, at) if at < width // 2 else (high, at - width // 2)
            out[:, first : first + width // 4] = value.astype(out.dtype)


def add_kernel(width, ints, got, own, out):
    inside = is_inner(ints[0])
    came = jnp.where(inside, got[:, :width].astype(F32), 0.0)
    out[:, :width] = (came + own[:, :width].astype(F32)).astype(MM)
    if out.shape[1] > width:
        came = jnp.where(inside, added_terms(got, width), 0.0)
        out[:, width:] = spread_terms(came + added_terms(own, width)).astype(MM)


def final_kernel(channels, takers, ints, *refs):
    own, received, out = refs[:2], refs[2:-1], refs[-1]
    half = out.shape[1] // 2
    inside = is_inner(ints[0])

    def taken(value, inner):
        if inner is None:
            return value
        return jnp.where(inside, value, 0.0) if inner else jnp.where(inside, 0.0, value)

    squares = added_terms(own[1], half)
    for got, inner in zip(received[1::2], takers):
        squares = squares + taken(added_terms(got, half), inner)
    factor = lax.rsqrt(squares[:, :1] / channels + epsilon)
    for side in range(2):
        total = own[side][:, :half]
        for got, inner in zip(received[side::2], takers):
            total = total + taken(got[:, :half].astype(F32), inner)
        out[:, side * half : (side + 1) * half] = (total * factor).astype(out.dtype)


def sum_over_tp(ints, blocks, own):
    tp_count = lax.axis_size("tp")
    if tp_count != 4:
        received = [[shift(x, j + 1) for x in block] for j, block in enumerate(blocks)]
        return own, received, (None,) * (tp_count - 1)

    def send(block, pairs):
        return [lax.ppermute(x, "tp", pairs) for x in block]

    def add(got, x, name):
        kernel = functools.partial(add_kernel, own[0].shape[1])
        specs = [SMEM, VMEM, VMEM]
        return call(kernel, [sds(x.shape, MM)], specs, moved=100_000, name=name)(ints, got, x)[0]

    first, second, third = blocks
    beside = send(first, [(0, 1), (1, 0), (2, 3), (3, 2)])
    to_middle = send(third, [(1, 2), (2, 1), (0, 0), (3, 3)])
    to_inner = send(third, [(0, 1), (3, 2)])
    joined = lax.optimization_barrier((*beside, *second, *own))
    beside, second, own = list(joined[:2]), joined[2:4], list(joined[4:])
    second = [add(got, x, "add_far") for got, x in zip(beside, second)]
    across = [shift(x, 2) for x in second]
    return own, [beside, across, to_middle, to_inner], (False, None, True, True)


def on_device(
    tokens,
    w_zx,
    w_dt,
    w_bc,
    conv_x_weight,
    conv_x_bias,
    conv_bc_weight,
    conv_bc_bias,
    dt_bias,
    a_log,
    skip,
    norm_weight,
    w_out,
    lengths,
    request_group,
):
    tp_count, seq_count = lax.axis_size("tp"), lax.axis_size("seq")
    t, s = lax.axis_index("tp"), lax.axis_index("seq")
    chips = seq_count // 2
    p, c = s // 2, s % 2
    tok_dev, width = tokens.shape
    rows = w_zx.shape[0]
    inner_all = w_zx.shape[1] // 2
    pair = conv_x_weight.shape[1]
    inner = pair // 2
    heads = dt_bias.shape[0] // 2
    head_width = inner // heads
    bc_width = w_bc.shape[1]
    state = bc_width // 2
    tok = 2 * tok_dev
    groups = tok // GROUP
    half = groups // 2
    conv = inner + bc_width
    prompts = lengths.shape[0]
    x_width = 2 * inner + bc_width + LANES
    depth = tp_count * rows

    ints = jnp.concatenate([jnp.stack([t, p, c]).astype(jnp.int32), lengths, request_group])
    floats = jnp.concatenate([dt_bias, a_log, skip])
    vecs = jnp.concatenate(
        [
            conv_x_weight,
            conv_x_bias[None, :],
            norm_weight[None, :],
            jnp.zeros((2, pair), F32),
            jnp.pad(conv_bc_weight, ((0, 0), (0, pair - bc_width))),
            jnp.pad(conv_bc_bias[None, :], ((0, 3), (0, pair - bc_width))),
        ],
        axis=0,
    )

    def packed(kernel, operands, specs, wide, name):
        return pl.pallas_call(
            functools.partial(kernel, tp_count),
            grid=(1,),
            out_shape=[sds((rows, wide), MM)] * tp_count,
            in_specs=specs,
            out_specs=[pl.BlockSpec((rows, wide), lambda i: (0, 0))] * tp_count,
            compiler_params=pltpu.CompilerParams(vmem_limit_bytes=VMEM_BYTES),
            name=name,
        )(*operands)

    def whole(x):
        return pl.BlockSpec(x.shape, lambda i: (0, 0))

    def sent_over_tp(pieces):
        return [pieces[0]] + [shift(x, j) for j, x in enumerate(pieces) if j]

    def assembled(kernel, outs, pieces, name):
        return call(
            functools.partial(kernel, tp_count), outs, [SMEM] + [VMEM] * tp_count, name=name
        )(ints, *pieces)

    def together(*lists):
        joined = lax.optimization_barrier(tuple(tuple(one) for one in lists))
        return [list(one) for one in joined]

    x_sent = packed(
        pack_x_kernel,
        (ints, w_zx, w_bc, w_dt),
        [SMEM, pl.BlockSpec((rows, inner_all), lambda i: (0, 1)), whole(w_bc), whole(w_dt)],
        x_width,
        "pack_x",
    )
    x_got = sent_over_tp(x_sent)

    out_near = plane_near(w_out.astype(MM))
    keys = list(out_near)
    other = flip(tokens, 1)
    first_tok = jnp.where(c == 0, tokens, other)
    second_tok = jnp.where(c == 0, other, tokens)
    out_got, (first_tok, second_tok) = together(
        [out_near[k][0] for k in keys], [first_tok, second_tok]
    )
    out_blocks = plane_far({k: (piece,) for k, piece in zip(keys, out_got)})
    out_own = [piece for k in out_blocks for piece in out_blocks[k]]
    out_where = [
        (k, 0, i * (w_out.shape[0] // 2)) for k in out_blocks for i in range(len(out_blocks[k]))
    ]
    x_got, out_own = together(x_got, out_own)
    (x_block,) = assembled(assemble_x_kernel, [sds((depth, x_width), MM)], x_got, "assemble_x")

    before = lax.ppermute(
        second_tok[tok_dev - HALO :], "seq", [(i, i + 2) for i in range(seq_count - 2)]
    )
    all_tok = jnp.concatenate([before, first_tok, second_tok], axis=0)

    ((x_block, all_tok, ints, floats, vecs),) = together([x_block, all_tok, ints, floats, vecs])
    near = plane_near(x_block)
    z_sent = packed(
        pack_z_kernel,
        (ints, w_zx),
        [SMEM, pl.BlockSpec((rows, inner_all), lambda i: (0, 0))],
        2 * inner,
        "pack_z",
    )
    z_got = sent_over_tp(z_sent)
    blocks, z_got, (x_own,) = together([near[k][0] for k in near if k], z_got, [x_block])
    own_other = flip(x_own, 1)
    far = plane_far({k: (block,) for k, block in zip(near, [x_block] + blocks)})
    z_mine, z_theirs = assembled(
        assemble_z_kernel, [sds((depth, inner), MM)] * 2, z_got, "assemble_z"
    )
    (z_block,) = call(
        merge_kernel, [sds((2 * depth, inner), MM)], [SMEM, VMEM, VMEM], name="merge_z"
    )(ints, z_mine, flip(z_theirs, 1))
    near_other = [flip(far[k][0], 1) for k in near if k]
    order = [k for k in far if k not in near]
    near_other, (z_block,) = together(near_other, [z_block])
    x_far, near_other = together([piece for k in order for piece in far[k]], near_other)
    far_other = [flip(piece, 1) for piece in x_far]
    where = [(k, 0) for k in near] + [(k, i * depth // 2) for k in order for i in range(2)]
    where = tuple((k, other, first) for other in range(2) for k, first in where)
    x_pieces = [far[k][0] for k in near] + x_far + [own_other] + near_other + far_other

    def front(side, where, operands):
        outs = [
            sds((tok_dev, inner), MM),
            sds((tok_dev, bc_width), MM),
            sds((tok_dev, LANES), F32),
            sds((tok_dev, LANES), F32),
            sds((half, inner + TERMS, state), MM),
        ]
        scratch = [pltpu.VMEM((2, HALO + GROUP, conv + LANES), F32)]
        if where:
            outs.append(sds((width, conv + LANES), MM))
            scratch.append(pltpu.SemaphoreType.DMA((2 * len(where),)))
        return call(
            functools.partial(
                front_kernel, (inner, bc_width, heads, prompts, where, depth, groups, side)
            ),
            outs,
            [SMEM, SMEM, VMEM, VMEM] + ([ANY] * len(where) if where else [VMEM]),
            scratch,
            flops=0,
            moved=1_000_000,
            name="front_%d" % side,
        )(ints, floats, vecs, all_tok, *operands)

    z_near = plane_near(z_block)
    *first, weights = front(0, where, x_pieces)
    ((*first, weights),) = together([*first, weights])

    low_near = plane_near(first[4])
    second = front(1, (), [weights])
    out_other = [flip(piece, 1) for piece in out_own]
    second, lows, z_blocks, out_other = together(
        second,
        [low_near[k][0] for k in low_near],
        [z_near[k][0] for k in z_near],
        out_other,
    )
    out_pieces = out_own + out_other
    out_where = tuple(out_where + [(k, 1, first_row) for k, _, first_row in out_where])
    z_far = plane_far({k: (block,) for k, block in zip(z_near, z_blocks)})
    z_order = [k for k in z_far if k in z_near] + [k for k in z_far if k not in z_near]
    z_where = tuple((k, i * depth) for k in z_order for i in range(len(z_far[k])))
    z_pieces = [piece for k in z_order for piece in z_far[k]]

    def mid(side, xs, bc, cum, step, message):
        return call(
            functools.partial(mid_kernel, (inner, heads, prompts, groups, side)),
            [sds((tok_dev, inner), F32)] * 2,
            [SMEM, SMEM] + [VMEM] * 4,
            flops=2 * tok_dev * GROUP * inner,
            moved=1_000_000,
            name="mid_%d" % side,
        )(ints, floats, xs, bc, cum, step)

    parts = {k: (block, None) for k, block in zip(low_near, lows)}
    high_near = plane_near(second[4])
    first_y = mid(0, *first)
    highs, first_y = together([high_near[k][0] for k in parts], first_y)
    parts = {k: (parts[k][0], high) for k, high in zip(parts, highs)}
    for k in range(1, chips):
        if k not in parts:
            low, high = k & -k, 1 << (k.bit_length() - 1)
            parts[k] = (flip(parts[k ^ low][0], 2 * low), flip(parts[k ^ high][1], 2 * high))
    parts = [piece for k in range(chips) for piece in parts[k]]

    y = [first_y, mid(1, *second)]
    near_count = len(z_near)
    gate = []
    for part in (slice(0, near_count), slice(near_count, None)):
        chosen = z_where[part]
        gate = call(
            functools.partial(gate_kernel, chosen, 2 * depth, len(gate) > 0),
            [sds((tok_dev, inner), F32)] * 2,
            [SMEM, VMEM] + [VMEM] * (len(chosen) + len(gate)),
            flops=tok * width * inner // 4,
            moved=1_000_000,
            name="gate_%d" % (len(gate) > 0),
        )(ints, all_tok, *z_pieces[part], *gate)
    sides = [*y[0], gate[0], first[1], *y[1], gate[1], second[1]]
    parts, sides = together(parts, sides)

    per = request_group.shape[0] // seq_count
    sent = sds((tok_dev, inner + LANES), MM)
    theirs, low_states, asked, own_asked = call(
        functools.partial(back_kernel, (inner, heads, prompts, groups, len(parts), per)),
        [
            sent,
            sds((groups, inner, state), MM),
            sds((per, inner, state), MM),
            sds((per, inner, state), F32),
        ],
        [SMEM, VMEM] + [ANY] * len(parts) + [VMEM] * 8,
        [
            pltpu.VMEM((chips * groups, inner + TERMS, state), MM),
            pltpu.VMEM((chips * groups + 1, inner, state), F32),
            pltpu.SemaphoreType.DMA((len(parts),)),
        ],
        flops=2 * tok * state * inner,
        moved=8_000_000,
        name="back",
    )(ints, vecs, *parts, *sides)
    theirs = flip(theirs, 1)
    (mine,) = call(
        functools.partial(back_own_kernel, (inner, heads, groups)),
        [sent],
        [SMEM] + [VMEM] * 10,
        flops=2 * tok_dev * state * inner,
        moved=4_000_000,
        name="back_own",
    )(ints, vecs, low_states, *sides)

    out_width = seq_count * w_out.shape[1]
    piece = tok_dev // tp_count
    ahead = 1 if tp_count == 4 else tp_count - 2

    def project_out(chosen, outs, where, operands):
        scratch, extra = [], []
        outs = [
            sds((piece, out_width // 2 + side * LANES), kind) for kind in outs for side in range(2)
        ]
        if where:
            extra = [sds((2 * inner, out_width), MM)]
            scratch = [pltpu.SemaphoreType.DMA((len(where),))]
        return call(
            functools.partial(out_kernel, (inner, tp_count, chosen, where)),
            outs + extra,
            [SMEM, VMEM, VMEM] + ([ANY] * len(where) if where else [VMEM]),
            scratch,
            flops=len(outs) * piece * inner * out_width,
            moved=1_000_000,
            name="out_%d" % len(chosen),
        )(ints, mine, theirs, *operands)

    *sent_first, out_weights = project_out(tuple(range(ahead)), [MM] * ahead, out_where, out_pieces)
    *sent_next, own_low, own_high = project_out(
        tuple(range(ahead, tp_count)), [MM] * (tp_count - 1 - ahead) + [F32], (), [out_weights]
    )
    halves = [*sent_first, *sent_next]
    own, received, takers = sum_over_tp(
        ints, [halves[i : i + 2] for i in range(0, len(halves), 2)], [own_low, own_high]
    )
    received = [half for block in received for half in block]
    (mixed,) = call(
        functools.partial(final_kernel, float(inner_all), takers),
        [sds((piece, out_width), MM)],
        [SMEM] + [VMEM] * (2 + len(received)),
        name="final",
    )(ints, *own, *received)

    other_asked = flip(asked, 1).astype(F32)
    states = jnp.where(
        c == 0,
        jnp.concatenate([own_asked, other_asked], axis=1),
        jnp.concatenate([other_asked, own_asked], axis=1),
    )
    return (mixed, states.reshape(per, 2 * heads, head_width, state))


def solution(mesh):
    return jax.shard_map(
        on_device,
        mesh=mesh,
        in_specs=(
            P("seq", None),
            P(("seq", "tp"), None),
            P(("seq", "tp"), None),
            P(("seq", "tp"), None),
            P(None, "tp"),
            P("tp"),
            P(),
            P(),
            P("tp"),
            P("tp"),
            P("tp"),
            P("tp"),
            P("tp", "seq"),
            P(),
            P(),
        ),
        out_specs=(P(("seq", "tp"), None), P("seq", "tp", None, None)),
        check_vma=False,
    )
```

profile of v0, /device:TPU:0, one launch (start us, length us, event | category | flops | bytes accessed | tf_op | source)
XLA Modules:
  0.0 158.4 jit_solution(15864572044136610273)
XLA Ops:
  1.2 1.3 convert_element_type.10.refs_0_
  2.5 2.6 %collective-permute-start.3 = (bf16[1024,256]{1,0:T(8,128)(2,1)S(1)}, bf16[1024,256]{1,0:T(8,128)(2,1)S(1)}, u32[]{:S(2)}, u32[]{:S(2)}) collective-permute-start(bf16[1024,256]{1,0:T(8,128)(2,1)S(1)} %convert_element_type.10.refs_0_), channel_id=1, source_target_pairs={{0,8},{4,12},{8,0},{12,4},{16,24},{20,28},{24,16},{28,20},{1,9},{5... | collective-permute-start | bytes 1572872 | tf_op jit(solution)/shard_map/ppermute | solution.py:29
  5.0 1.5 collective-permute-start.4
  6.6 0.7 concatenate.18.ints.ints_ref
  7.3 1.6 %copy-done = f32[64,8192]{1,0:T(8,128)S(1)} copy-done((f32[64,8192]{1,0:T(8,128)S(1)}, f32[64,8192]{1,0:T(8,128)}, u32[]{:S(2)}) %copy-start) | copy-done | bytes 2097176
  8.9 0.8 copy-done.2
  9.8 0.8 copy-done.3
  10.5 0.9 pack_x.1
  11.4 1.6 %collective-permute-start = (bf16[64,1408]{1,0:T(8,128)(2,1)S(1)}, bf16[64,1408]{1,0:T(8,128)(2,1)S(1)}, u32[]{:S(2)}, u32[]{:S(2)}) collective-permute-start(bf16[64,1408]{1,0:T(8,128)(2,1)S(1)} %get-tuple-element.121), channel_id=1, source_target_pairs={{0,1},{1,2},{2,3},{3,0},{4,5},{5,6},{6,7},{7,4},{8,9},{9,10},{10,1... | collective-permute-start | bytes 540680 | tf_op jit(solution)/shard_map/ppermute | solution.py:34
  13.0 2.6 %collective-permute-start.1 = (bf16[64,1408]{1,0:T(8,128)(2,1)S(1)}, bf16[64,1408]{1,0:T(8,128)(2,1)S(1)}, u32[]{:S(2)}, u32[]{:S(2)}) collective-permute-start(bf16[64,1408]{1,0:T(8,128)(2,1)S(1)} %get-tuple-element.122), channel_id=1, source_target_pairs={{0,2},{1,3},{2,0},{3,1},{4,6},{5,7},{6,4},{7,5},{8,10},{9,11},{10,... | collective-permute-start | bytes 540680 | tf_op jit(solution)/shard_map/ppermute | solution.py:34
  15.8 1.4 collective-permute-start.2
  17.2 2.5 %broadcast_select_fusion = (bf16[512,2048]{1,0:T(8,128)(2,1)S(1)}, bf16[512,2048]{1,0:T(8,128)(2,1)S(1)}) fusion(bf16[512,2048]{1,0:T(8,128)(2,1)} %collective-permute-done.5, bf16[512,2048]{1,0:T(8,128)(2,1)} %param.15, pred[]{:T(512)S(6)} %eq.4), kind=kLoop, calls=%fused_computation.1 | loop fusion | flops 2097152 | bytes 8388609 | tf_op jit(solution)/shard_map/jit(_where)/select_n | solution.py:642
  19.7 2.4 %collective-permute-start.8 = (bf16[16,2048]{1,0:T(8,128)(2,1)S(1)}, bf16[16,2048]{1,0:T(8,128)(2,1)S(1)}, u32[]{:S(2)}, u32[]{:S(2)}) collective-permute-start(bf16[16,2048]{1,0:T(8,128)(2,1)S(1)} %slice.23), channel_id=1, source_target_pairs={{0,8},{4,12},{8,16},{12,20},{16,24},{20,28},{1,9},{5,13},{9,17},{1... | collective-permute-start | bytes 196616 | tf_op jit(solution)/shard_map/ppermute | solution.py:654
  22.3 1.9 %collective-permute-start.6 = (bf16[512,256]{1,0:T(8,128)(2,1)S(1)}, bf16[512,256]{1,0:T(8,128)(2,1)S(1)}, u32[]{:S(2)}, u32[]{:S(2)}) collective-permute-start(bf16[512,256]{1,0:T(8,128)(2,1)S(1)} %slice.21), channel_id=1, source_target_pairs={{0,8},{4,12},{8,0},{12,4},{16,24},{20,28},{24,16},{28,20},{1,9},{5... | collective-permute-start | bytes 786440 | tf_op jit(solution)/shard_map/ppermute | solution.py:29
  24.4 4.0 %collective-permute-start.7 = (bf16[512,256]{1,0:T(8,128)(2,1)S(1)}, bf16[512,256]{1,0:T(8,128)(2,1)S(1)}, u32[]{:S(2)}, u32[]{:S(2)}) collective-permute-start(bf16[512,256]{1,0:T(8,128)(2,1)S(1)} %slice.22), channel_id=1, source_target_pairs={{0,16},{4,20},{8,24},{12,28},{16,0},{20,4},{24,8},{28,12},{1,17},{... | collective-permute-start | bytes 786440 | tf_op jit(solution)/shard_map/ppermute | solution.py:29
  28.8 2.1 %collective-permute-done.6.refs_3_ = bf16[512,256]{1,0:T(8,128)(2,1)S(1)} collective-permute-done((bf16[512,256]{1,0:T(8,128)(2,1)S(1)}, bf16[512,256]{1,0:T(8,128)(2,1)S(1)}, u32[]{:S(2)}, u32[]{:S(2)}) %collective-permute-start.6) | collective-permute-done | bytes 262176 | tf_op jit(solution)/shard_map/ppermute | solution.py:29
  30.9 1.8 %collective-permute-done.7.refs_4_ = bf16[512,256]{1,0:T(8,128)(2,1)S(1)} collective-permute-done((bf16[512,256]{1,0:T(8,128)(2,1)S(1)}, bf16[512,256]{1,0:T(8,128)(2,1)S(1)}, u32[]{:S(2)}, u32[]{:S(2)}) %collective-permute-start.7) | collective-permute-done | bytes 262176 | tf_op jit(solution)/shard_map/ppermute | solution.py:29
  33.4 2.1 %collective-permute-start.10 = (bf16[256,1408]{1,0:T(8,128)(2,1)S(1)}, bf16[256,1408]{1,0:T(8,128)(2,1)S(1)}, u32[]{:S(2)}, u32[]{:S(2)}) collective-permute-start(bf16[256,1408]{1,0:T(8,128)(2,1)S(1)} %assemble_x.1.refs_0_), channel_id=1, source_target_pairs={{0,16},{4,20},{8,24},{12,28},{16,0},{20,4},{24,8},{28,12},{1,17},{... | collective-permute-start | bytes 2162696 | tf_op jit(solution)/shard_map/ppermute | solution.py:29
  36.1 1.9 %collective-permute-start.11 = (bf16[64,1024]{1,0:T(8,128)(2,1)S(1)}, bf16[64,1024]{1,0:T(8,128)(2,1)S(1)}, u32[]{:S(2)}, u32[]{:S(2)}) collective-permute-start(bf16[64,1024]{1,0:T(8,128)(2,1)S(1)} %get-tuple-element.139), channel_id=1, source_target_pairs={{0,1},{1,2},{2,3},{3,0},{4,5},{5,6},{6,7},{7,4},{8,9},{9,10},{10,1... | collective-permute-start | bytes 393224 | tf_op jit(solution)/shard_map/ppermute | solution.py:34
  38.1 2.5 %collective-permute-start.12 = (bf16[64,1024]{1,0:T(8,128)(2,1)S(1)}, bf16[64,1024]{1,0:T(8,128)(2,1)S(1)}, u32[]{:S(2)}, u32[]{:S(2)}) collective-permute-start(bf16[64,1024]{1,0:T(8,128)(2,1)S(1)} %get-tuple-element.140), channel_id=1, source_target_pairs={{0,2},{1,3},{2,0},{3,1},{4,6},{5,7},{6,4},{7,5},{8,10},{9,11},{10,... | collective-permute-start | bytes 393224 | tf_op jit(solution)/shard_map/ppermute | solution.py:34
  40.6 1.4 collective-permute-start.13
  42.0 1.1 collective-permute-done.11.refs_1_
  43.1 3.7 %collective-permute-done.12.refs_2_ = bf16[64,1024]{1,0:T(8,128)(2,1)S(1)} collective-permute-done((bf16[64,1024]{1,0:T(8,128)(2,1)S(1)}, bf16[64,1024]{1,0:T(8,128)(2,1)S(1)}, u32[]{:S(2)}, u32[]{:S(2)}) %collective-permute-start.12) | collective-permute-done | bytes 131104 | tf_op jit(solution)/shard_map/ppermute | solution.py:34
  46.7 2.0 %collective-permute-done.10.refs_2_ = bf16[256,1408]{1,0:T(8,128)(2,1)S(1)} collective-permute-done((bf16[256,1408]{1,0:T(8,128)(2,1)S(1)}, bf16[256,1408]{1,0:T(8,128)(2,1)S(1)}, u32[]{:S(2)}, u32[]{:S(2)}) %collective-permute-start.10) | collective-permute-done | bytes 720928 | tf_op jit(solution)/shard_map/ppermute | solution.py:29
  48.7 1.2 collective-permute-done.9.refs_1_
  51.5 1.0 collective-permute-start.15
  52.5 1.0 collective-permute-done.18.theirs
  54.7 7.3 %collective-permute-done.14.refs_3_ = bf16[128,1408]{1,0:T(8,128)(2,1)S(1)} collective-permute-done((bf16[128,1408]{1,0:T(8,128)(2,1)S(1)}, bf16[128,1408]{1,0:T(8,128)(2,1)S(1)}, u32[]{:S(2)}, u32[]{:S(2)}) %collective-permute-start.14) | collective-permute-done | bytes 360480 | tf_op jit(solution)/shard_map/ppermute | solution.py:29
  63.7 1.7 %collective-permute-start.24 = (bf16[512,512]{1,0:T(8,128)(2,1)S(1)}, bf16[512,512]{1,0:T(8,128)(2,1)S(1)}, u32[]{:S(2)}, u32[]{:S(2)}) collective-permute-start(bf16[512,512]{1,0:T(8,128)(2,1)S(1)} %merge_z.1.refs_0_), channel_id=1, source_target_pairs={{0,8},{4,12},{8,0},{12,4},{16,24},{20,28},{24,16},{28,20},{1,9},{5... | collective-permute-start | bytes 1572872 | tf_op jit(solution)/shard_map/ppermute | solution.py:29
  66.0 6.5 %front_0.1 = (bf16[512,512]{1,0:T(8,128)(2,1)S(1)}, bf16[512,256]{1,0:T(8,128)(2,1)S(1)}, f32[512,128]{1,0:T(8,128)S(1)}, f32[512,128]{1,0:T(8,128)S(1)}, bf16[2...) custom-call(s32[27]{0:T(128)S(1)} %concatenate.18.ints.ints_ref, f32[48]{0:T(128)S(1)} %pad_maximum_fusion.1.floats, ...), custom_call_target="tpu_custom_call" | custom-call | bytes 1000000 | tf_op jit(solution)/shard_map/front_0/pallas_call | solution.py:699
  72.5 0.8 collective-permute-start.22
  73.3 1.2 collective-permute-start.23
  74.5 5.7 %front_1.1 = (bf16[512,512]{1,0:T(8,128)(2,1)S(1)}, bf16[512,256]{1,0:T(8,128)(2,1)S(1)}, f32[512,128]{1,0:T(8,128)S(1)}, f32[512,128]{1,0:T(8,128)S(1)}, bf16[2,544,128]{2,1,0:T(8,128)(2,1)S(1)}) custom-call(s32[27]{0:T(128)S(1)} %concatenate.18.ints.ints_ref, f32[48]{0:T(128)S(1)} %pad_maximum_fusion.1.floats, f32[16,1024]{1,0:T(8,128)S(1)} %concatenate.21.vecs, ...), custom_call_target="tpu_custom_call" | custom-call | bytes 1000000 | tf_op jit(solution)/shard_map/front_1/pallas_call | solution.py:699
  80.3 3.4 %collective-permute-done.22.refs_2_ = bf16[2,544,128]{2,1,0:T(8,128)(2,1)S(1)} collective-permute-done((bf16[2,544,128]{2,1,0:T(8,128)(2,1)S(1)}, bf16[2,544,128]{2,1,0:T(8,128)(2,1)S(1)}, u32[]{:S(2)}, u32[]{:S(2)}) %collective-permute-start.22) | collective-permute-done | bytes 278560 | tf_op jit(solution)/shard_map/ppermute | solution.py:29
  83.7 1.4 collective-permute-done.23.refs_4_
  85.1 0.8 collective-permute-start.31
  86.5 1.3 collective-permute-start.35
  87.8 1.5 collective-permute-start.36
  89.3 2.4 %mid_0.1 = (f32[512,512]{1,0:T(8,128)S(1)}, f32[512,512]{1,0:T(8,128)S(1)}) custom-call(s32[27]{0:T(128)S(1)} %concatenate.18.ints.ints_ref, f32[48]{0:T(128)S(1)} %pad_maximum_fusion.1.floats, bf16[512,512]{1,0:T(8,128)(2,1)S(1)} %get-tuple-element.172.xs_ref, bf16[512,256]{1,0:T(8,128)(2,1)S(1)} %get-tuple-element.209.bc_ref.refs_11_.refs_3_, ...), custom_call_target="tpu_custom_call" | custom-call | flops 134217728 | bytes 1000000 | tf_op jit(solution)/shard_map/mid_0/pallas_call | solution.py:732
  91.7 0.9 collective-permute-start.33
  92.6 2.1 %collective-permute-done.31.refs_3_ = bf16[2,544,128]{2,1,0:T(8,128)(2,1)S(1)} collective-permute-done((bf16[2,544,128]{2,1,0:T(8,128)(2,1)S(1)}, bf16[2,544,128]{2,1,0:T(8,128)(2,1)S(1)}, u32[]{:S(2)}, u32[]{:S(2)}) %collective-permute-start.31) | collective-permute-done | bytes 278560 | tf_op jit(solution)/shard_map/ppermute | solution.py:29
  94.7 0.8 collective-permute-done.32.refs_5_
  96.0 2.4 %mid_1.1 = (f32[512,512]{1,0:T(8,128)S(1)}, f32[512,512]{1,0:T(8,128)S(1)}) custom-call(s32[27]{0:T(128)S(1)} %concatenate.18.ints.ints_ref, f32[48]{0:T(128)S(1)} %pad_maximum_fusion.1.floats, bf16[512,512]{1,0:T(8,128)(2,1)S(1)} %get-tuple-element.191.xs_ref, bf16[512,256]{1,0:T(8,128)(2,1)S(1)} %get-tuple-element.213.bc_ref.refs_15_.refs_7_, ...), custom_call_target="tpu_custom_call" | custom-call | flops 134217728 | bytes 1000000 | tf_op jit(solution)/shard_map/mid_1/pallas_call | solution.py:732
  98.5 2.9 %gate_0.1 = (f32[512,512]{1,0:T(8,128)S(1)}, f32[512,512]{1,0:T(8,128)S(1)}) custom-call(s32[27]{0:T(128)S(1)} %concatenate.18.ints.ints_ref, bf16[1040,2048]{1,0:T(8,128)(2,1)S(1)} %pad_maximum_fusion.tok_ref, bf16[512,512]{1,0:T(8,128)(2,1)S(1)} %merge_z.1.refs_0_, bf16[512,512]{1,0:T(8,128)(2,1)S(1)} %collective-permute-done.24.refs_1_, ...), custom_call_target="tpu_custom_call" | custom-call | flops 268435456 | bytes 1000000 | tf_op jit(solution)/shard_map/gate_0/pallas_call | solution.py:757
  101.4 2.2 %gate_1.1 = (f32[512,512]{1,0:T(8,128)S(1)}, f32[512,512]{1,0:T(8,128)S(1)}) custom-call(s32[27]{0:T(128)S(1)} %concatenate.18.ints.ints_ref, bf16[1040,2048]{1,0:T(8,128)(2,1)S(1)} %pad_maximum_fusion.tok_ref, bf16[256,512]{1,0:T(8,128)(2,1)S(1)} %collective-permute-done.35.refs_0_, bf16[256,512]{1,0:T(8,128)(2,1)S(1)} %collective-permute-done.36.refs_1_, ...), custom_call_target="tpu_custom_call" | custom-call | flops 268435456 | bytes 1000000 | tf_op jit(solution)/shard_map/gate_1/pallas_call | solution.py:757
  103.6 0.6 collective-permute-done.33.refs_6_
  104.2 0.8 collective-permute-done.34.refs_7_
  105.0 2.2 %back.1 = (bf16[512,640]{1,0:T(8,128)(2,1)S(1)}, bf16[4,512,128]{2,1,0:T(8,128)(2,1)S(1)}, bf16[2,512,128]{2,1,0:T(8,128)(2,1)S(1)}, f32[2,512,128]{2,1,0:T(8,128)S(1)}) custom-call(s32[27]{0:T(128)S(1)} %concatenate.18.ints.ints_ref, f32[16,1024]{1,0:T(8,128)S(1)} %concatenate.21.vecs, bf16[2,544,128]{2,1,0:T(8,128)(2,1)S(1)} %get-tuple-element.198.refs_0_, ...), custom_call_target="tpu_custom_call" | custom-call | flops 134217728 | bytes 8000000 | tf_op jit(solution)/shard_map/back/pallas_call | solution.py:770
  107.8 1.1 back_own.1.mine
  109.4 2.0 %out_1.1 = (bf16[128,1024]{1,0:T(8,128)(2,1)S(1)}, bf16[128,1152]{1,0:T(8,128)(2,1)S(1)}, bf16[1024,2048]{1,0:T(8,128)(2,1)S(1)}) custom-call(s32[27]{0:T(128)S(1)} %concatenate.18.ints.ints_ref, bf16[512,640]{1,0:T(8,128)(2,1)S(1)} %back_own.1.mine, bf16[512,640]{1,0:T(8,128)(2,1)S(1)} %collective-permute-done.37.theirs, ...), custom_call_target="tpu_custom_call" | custom-call | flops 268435456 | bytes 1000000 | tf_op jit(solution)/shard_map/out_1/pallas_call | solution.py:810
  111.4 1.3 collective-permute-start.39
  112.7 0.7 collective-permute-start.38
  113.5 2.4 %out_3.1 = (bf16[128,1024]{1,0:T(8,128)(2,1)S(1)}, bf16[128,1152]{1,0:T(8,128)(2,1)S(1)}, bf16[128,1024]{1,0:T(8,128)(2,1)S(1)}, bf16[128,1152]{1,0:T(8,128)(2,1...) custom-call(s32[27]{0:T(128)S(1)} %concatenate.18.ints.ints_ref, bf16[512,640]{1,0:T(8,128)(2,1)S(1)} %back_own.1.mine, ...), custom_call_target="tpu_custom_call" | custom-call | flops 805306368 | bytes 1000000 | tf_op jit(solution)/shard_map/out_3/pallas_call | solution.py:810
  115.8 0.7 collective-permute-start.42
  116.5 0.7 collective-permute-start.43
  117.2 8.9 %collective-permute-done.38.got.refs_2_ = bf16[128,1024]{1,0:T(8,128)(2,1)S(1)} collective-permute-done((bf16[128,1024]{1,0:T(8,128)(2,1)S(1)}, bf16[128,1024]{1,0:T(8,128)(2,1)S(1)}, u32[]{:S(2)}, u32[]{:S(2)}) %collective-permute-start.38) | collective-permute-done | bytes 262176 | tf_op jit(solution)/shard_map/ppermute | solution.py:533
  126.1 3.2 %collective-permute-start.45 = (bf16[128,1152]{1,0:T(8,128)(2,1)S(1)}, bf16[128,1152]{1,0:T(8,128)(2,1)S(1)}, u32[]{:S(2)}, u32[]{:S(2)}) collective-permute-start(bf16[128,1152]{1,0:T(8,128)(2,1)S(1)} %get-tuple-element.235), channel_id=1, source_target_pairs={{0,1},{3,2},{4,5},{7,6},{8,9},{11,10},{12,13},{15,14},{16,17},{19,... | collective-permute-start | bytes 884744 | tf_op jit(solution)/shard_map/ppermute | solution.py:533
  129.3 0.7 add_far.3
  130.5 4.6 %collective-permute-start.44 = (bf16[128,1024]{1,0:T(8,128)(2,1)S(1)}, bf16[128,1024]{1,0:T(8,128)(2,1)S(1)}, u32[]{:S(2)}, u32[]{:S(2)}) collective-permute-start(bf16[128,1024]{1,0:T(8,128)(2,1)S(1)} %get-tuple-element.234), channel_id=1, source_target_pairs={{0,1},{3,2},{4,5},{7,6},{8,9},{11,10},{12,13},{15,14},{16,17},{19,... | collective-permute-start | bytes 786440 | tf_op jit(solution)/shard_map/ppermute | solution.py:533
  135.1 0.6 add_far.2
  135.8 1.1 maximum_select_fusion
  136.9 11.8 %collective-permute-done.44.refs_8_ = bf16[128,1024]{1,0:T(8,128)(2,1)S(1)} collective-permute-done((bf16[128,1024]{1,0:T(8,128)(2,1)S(1)}, bf16[128,1024]{1,0:T(8,128)(2,1)S(1)}, u32[]{:S(2)}, u32[]{:S(2)}) %collective-permute-start.44) | collective-permute-done | bytes 262176 | tf_op jit(solution)/shard_map/ppermute | solution.py:533
  148.7 7.8 %collective-permute-done.40.refs_4_ = bf16[128,1024]{1,0:T(8,128)(2,1)S(1)} collective-permute-done((bf16[128,1024]{1,0:T(8,128)(2,1)S(1)}, bf16[128,1024]{1,0:T(8,128)(2,1)S(1)}, u32[]{:S(2)}, u32[]{:S(2)}) %collective-permute-start.40) | collective-permute-done | bytes 262176 | tf_op jit(solution)/shard_map/ppermute | solution.py:34
  156.5 1.9 %final.1 = bf16[128,2048]{1,0:T(8,128)(2,1)} custom-call(s32[27]{0:T(128)S(1)} %concatenate.18.ints.ints_ref, f32[128,1024]{1,0:T(8,128)S(1)} %get-tuple-element.228.refs_0_, f32[128,1152]{1,0:T(8,128)S(1)} %get-tuple-element.229.refs_1_, bf16[128,1024]{1,0:T(8,128)(2,1)S(1)} %collective-permute-done.38.got.refs_2_, ...), custom_call_target="tpu_custom_call" | custom-call | tf_op jit(solution)/shard_map/final/pallas_call | solution.py:829
  (90 shorter events, 10.5 us)
Async XLA Ops:
  0.6 15.0 %copy-start.7 = (f32[4,256]{1,0:T(4,128)S(1)}, f32[4,256]{1,0:T(4,128)}, u32[]{:S(2)}) copy-start(f32[4,256]{1,0:T(4,128)} %param.21) | copy-start | bytes 12292
  0.6 15.0 %copy-start.8 = (f32[256]{0:T(256)S(1)}, f32[256]{0:T(256)}, u32[]{:S(2)}) copy-start(f32[256]{0:T(256)} %param.22) | copy-start | bytes 3076
  0.7 15.0 %copy-start.5 = (f32[1024]{0:T(1024)S(1)}, f32[1024]{0:T(1024)}, u32[]{:S(2)}) copy-start(f32[1024]{0:T(1024)} %param.20) | copy-start | bytes 12292
  0.7 15.0 %copy-start.6 = (f32[1024]{0:T(1024)S(1)}, f32[1024]{0:T(1024)}, u32[]{:S(2)}) copy-start(f32[1024]{0:T(1024)} %param.26) | copy-start | bytes 12292
  0.7 15.0 %copy-start.4 = (f32[4,1024]{1,0:T(4,128)S(1)}, f32[4,1024]{1,0:T(4,128)}, u32[]{:S(2)}) copy-start(f32[4,1024]{1,0:T(4,128)} %param.19) | copy-start | bytes 49156
  0.7 15.0 %collective-permute-start.5 = (bf16[512,2048]{1,0:T(8,128)(2,1)}, bf16[512,2048]{1,0:T(8,128)(2,1)}, u32[]{:S(2)}, u32[]{:S(2)}) collective-permute-start(bf16[512,2048]{1,0:T(8,128)(2,1)} %param.15), channel_id=1, source_target_pairs={{0,4},{4,0},{8,12},{12,8},{16,20},{20,16},{24,28},{28,24},{1,5},{5... | collective-permute-start | bytes 6291464 | tf_op jit(solution)/shard_map/ppermute | solution.py:29
  2.5 17.2 %collective-permute-start.3 = (bf16[1024,256]{1,0:T(8,128)(2,1)S(1)}, bf16[1024,256]{1,0:T(8,128)(2,1)S(1)}, u32[]{:S(2)}, u32[]{:S(2)}) collective-permute-start(bf16[1024,256]{1,0:T(8,128)(2,1)S(1)} %convert_element_type.10.refs_0_), channel_id=1, source_target_pairs={{0,8},{4,12},{8,0},{12,4},{16,24},{20,28},{24,16},{28,20},{1,9},{5... | collective-permute-start | bytes 1572872 | tf_op jit(solution)/shard_map/ppermute | solution.py:29
  5.0 14.6 %collective-permute-start.4 = (bf16[1024,256]{1,0:T(8,128)(2,1)S(1)}, bf16[1024,256]{1,0:T(8,128)(2,1)S(1)}, u32[]{:S(2)}, u32[]{:S(2)}) collective-permute-start(bf16[1024,256]{1,0:T(8,128)(2,1)S(1)} %convert_element_type.10.refs_0_), channel_id=1, source_target_pairs={{0,16},{4,20},{8,24},{12,28},{16,0},{20,4},{24,8},{28,12},{1,17},{... | collective-permute-start | bytes 1572872 | tf_op jit(solution)/shard_map/ppermute | solution.py:29
  7.3 1.6 %copy-start = (f32[64,8192]{1,0:T(8,128)S(1)}, f32[64,8192]{1,0:T(8,128)}, u32[]{:S(2)}) copy-start(f32[64,8192]{1,0:T(8,128)} %w_ref.3) | copy-start | bytes 6291460
  8.9 0.8 copy-start.2
  9.8 0.8 copy-start.3
  11.4 17.4 %collective-permute-start = (bf16[64,1408]{1,0:T(8,128)(2,1)S(1)}, bf16[64,1408]{1,0:T(8,128)(2,1)S(1)}, u32[]{:S(2)}, u32[]{:S(2)}) collective-permute-start(bf16[64,1408]{1,0:T(8,128)(2,1)S(1)} %get-tuple-element.121), channel_id=1, source_target_pairs={{0,1},{1,2},{2,3},{3,0},{4,5},{5,6},{6,7},{7,4},{8,9},{9,10},{10,1... | collective-permute-start | bytes 540680 | tf_op jit(solution)/shard_map/ppermute | solution.py:34
  13.0 15.8 %collective-permute-start.1 = (bf16[64,1408]{1,0:T(8,128)(2,1)S(1)}, bf16[64,1408]{1,0:T(8,128)(2,1)S(1)}, u32[]{:S(2)}, u32[]{:S(2)}) collective-permute-start(bf16[64,1408]{1,0:T(8,128)(2,1)S(1)} %get-tuple-element.122), channel_id=1, source_target_pairs={{0,2},{1,3},{2,0},{3,1},{4,6},{5,7},{6,4},{7,5},{8,10},{9,11},{10,... | collective-permute-start | bytes 540680 | tf_op jit(solution)/shard_map/ppermute | solution.py:34
  15.7 6.4 %copy-start.9 = (f32[16]{0:T(128)S(1)}, f32[16]{0:T(128)}, u32[]{:S(2)}) copy-start(f32[16]{0:T(128)} %param.25) | copy-start | bytes 196
  15.7 6.4 %copy-start.10 = (f32[16]{0:T(128)S(1)}, f32[16]{0:T(128)}, u32[]{:S(2)}) copy-start(f32[16]{0:T(128)} %param.24) | copy-start | bytes 196
  15.8 6.4 %copy-start.11 = (f32[16]{0:T(128)S(1)}, f32[16]{0:T(128)}, u32[]{:S(2)}) copy-start(f32[16]{0:T(128)} %param.23) | copy-start | bytes 196
  15.8 13.1 %collective-permute-start.2 = (bf16[64,1408]{1,0:T(8,128)(2,1)S(1)}, bf16[64,1408]{1,0:T(8,128)(2,1)S(1)}, u32[]{:S(2)}, u32[]{:S(2)}) collective-permute-start(bf16[64,1408]{1,0:T(8,128)(2,1)S(1)} %get-tuple-element.123), channel_id=1, source_target_pairs={{0,3},{1,0},{2,1},{3,2},{4,7},{5,4},{6,5},{7,6},{8,11},{9,8},{10,9... | collective-permute-start | bytes 540680 | tf_op jit(solution)/shard_map/ppermute | solution.py:34
  19.7 4.7 %collective-permute-start.8 = (bf16[16,2048]{1,0:T(8,128)(2,1)S(1)}, bf16[16,2048]{1,0:T(8,128)(2,1)S(1)}, u32[]{:S(2)}, u32[]{:S(2)}) collective-permute-start(bf16[16,2048]{1,0:T(8,128)(2,1)S(1)} %slice.23), channel_id=1, source_target_pairs={{0,8},{4,12},{8,16},{12,20},{16,24},{20,28},{1,9},{5,13},{9,17},{1... | collective-permute-start | bytes 196616 | tf_op jit(solution)/shard_map/ppermute | solution.py:654
  22.3 8.7 %collective-permute-start.6 = (bf16[512,256]{1,0:T(8,128)(2,1)S(1)}, bf16[512,256]{1,0:T(8,128)(2,1)S(1)}, u32[]{:S(2)}, u32[]{:S(2)}) collective-permute-start(bf16[512,256]{1,0:T(8,128)(2,1)S(1)} %slice.21), channel_id=1, source_target_pairs={{0,8},{4,12},{8,0},{12,4},{16,24},{20,28},{24,16},{28,20},{1,9},{5... | collective-permute-start | bytes 786440 | tf_op jit(solution)/shard_map/ppermute | solution.py:29
  24.2 11.3 %copy-start.1 = (f32[64,8192]{1,0:T(8,128)S(1)}, f32[64,8192]{1,0:T(8,128)}, u32[]{:S(2)}) copy-start(f32[64,8192]{1,0:T(8,128)} %w_ref.3) | copy-start | bytes 6291460
  24.4 8.4 %collective-permute-start.7 = (bf16[512,256]{1,0:T(8,128)(2,1)S(1)}, bf16[512,256]{1,0:T(8,128)(2,1)S(1)}, u32[]{:S(2)}, u32[]{:S(2)}) collective-permute-start(bf16[512,256]{1,0:T(8,128)(2,1)S(1)} %slice.22), channel_id=1, source_target_pairs={{0,16},{4,20},{8,24},{12,28},{16,0},{20,4},{24,8},{28,12},{1,17},{... | collective-permute-start | bytes 786440 | tf_op jit(solution)/shard_map/ppermute | solution.py:29
  33.4 15.3 %collective-permute-start.10 = (bf16[256,1408]{1,0:T(8,128)(2,1)S(1)}, bf16[256,1408]{1,0:T(8,128)(2,1)S(1)}, u32[]{:S(2)}, u32[]{:S(2)}) collective-permute-start(bf16[256,1408]{1,0:T(8,128)(2,1)S(1)} %assemble_x.1.refs_0_), channel_id=1, source_target_pairs={{0,16},{4,20},{8,24},{12,28},{16,0},{20,4},{24,8},{28,12},{1,17},{... | collective-permute-start | bytes 2162696 | tf_op jit(solution)/shard_map/ppermute | solution.py:29
  35.5 14.3 %collective-permute-start.9 = (bf16[256,1408]{1,0:T(8,128)(2,1)S(1)}, bf16[256,1408]{1,0:T(8,128)(2,1)S(1)}, u32[]{:S(2)}, u32[]{:S(2)}) collective-permute-start(bf16[256,1408]{1,0:T(8,128)(2,1)S(1)} %assemble_x.1.refs_0_), channel_id=1, source_target_pairs={{0,8},{4,12},{8,0},{12,4},{16,24},{20,28},{24,16},{28,20},{1,9},{5... | collective-permute-start | bytes 2162696 | tf_op jit(solution)/shard_map/ppermute | solution.py:29
  36.1 6.9 %collective-permute-start.11 = (bf16[64,1024]{1,0:T(8,128)(2,1)S(1)}, bf16[64,1024]{1,0:T(8,128)(2,1)S(1)}, u32[]{:S(2)}, u32[]{:S(2)}) collective-permute-start(bf16[64,1024]{1,0:T(8,128)(2,1)S(1)} %get-tuple-element.139), channel_id=1, source_target_pairs={{0,1},{1,2},{2,3},{3,0},{4,5},{5,6},{6,7},{7,4},{8,9},{9,10},{10,1... | collective-permute-start | bytes 393224 | tf_op jit(solution)/shard_map/ppermute | solution.py:34
  38.1 8.7 %collective-permute-start.12 = (bf16[64,1024]{1,0:T(8,128)(2,1)S(1)}, bf16[64,1024]{1,0:T(8,128)(2,1)S(1)}, u32[]{:S(2)}, u32[]{:S(2)}) collective-permute-start(bf16[64,1024]{1,0:T(8,128)(2,1)S(1)} %get-tuple-element.140), channel_id=1, source_target_pairs={{0,2},{1,3},{2,0},{3,1},{4,6},{5,7},{6,4},{7,5},{8,10},{9,11},{10,... | collective-permute-start | bytes 393224 | tf_op jit(solution)/shard_map/ppermute | solution.py:34
  40.6 6.2 %collective-permute-start.13 = (bf16[64,1024]{1,0:T(8,128)(2,1)S(1)}, bf16[64,1024]{1,0:T(8,128)(2,1)S(1)}, u32[]{:S(2)}, u32[]{:S(2)}) collective-permute-start(bf16[64,1024]{1,0:T(8,128)(2,1)S(1)} %get-tuple-element.141), channel_id=1, source_target_pairs={{0,3},{1,0},{2,1},{3,2},{4,7},{5,4},{6,5},{7,6},{8,11},{9,8},{10,9... | collective-permute-start | bytes 393224 | tf_op jit(solution)/shard_map/ppermute | solution.py:34
  49.9 3.7 %collective-permute-start.16 = (bf16[256,1408]{1,0:T(8,128)(2,1)S(1)}, bf16[256,1408]{1,0:T(8,128)(2,1)S(1)}, u32[]{:S(2)}, u32[]{:S(2)}) collective-permute-start(bf16[256,1408]{1,0:T(8,128)(2,1)S(1)} %collective-permute-done.9.refs_1_), channel_id=1, source_target_pairs={{0,4},{4,0},{8,12},{12,8},{16,20},{20,16},{24,28},{28,24},{1,5},{5... | collective-permute-start | bytes 2162696 | tf_op jit(solution)/shard_map/ppermute | solution.py:29
  49.9 4.1 %collective-permute-start.17 = (bf16[256,1408]{1,0:T(8,128)(2,1)S(1)}, bf16[256,1408]{1,0:T(8,128)(2,1)S(1)}, u32[]{:S(2)}, u32[]{:S(2)}) collective-permute-start(bf16[256,1408]{1,0:T(8,128)(2,1)S(1)} %collective-permute-done.10.refs_2_), channel_id=1, source_target_pairs={{0,4},{4,0},{8,12},{12,8},{16,20},{20,16},{24,28},{28,24},{1,5},{5... | collective-permute-start | bytes 2162696 | tf_op jit(solution)/shard_map/ppermute | solution.py:29
  51.0 2.5 %collective-permute-start.18 = (bf16[256,512]{1,0:T(8,128)(2,1)S(1)}, bf16[256,512]{1,0:T(8,128)(2,1)S(1)}, u32[]{:S(2)}, u32[]{:S(2)}) collective-permute-start(bf16[256,512]{1,0:T(8,128)(2,1)S(1)} %get-tuple-element.149), channel_id=1, source_target_pairs={{0,4},{4,0},{8,12},{12,8},{16,20},{20,16},{24,28},{28,24},{1,5},{5... | collective-permute-start | bytes 786440 | tf_op jit(solution)/shard_map/ppermute | solution.py:29
  51.1 10.9 %collective-permute-start.14 = (bf16[128,1408]{1,0:T(8,128)(2,1)S(1)}, bf16[128,1408]{1,0:T(8,128)(2,1)S(1)}, u32[]{:S(2)}, u32[]{:S(2)}) collective-permute-start(bf16[128,1408]{1,0:T(8,128)(2,1)S(1)} %slice.24), channel_id=1, source_target_pairs={{0,8},{4,12},{8,0},{12,4},{16,24},{20,28},{24,16},{28,20},{1,9},{5... | collective-permute-start | bytes 1081352 | tf_op jit(solution)/shard_map/ppermute | solution.py:29
  51.5 10.6 %collective-permute-start.15 = (bf16[128,1408]{1,0:T(8,128)(2,1)S(1)}, bf16[128,1408]{1,0:T(8,128)(2,1)S(1)}, u32[]{:S(2)}, u32[]{:S(2)}) collective-permute-start(bf16[128,1408]{1,0:T(8,128)(2,1)S(1)} %slice.25), channel_id=1, source_target_pairs={{0,16},{4,20},{8,24},{12,28},{16,0},{20,4},{24,8},{28,12},{1,17},{... | collective-permute-start | bytes 1081352 | tf_op jit(solution)/shard_map/ppermute | solution.py:29
  53.5 9.6 %collective-permute-start.19 = (bf16[256,1408]{1,0:T(8,128)(2,1)S(1)}, bf16[256,1408]{1,0:T(8,128)(2,1)S(1)}, u32[]{:S(2)}, u32[]{:S(2)}) collective-permute-start(bf16[256,1408]{1,0:T(8,128)(2,1)S(1)} %assemble_x.1.refs_0_), channel_id=1, source_target_pairs={{0,4},{4,0},{8,12},{12,8},{16,20},{20,16},{24,28},{28,24},{1,5},{5... | collective-permute-start | bytes 2162696 | tf_op jit(solution)/shard_map/ppermute | solution.py:29
  53.6 9.0 %collective-permute-start.29 = (bf16[512,256]{1,0:T(8,128)(2,1)S(1)}, bf16[512,256]{1,0:T(8,128)(2,1)S(1)}, u32[]{:S(2)}, u32[]{:S(2)}) collective-permute-start(bf16[512,256]{1,0:T(8,128)(2,1)S(1)} %collective-permute-done.6.refs_3_), channel_id=1, source_target_pairs={{0,4},{4,0},{8,12},{12,8},{16,20},{20,16},{24,28},{28,24},{1,5},{5... | collective-permute-start | bytes 786440 | tf_op jit(solution)/shard_map/ppermute | solution.py:29
  54.0 8.6 %collective-permute-start.30 = (bf16[512,256]{1,0:T(8,128)(2,1)S(1)}, bf16[512,256]{1,0:T(8,128)(2,1)S(1)}, u32[]{:S(2)}, u32[]{:S(2)}) collective-permute-start(bf16[512,256]{1,0:T(8,128)(2,1)S(1)} %collective-permute-done.7.refs_4_), channel_id=1, source_target_pairs={{0,4},{4,0},{8,12},{12,8},{16,20},{20,16},{24,28},{28,24},{1,5},{5... | collective-permute-start | bytes 786440 | tf_op jit(solution)/shard_map/ppermute | solution.py:29
  62.1 1.7 %collective-permute-start.20 = (bf16[128,1408]{1,0:T(8,128)(2,1)S(1)}, bf16[128,1408]{1,0:T(8,128)(2,1)S(1)}, u32[]{:S(2)}, u32[]{:S(2)}) collective-permute-start(bf16[128,1408]{1,0:T(8,128)(2,1)S(1)} %collective-permute-done.14.refs_3_), channel_id=1, source_target_pairs={{0,4},{4,0},{8,12},{12,8},{16,20},{20,16},{24,28},{28,24},{1,5},{5... | collective-permute-start | bytes 1081352 | tf_op jit(solution)/shard_map/ppermute | solution.py:29
  62.1 3.3 %collective-permute-start.21 = (bf16[128,1408]{1,0:T(8,128)(2,1)S(1)}, bf16[128,1408]{1,0:T(8,128)(2,1)S(1)}, u32[]{:S(2)}, u32[]{:S(2)}) collective-permute-start(bf16[128,1408]{1,0:T(8,128)(2,1)S(1)} %collective-permute-done.15.refs_4_), channel_id=1, source_target_pairs={{0,4},{4,0},{8,12},{12,8},{16,20},{20,16},{24,28},{28,24},{1,5},{5... | collective-permute-start | bytes 1081352 | tf_op jit(solution)/shard_map/ppermute | solution.py:29
  62.6 9.9 %collective-permute-start.26 = (bf16[1024,256]{1,0:T(8,128)(2,1)S(1)}, bf16[1024,256]{1,0:T(8,128)(2,1)S(1)}, u32[]{:S(2)}, u32[]{:S(2)}) collective-permute-start(bf16[1024,256]{1,0:T(8,128)(2,1)S(1)} %convert_element_type.10.refs_0_), channel_id=1, source_target_pairs={{0,4},{4,0},{8,12},{12,8},{16,20},{20,16},{24,28},{28,24},{1,5},{5... | collective-permute-start | bytes 1572872 | tf_op jit(solution)/shard_map/ppermute | solution.py:29
  62.6 10.7 %collective-permute-start.27 = (bf16[1024,256]{1,0:T(8,128)(2,1)S(1)}, bf16[1024,256]{1,0:T(8,128)(2,1)S(1)}, u32[]{:S(2)}, u32[]{:S(2)}) collective-permute-start(bf16[1024,256]{1,0:T(8,128)(2,1)S(1)} %collective-permute-done.3.refs_1_), channel_id=1, source_target_pairs={{0,4},{4,0},{8,12},{12,8},{16,20},{20,16},{24,28},{28,24},{1,5},{5... | collective-permute-start | bytes 1572872 | tf_op jit(solution)/shard_map/ppermute | solution.py:29
  63.1 17.1 %collective-permute-start.28 = (bf16[1024,256]{1,0:T(8,128)(2,1)S(1)}, bf16[1024,256]{1,0:T(8,128)(2,1)S(1)}, u32[]{:S(2)}, u32[]{:S(2)}) collective-permute-start(bf16[1024,256]{1,0:T(8,128)(2,1)S(1)} %collective-permute-done.4.refs_2_), channel_id=1, source_target_pairs={{0,4},{4,0},{8,12},{12,8},{16,20},{20,16},{24,28},{28,24},{1,5},{5... | collective-permute-start | bytes 1572872 | tf_op jit(solution)/shard_map/ppermute | solution.py:29
  63.7 16.5 %collective-permute-start.24 = (bf16[512,512]{1,0:T(8,128)(2,1)S(1)}, bf16[512,512]{1,0:T(8,128)(2,1)S(1)}, u32[]{:S(2)}, u32[]{:S(2)}) collective-permute-start(bf16[512,512]{1,0:T(8,128)(2,1)S(1)} %merge_z.1.refs_0_), channel_id=1, source_target_pairs={{0,8},{4,12},{8,0},{12,4},{16,24},{20,28},{24,16},{28,20},{1,9},{5... | collective-permute-start | bytes 1572872 | tf_op jit(solution)/shard_map/ppermute | solution.py:29
  65.4 14.8 %collective-permute-start.25 = (bf16[512,512]{1,0:T(8,128)(2,1)S(1)}, bf16[512,512]{1,0:T(8,128)(2,1)S(1)}, u32[]{:S(2)}, u32[]{:S(2)}) collective-permute-start(bf16[512,512]{1,0:T(8,128)(2,1)S(1)} %merge_z.1.refs_0_), channel_id=1, source_target_pairs={{0,16},{4,20},{8,24},{12,28},{16,0},{20,4},{24,8},{28,12},{1,17},{... | collective-permute-start | bytes 1572872 | tf_op jit(solution)/shard_map/ppermute | solution.py:29
  72.5 11.2 %collective-permute-start.22 = (bf16[2,544,128]{2,1,0:T(8,128)(2,1)S(1)}, bf16[2,544,128]{2,1,0:T(8,128)(2,1)S(1)}, u32[]{:S(2)}, u32[]{:S(2)}) collective-permute-start(bf16[2,544,128]{2,1,0:T(8,128)(2,1)S(1)} %get-tuple-element.198.refs_0_), channel_id=1, source_target_pairs={{0,8},{4,12},{8,0},{12,4},{16,24},{20,28},{24,16},{28,20},{1,9},{5... | collective-permute-start | bytes 835592 | tf_op jit(solution)/shard_map/ppermute | solution.py:29
  73.3 11.8 %collective-permute-start.23 = (bf16[2,544,128]{2,1,0:T(8,128)(2,1)S(1)}, bf16[2,544,128]{2,1,0:T(8,128)(2,1)S(1)}, u32[]{:S(2)}, u32[]{:S(2)}) collective-permute-start(bf16[2,544,128]{2,1,0:T(8,128)(2,1)S(1)} %get-tuple-element.198.refs_0_), channel_id=1, source_target_pairs={{0,16},{4,20},{8,24},{12,28},{16,0},{20,4},{24,8},{28,12},{1,17},{... | collective-permute-start | bytes 835592 | tf_op jit(solution)/shard_map/ppermute | solution.py:29
  85.1 9.6 %collective-permute-start.31 = (bf16[2,544,128]{2,1,0:T(8,128)(2,1)S(1)}, bf16[2,544,128]{2,1,0:T(8,128)(2,1)S(1)}, u32[]{:S(2)}, u32[]{:S(2)}) collective-permute-start(bf16[2,544,128]{2,1,0:T(8,128)(2,1)S(1)} %get-tuple-element.199.refs_1_), channel_id=1, source_target_pairs={{0,8},{4,12},{8,0},{12,4},{16,24},{20,28},{24,16},{28,20},{1,9},{5... | collective-permute-start | bytes 835592 | tf_op jit(solution)/shard_map/ppermute | solution.py:29
  85.9 9.6 %collective-permute-start.32 = (bf16[2,544,128]{2,1,0:T(8,128)(2,1)S(1)}, bf16[2,544,128]{2,1,0:T(8,128)(2,1)S(1)}, u32[]{:S(2)}, u32[]{:S(2)}) collective-permute-start(bf16[2,544,128]{2,1,0:T(8,128)(2,1)S(1)} %get-tuple-element.199.refs_1_), channel_id=1, source_target_pairs={{0,16},{4,20},{8,24},{12,28},{16,0},{20,4},{24,8},{28,12},{1,17},{... | collective-permute-start | bytes 835592 | tf_op jit(solution)/shard_map/ppermute | solution.py:29
  86.5 14.9 %collective-permute-start.35 = (bf16[256,512]{1,0:T(8,128)(2,1)S(1)}, bf16[256,512]{1,0:T(8,128)(2,1)S(1)}, u32[]{:S(2)}, u32[]{:S(2)}) collective-permute-start(bf16[256,512]{1,0:T(8,128)(2,1)S(1)} %slice.26), channel_id=1, source_target_pairs={{0,8},{4,12},{8,0},{12,4},{16,24},{20,28},{24,16},{28,20},{1,9},{5... | collective-permute-start | bytes 786440 | tf_op jit(solution)/shard_map/ppermute | solution.py:29
  87.8 13.6 %collective-permute-start.36 = (bf16[256,512]{1,0:T(8,128)(2,1)S(1)}, bf16[256,512]{1,0:T(8,128)(2,1)S(1)}, u32[]{:S(2)}, u32[]{:S(2)}) collective-permute-start(bf16[256,512]{1,0:T(8,128)(2,1)S(1)} %slice.27), channel_id=1, source_target_pairs={{0,16},{4,20},{8,24},{12,28},{16,0},{20,4},{24,8},{28,12},{1,17},{... | collective-permute-start | bytes 786440 | tf_op jit(solution)/shard_map/ppermute | solution.py:29
  91.7 12.5 %collective-permute-start.33 = (bf16[2,544,128]{2,1,0:T(8,128)(2,1)S(1)}, bf16[2,544,128]{2,1,0:T(8,128)(2,1)S(1)}, u32[]{:S(2)}, u32[]{:S(2)}) collective-permute-start(bf16[2,544,128]{2,1,0:T(8,128)(2,1)S(1)} %collective-permute-done.23.refs_4_), channel_id=1, source_target_pairs={{0,8},{4,12},{8,0},{12,4},{16,24},{20,28},{24,16},{28,20},{1,9},{5... | collective-permute-start | bytes 835592 | tf_op jit(solution)/shard_map/ppermute | solution.py:29
  95.5 9.6 %collective-permute-start.34 = (bf16[2,544,128]{2,1,0:T(8,128)(2,1)S(1)}, bf16[2,544,128]{2,1,0:T(8,128)(2,1)S(1)}, u32[]{:S(2)}, u32[]{:S(2)}) collective-permute-start(bf16[2,544,128]{2,1,0:T(8,128)(2,1)S(1)} %collective-permute-done.31.refs_3_), channel_id=1, source_target_pairs={{0,16},{4,20},{8,24},{12,28},{16,0},{20,4},{24,8},{28,12},{1,17},{... | collective-permute-start | bytes 835592 | tf_op jit(solution)/shard_map/ppermute | solution.py:29
  107.2 2.2 %collective-permute-start.37 = (bf16[512,640]{1,0:T(8,128)(2,1)S(1)}, bf16[512,640]{1,0:T(8,128)(2,1)S(1)}, u32[]{:S(2)}, u32[]{:S(2)}) collective-permute-start(bf16[512,640]{1,0:T(8,128)(2,1)S(1)} %get-tuple-element.215), channel_id=1, source_target_pairs={{0,4},{4,0},{8,12},{12,8},{16,20},{20,16},{24,28},{28,24},{1,5},{5... | collective-permute-start | bytes 1966088 | tf_op jit(solution)/shard_map/ppermute | solution.py:29
  107.3 23.2 %collective-permute-start.46 = (bf16[2,512,128]{2,1,0:T(8,128)(2,1)S(1)}, bf16[2,512,128]{2,1,0:T(8,128)(2,1)S(1)}, u32[]{:S(2)}, u32[]{:S(2)}) collective-permute-start(bf16[2,512,128]{2,1,0:T(8,128)(2,1)S(1)} %get-tuple-element.237), channel_id=1, source_target_pairs={{0,4},{4,0},{8,12},{12,8},{16,20},{20,16},{24,28},{28,24},{1,5},{5... | collective-permute-start | bytes 786440 | tf_op jit(solution)/shard_map/ppermute | solution.py:29
  111.4 17.9 %collective-permute-start.39 = (bf16[128,1152]{1,0:T(8,128)(2,1)S(1)}, bf16[128,1152]{1,0:T(8,128)(2,1)S(1)}, u32[]{:S(2)}, u32[]{:S(2)}) collective-permute-start(bf16[128,1152]{1,0:T(8,128)(2,1)S(1)} %get-tuple-element.222), channel_id=1, source_target_pairs={{0,1},{1,0},{2,3},{3,2},{4,5},{5,4},{6,7},{7,6},{8,9},{9,8},{10,11... | collective-permute-start | bytes 884744 | tf_op jit(solution)/shard_map/ppermute | solution.py:533
  112.7 13.4 %collective-permute-start.38 = (bf16[128,1024]{1,0:T(8,128)(2,1)S(1)}, bf16[128,1024]{1,0:T(8,128)(2,1)S(1)}, u32[]{:S(2)}, u32[]{:S(2)}) collective-permute-start(bf16[128,1024]{1,0:T(8,128)(2,1)S(1)} %get-tuple-element.221), channel_id=1, source_target_pairs={{0,1},{1,0},{2,3},{3,2},{4,5},{5,4},{6,7},{7,6},{8,9},{9,8},{10,11... | collective-permute-start | bytes 786440 | tf_op jit(solution)/shard_map/ppermute | solution.py:533
  115.8 19.9 %collective-permute-start.42 = (bf16[128,1024]{1,0:T(8,128)(2,1)S(1)}, bf16[128,1024]{1,0:T(8,128)(2,1)S(1)}, u32[]{:S(2)}, u32[]{:S(2)}) collective-permute-start(bf16[128,1024]{1,0:T(8,128)(2,1)S(1)} %get-tuple-element.234), channel_id=1, source_target_pairs={{1,2},{2,1},{0,0},{3,3},{5,6},{6,5},{4,4},{7,7},{9,10},{10,9},{8,8... | collective-permute-start | bytes 786440 | tf_op jit(solution)/shard_map/ppermute | solution.py:533
  116.5 32.2 %collective-permute-start.43 = (bf16[128,1152]{1,0:T(8,128)(2,1)S(1)}, bf16[128,1152]{1,0:T(8,128)(2,1)S(1)}, u32[]{:S(2)}, u32[]{:S(2)}) collective-permute-start(bf16[128,1152]{1,0:T(8,128)(2,1)S(1)} %get-tuple-element.235), channel_id=1, source_target_pairs={{1,2},{2,1},{0,0},{3,3},{5,6},{6,5},{4,4},{7,7},{9,10},{10,9},{8,8... | collective-permute-start | bytes 884744 | tf_op jit(solution)/shard_map/ppermute | solution.py:533
  126.1 22.6 %collective-permute-start.45 = (bf16[128,1152]{1,0:T(8,128)(2,1)S(1)}, bf16[128,1152]{1,0:T(8,128)(2,1)S(1)}, u32[]{:S(2)}, u32[]{:S(2)}) collective-permute-start(bf16[128,1152]{1,0:T(8,128)(2,1)S(1)} %get-tuple-element.235), channel_id=1, source_target_pairs={{0,1},{3,2},{4,5},{7,6},{8,9},{11,10},{12,13},{15,14},{16,17},{19,... | collective-permute-start | bytes 884744 | tf_op jit(solution)/shard_map/ppermute | solution.py:533
  130.0 26.5 %collective-permute-start.41 = (bf16[128,1152]{1,0:T(8,128)(2,1)S(1)}, bf16[128,1152]{1,0:T(8,128)(2,1)S(1)}, u32[]{:S(2)}, u32[]{:S(2)}) collective-permute-start(bf16[128,1152]{1,0:T(8,128)(2,1)S(1)} %add_far.3), channel_id=1, source_target_pairs={{0,2},{1,3},{2,0},{3,1},{4,6},{5,7},{6,4},{7,5},{8,10},{9,11},{10,... | collective-permute-start | bytes 884744 | tf_op jit(solution)/shard_map/ppermute | solution.py:34
  130.5 18.2 %collective-permute-start.44 = (bf16[128,1024]{1,0:T(8,128)(2,1)S(1)}, bf16[128,1024]{1,0:T(8,128)(2,1)S(1)}, u32[]{:S(2)}, u32[]{:S(2)}) collective-permute-start(bf16[128,1024]{1,0:T(8,128)(2,1)S(1)} %get-tuple-element.234), channel_id=1, source_target_pairs={{0,1},{3,2},{4,5},{7,6},{8,9},{11,10},{12,13},{15,14},{16,17},{19,... | collective-permute-start | bytes 786440 | tf_op jit(solution)/shard_map/ppermute | solution.py:533
  135.7 20.8 %collective-permute-start.40 = (bf16[128,1024]{1,0:T(8,128)(2,1)S(1)}, bf16[128,1024]{1,0:T(8,128)(2,1)S(1)}, u32[]{:S(2)}, u32[]{:S(2)}) collective-permute-start(bf16[128,1024]{1,0:T(8,128)(2,1)S(1)} %add_far.2), channel_id=1, source_target_pairs={{0,2},{1,3},{2,0},{3,1},{4,6},{5,7},{6,4},{7,5},{8,10},{9,11},{10,... | collective-permute-start | bytes 786440 | tf_op jit(solution)/shard_map/ppermute | solution.py:34
where the time goes:
time: 159 us; the launch traced here: 158 us
  waiting for transfers between devices  59 us (37%)
  starting transfers between devices  52.4 us (33%)
  Pallas kernels  36.2 us (23%)
  other arithmetic  5.36 us (3%)
  local copies, waits for them, and re-layouts  4.2 us (3%)
    ppermute x32, starting transfers between devices, flip(): return lax.ppermute(x, 'seq', [(i, i ^ bits) for i in range(count)])  26.8 us
    ppermute x32, waiting for transfers between devices, flip(): return lax.ppermute(x, 'seq', [(i, i ^ bits) for i in range(count)])  25.6 us
    ppermute x6, waiting for transfers between devices, send(): return [lax.ppermute(x, 'tp', pairs) for x in block]  20.7 us
    ppermute x8, waiting for transfers between devices, shift(): return lax.ppermute(x, 'tp', [(i, (i + by) % count) for i in range(count)])  12.5 us
    pallas_call x2, Pallas kernels, front(): call(functools.partial(front_kernel, (inner, bc_width, heads, prompts, wh...  12.2 us
    ppermute x8, starting transfers between devices, shift(): return lax.ppermute(x, 'tp', [(i, (i + by) % count) for i in range(count)])  12 us
    ppermute x6, starting transfers between devices, send(): return [lax.ppermute(x, 'tp', pairs) for x in block]  11.2 us
    pallas_call x2, Pallas kernels, on_device(): call(functools.partial(gate_kernel, chosen, 2 * depth, len(gate) > 0), [s...  5.07 us
  transfers between devices with their start and end apart: 47, of which 21 were waited for; matrix products, arithmetic and copies ran while one was open for 4% of the time, Pallas kernels for 20%

commit v1 on v0

--- a/solution.py
+++ b/solution.py
@@ -440,6 +440,10 @@
             gating(sizes, ints_ref, low_states, vecs, side, *sides[side], mine)
 
 
+def goes_whole(i, tp_count):
+    return tp_count == 4 and i == 2
+
+
 def is_inner(t):
     return (t == 1) | (t == 2)
 
@@ -476,21 +480,25 @@
     piece_rows = mine.shape[0] // tp_count
     own_rows = rows_at(c * inner, inner)
     other_rows = rows_at((1 - c) * inner, inner)
-    for i, low, high in zip(chosen, outs[::2], outs[1::2]):
+    outs = list(outs)
+    for i in chosen:
+        sides = [(outs.pop(0), 0)] if goes_whole(i, tp_count) else []
+        sides = sides * 2 or [(outs.pop(0), 0), (outs.pop(0), width // 2)]
+        last, last_at = sides[1]
         rows = rows_at(block_places(t, tp_count)[i] * piece_rows, piece_rows)
         sums = jnp.sum(
             mine[rows, inner:].astype(F32) + theirs[rows, inner:].astype(F32), axis=1, keepdims=True
         )
         sums = spread_terms(jnp.broadcast_to(sums, (piece_rows, LANES)))
-        high[:, width // 2 :] = sums.astype(high.dtype)
+        last[:, width - last_at :] = sums.astype(last.dtype)
         for at in range(0, width, width // 4):
             lanes = slice(at, at + width // 4)
             value = jnp.dot(mine[rows, :inner], weights[own_rows, lanes], preferred_element_type=F32)
             value = value + jnp.dot(
                 theirs[rows, :inner], weights[other_rows, lanes], preferred_element_type=F32
             )
-            out, first = (low, at) if at < width // 2 else (high, at - width // 2)
-            out[:, first : first + width // 4] = value.astype(out.dtype)
+            out, start = sides[at // (width // 2)]
+            out[:, at - start : at - start + width // 4] = value.astype(out.dtype)
 
 
 def add_kernel(width, ints, got, own, out):
@@ -503,9 +511,14 @@
 
 
 def final_kernel(channels, takers, ints, *refs):
-    own, received, out = refs[:2], refs[2:-1], refs[-1]
-    half = out.shape[1] // 2
+    own, refs, out = refs[:2], list(refs[2:-1]), refs[-1]
+    width = out.shape[1]
+    half = width // 2
     inside = is_inner(ints[0])
+    received = []
+    for whole, inner in takers:
+        low = refs.pop(0)
+        received.append((low, low if whole else refs.pop(0), half if whole else 0, inner))
 
     def taken(value, inner):
         if inner is None:
@@ -513,21 +526,22 @@
         return jnp.where(inside, value, 0.0) if inner else jnp.where(inside, 0.0, value)
 
     squares = added_terms(own[1], half)
-    for got, inner in zip(received[1::2], takers):
-        squares = squares + taken(added_terms(got, half), inner)
+    for _, high, skipped, inner in received:
+        squares = squares + taken(added_terms(high, skipped + half), inner)
     factor = lax.rsqrt(squares[:, :1] / channels + epsilon)
     for side in range(2):
         total = own[side][:, :half]
-        for got, inner in zip(received[side::2], takers):
-            total = total + taken(got[:, :half].astype(F32), inner)
+        for low, high, skipped, inner in received:
+            got = high[:, skipped : skipped + half] if side else low[:, :half]
+            total = total + taken(got.astype(F32), inner)
         out[:, side * half : (side + 1) * half] = (total * factor).astype(out.dtype)
 
 
-def sum_over_tp(ints, blocks, own):
+def sum_over_tp(ints, blocks, own, later):
     tp_count = lax.axis_size("tp")
     if tp_count != 4:
         received = [[shift(x, j + 1) for x in block] for j, block in enumerate(blocks)]
-        return own, received, (None,) * (tp_count - 1)
+        return own, received, ((False, None),) * (tp_count - 1), later
 
     def send(block, pairs):
         return [lax.ppermute(x, "tp", pairs) for x in block]
@@ -539,13 +553,14 @@
 
     first, second, third = blocks
     beside = send(first, [(0, 1), (1, 0), (2, 3), (3, 2)])
+    to_inner = send(third, [(0, 1), (3, 2)])
     to_middle = send(third, [(1, 2), (2, 1), (0, 0), (3, 3)])
-    to_inner = send(third, [(0, 1), (3, 2)])
-    joined = lax.optimization_barrier((*beside, *second, *own))
-    beside, second, own = list(joined[:2]), joined[2:4], list(joined[4:])
+    joined = lax.optimization_barrier((*beside, *second, *own, later))
+    beside, second, own, later = list(joined[:2]), joined[2:4], list(joined[4:6]), joined[6]
     second = [add(got, x, "add_far") for got, x in zip(beside, second)]
     across = [shift(x, 2) for x in second]
-    return own, [beside, across, to_middle, to_inner], (False, None, True, True)
+    takers = ((False, False), (False, None), (True, True), (True, True))
+    return own, [beside, across, to_middle, to_inner], takers, later
 
 
 def on_device(
@@ -801,9 +816,13 @@
 
     def project_out(chosen, outs, where, operands):
         scratch, extra = [], []
-        outs = [
-            sds((piece, out_width // 2 + side * LANES), kind) for kind in outs for side in range(2)
-        ]
+        shapes = []
+        for i, kind in zip(chosen, outs):
+            if goes_whole(i, tp_count):
+                shapes.append(sds((piece, out_width + LANES), kind))
+            else:
+                shapes += [sds((piece, out_width // 2 + side * LANES), kind) for side in range(2)]
+        outs = shapes
         if where:
             extra = [sds((2 * inner, out_width), MM)]
             scratch = [pltpu.SemaphoreType.DMA((len(where),))]
@@ -821,10 +840,11 @@
     *sent_next, own_low, own_high = project_out(
         tuple(range(ahead, tp_count)), [MM] * (tp_count - 1 - ahead) + [F32], (), [out_weights]
     )
-    halves = [*sent_first, *sent_next]
-    own, received, takers = sum_over_tp(
-        ints, [halves[i : i + 2] for i in range(0, len(halves), 2)], [own_low, own_high]
-    )
+    sent_all, blocks = [*sent_first, *sent_next], []
+    for i in range(tp_count - 1):
+        size = 1 if goes_whole(i, tp_count) else 2
+        blocks, sent_all = blocks + [sent_all[:size]], sent_all[size:]
+    own, received, takers, asked = sum_over_tp(ints, blocks, [own_low, own_high], asked)
     received = [half for block in received for half in block]
     (mixed,) = call(
         functools.partial(final_kernel, float(inner_all), takers),

time: 159 us -> 159 us (level)
    ppermute x6 -> x4, waiting for transfers between devices: 20.7 us -> 9.2 us  [send(): return [lax.ppermute(x, 'tp', pairs) for x in block]]
    ppermute x8, waiting for transfers between devices: 12.5 us -> 23.6 us  [shift(): return lax.ppermute(x, 'tp', [(i, (i + by) % count) for i in range(count)])]
    ppermute x8, starting transfers between devices: 12 us -> 14.7 us  [shift(): return lax.ppermute(x, 'tp', [(i, (i + by) % count) for i in range(count)])]
    ppermute x6 -> x4, starting transfers between devices: 11.2 us -> 8.8 us  [send(): return [lax.ppermute(x, 'tp', pairs) for x in block]]
  transfers between devices with their start and end apart: 47 -> 45, of which waited for: 21 -> 21; matrix products, arithmetic and copies ran while one was open for 4% -> 4% of each run, Pallas kernels for 20% -> 19%
where the time goes in v1:
time: 159 us; the launch traced here: 158 us
  waiting for transfers between devices  59.1 us (37%)
  starting transfers between devices  52.3 us (33%)
  Pallas kernels  36.4 us (23%)
  other arithmetic  5.36 us (3%)
  local copies, waits for them, and re-layouts  4.2 us (3%)
    ppermute x32, starting transfers between devices, flip(): return lax.ppermute(x, 'seq', [(i, i ^ bits) for i in range(count)])  26.3 us
    ppermute x32, waiting for transfers between devices, flip(): return lax.ppermute(x, 'seq', [(i, i ^ bits) for i in range(count)])  26.1 us
    ppermute x8, waiting for transfers between devices, shift(): return lax.ppermute(x, 'tp', [(i, (i + by) % count) for i in range(count)])  23.6 us
    ppermute x8, starting transfers between devices, shift(): return lax.ppermute(x, 'tp', [(i, (i + by) % count) for i in range(count)])  14.7 us
    pallas_call x2, Pallas kernels, front(): call(functools.partial(front_kernel, (inner, bc_width, heads, prompts, wh...  12.2 us
    ppermute x4, waiting for transfers between devices, send(): return [lax.ppermute(x, 'tp', pairs) for x in block]  9.2 us
    ppermute x4, starting transfers between devices, send(): return [lax.ppermute(x, 'tp', pairs) for x in block]  8.8 us
    pallas_call x2, Pallas kernels, on_device(): call(functools.partial(gate_kernel, chosen, 2 * depth, len(gate) > 0), [s...  5.07 us
  transfers between devices with their start and end apart: 45, of which 21 were waited for; matrix products, arithmetic and copies ran while one was open for 4% of the time, Pallas kernels for 19%

profile of v1, /device:TPU:0, one launch (start us, length us, event | category | flops | bytes accessed | tf_op | source)
XLA Modules:
  0.0 158.5 jit_solution(14035409075528885551)
XLA Ops:
  1.2 1.3 convert_element_type.10.refs_0_
  2.5 2.6 %collective-permute-start.3 = (bf16[1024,256]{1,0:T(8,128)(2,1)S(1)}, bf16[1024,256]{1,0:T(8,128)(2,1)S(1)}, u32[]{:S(2)}, u32[]{:S(2)}) collective-permute-start(bf16[1024,256]{1,0:T(8,128)(2,1)S(1)} %convert_element_type.10.refs_0_), channel_id=1, source_target_pairs={{0,8},{4,12},{8,0},{12,4},{16,24},{20,28},{24,16},{28,20},{1,9},{5... | collective-permute-start | bytes 1572872 | tf_op jit(solution)/shard_map/ppermute | solution.py:29
  5.0 1.5 collective-permute-start.4
  6.6 0.7 concatenate.18.ints.ints_ref
  7.3 1.6 %copy-done = f32[64,8192]{1,0:T(8,128)S(1)} copy-done((f32[64,8192]{1,0:T(8,128)S(1)}, f32[64,8192]{1,0:T(8,128)}, u32[]{:S(2)}) %copy-start) | copy-done | bytes 2097176
  8.9 0.8 copy-done.2
  9.8 0.8 copy-done.3
  10.5 0.9 pack_x.1
  11.4 1.6 %collective-permute-start = (bf16[64,1408]{1,0:T(8,128)(2,1)S(1)}, bf16[64,1408]{1,0:T(8,128)(2,1)S(1)}, u32[]{:S(2)}, u32[]{:S(2)}) collective-permute-start(bf16[64,1408]{1,0:T(8,128)(2,1)S(1)} %get-tuple-element.121), channel_id=1, source_target_pairs={{0,1},{1,2},{2,3},{3,0},{4,5},{5,6},{6,7},{7,4},{8,9},{9,10},{10,1... | collective-permute-start | bytes 540680 | tf_op jit(solution)/shard_map/ppermute | solution.py:34
  13.0 2.6 %collective-permute-start.1 = (bf16[64,1408]{1,0:T(8,128)(2,1)S(1)}, bf16[64,1408]{1,0:T(8,128)(2,1)S(1)}, u32[]{:S(2)}, u32[]{:S(2)}) collective-permute-start(bf16[64,1408]{1,0:T(8,128)(2,1)S(1)} %get-tuple-element.122), channel_id=1, source_target_pairs={{0,2},{1,3},{2,0},{3,1},{4,6},{5,7},{6,4},{7,5},{8,10},{9,11},{10,... | collective-permute-start | bytes 540680 | tf_op jit(solution)/shard_map/ppermute | solution.py:34
  15.8 1.4 collective-permute-start.2
  17.2 2.5 %broadcast_select_fusion = (bf16[512,2048]{1,0:T(8,128)(2,1)S(1)}, bf16[512,2048]{1,0:T(8,128)(2,1)S(1)}) fusion(bf16[512,2048]{1,0:T(8,128)(2,1)} %collective-permute-done.5, bf16[512,2048]{1,0:T(8,128)(2,1)} %param.15, pred[]{:T(512)S(6)} %eq.4), kind=kLoop, calls=%fused_computation.1 | loop fusion | flops 2097152 | bytes 8388609 | tf_op jit(solution)/shard_map/jit(_where)/select_n | solution.py:657
  19.7 2.4 %collective-permute-start.8 = (bf16[16,2048]{1,0:T(8,128)(2,1)S(1)}, bf16[16,2048]{1,0:T(8,128)(2,1)S(1)}, u32[]{:S(2)}, u32[]{:S(2)}) collective-permute-start(bf16[16,2048]{1,0:T(8,128)(2,1)S(1)} %slice.23), channel_id=1, source_target_pairs={{0,8},{4,12},{8,16},{12,20},{16,24},{20,28},{1,9},{5,13},{9,17},{1... | collective-permute-start | bytes 196616 | tf_op jit(solution)/shard_map/ppermute | solution.py:669
  22.3 1.9 %collective-permute-start.6 = (bf16[512,256]{1,0:T(8,128)(2,1)S(1)}, bf16[512,256]{1,0:T(8,128)(2,1)S(1)}, u32[]{:S(2)}, u32[]{:S(2)}) collective-permute-start(bf16[512,256]{1,0:T(8,128)(2,1)S(1)} %slice.21), channel_id=1, source_target_pairs={{0,8},{4,12},{8,0},{12,4},{16,24},{20,28},{24,16},{28,20},{1,9},{5... | collective-permute-start | bytes 786440 | tf_op jit(solution)/shard_map/ppermute | solution.py:29
  24.4 4.0 %collective-permute-start.7 = (bf16[512,256]{1,0:T(8,128)(2,1)S(1)}, bf16[512,256]{1,0:T(8,128)(2,1)S(1)}, u32[]{:S(2)}, u32[]{:S(2)}) collective-permute-start(bf16[512,256]{1,0:T(8,128)(2,1)S(1)} %slice.22), channel_id=1, source_target_pairs={{0,16},{4,20},{8,24},{12,28},{16,0},{20,4},{24,8},{28,12},{1,17},{... | collective-permute-start | bytes 786440 | tf_op jit(solution)/shard_map/ppermute | solution.py:29
  28.8 2.1 %collective-permute-done.6.refs_3_ = bf16[512,256]{1,0:T(8,128)(2,1)S(1)} collective-permute-done((bf16[512,256]{1,0:T(8,128)(2,1)S(1)}, bf16[512,256]{1,0:T(8,128)(2,1)S(1)}, u32[]{:S(2)}, u32[]{:S(2)}) %collective-permute-start.6) | collective-permute-done | bytes 262176 | tf_op jit(solution)/shard_map/ppermute | solution.py:29
  30.9 1.8 %collective-permute-done.7.refs_4_ = bf16[512,256]{1,0:T(8,128)(2,1)S(1)} collective-permute-done((bf16[512,256]{1,0:T(8,128)(2,1)S(1)}, bf16[512,256]{1,0:T(8,128)(2,1)S(1)}, u32[]{:S(2)}, u32[]{:S(2)}) %collective-permute-start.7) | collective-permute-done | bytes 262176 | tf_op jit(solution)/shard_map/ppermute | solution.py:29
  33.4 2.1 %collective-permute-start.10 = (bf16[256,1408]{1,0:T(8,128)(2,1)S(1)}, bf16[256,1408]{1,0:T(8,128)(2,1)S(1)}, u32[]{:S(2)}, u32[]{:S(2)}) collective-permute-start(bf16[256,1408]{1,0:T(8,128)(2,1)S(1)} %assemble_x.1.refs_0_), channel_id=1, source_target_pairs={{0,16},{4,20},{8,24},{12,28},{16,0},{20,4},{24,8},{28,12},{1,17},{... | collective-permute-start | bytes 2162696 | tf_op jit(solution)/shard_map/ppermute | solution.py:29
  36.1 1.9 %collective-permute-start.11 = (bf16[64,1024]{1,0:T(8,128)(2,1)S(1)}, bf16[64,1024]{1,0:T(8,128)(2,1)S(1)}, u32[]{:S(2)}, u32[]{:S(2)}) collective-permute-start(bf16[64,1024]{1,0:T(8,128)(2,1)S(1)} %get-tuple-element.139), channel_id=1, source_target_pairs={{0,1},{1,2},{2,3},{3,0},{4,5},{5,6},{6,7},{7,4},{8,9},{9,10},{10,1... | collective-permute-start | bytes 393224 | tf_op jit(solution)/shard_map/ppermute | solution.py:34
  38.1 2.5 %collective-permute-start.12 = (bf16[64,1024]{1,0:T(8,128)(2,1)S(1)}, bf16[64,1024]{1,0:T(8,128)(2,1)S(1)}, u32[]{:S(2)}, u32[]{:S(2)}) collective-permute-start(bf16[64,1024]{1,0:T(8,128)(2,1)S(1)} %get-tuple-element.140), channel_id=1, source_target_pairs={{0,2},{1,3},{2,0},{3,1},{4,6},{5,7},{6,4},{7,5},{8,10},{9,11},{10,... | collective-permute-start | bytes 393224 | tf_op jit(solution)/shard_map/ppermute | solution.py:34
  40.6 1.4 collective-permute-start.13
  42.0 1.1 collective-permute-done.11.refs_1_
  43.1 3.7 %collective-permute-done.12.refs_2_ = bf16[64,1024]{1,0:T(8,128)(2,1)S(1)} collective-permute-done((bf16[64,1024]{1,0:T(8,128)(2,1)S(1)}, bf16[64,1024]{1,0:T(8,128)(2,1)S(1)}, u32[]{:S(2)}, u32[]{:S(2)}) %collective-permute-start.12) | collective-permute-done | bytes 131104 | tf_op jit(solution)/shard_map/ppermute | solution.py:34
  46.7 2.0 %collective-permute-done.10.refs_2_ = bf16[256,1408]{1,0:T(8,128)(2,1)S(1)} collective-permute-done((bf16[256,1408]{1,0:T(8,128)(2,1)S(1)}, bf16[256,1408]{1,0:T(8,128)(2,1)S(1)}, u32[]{:S(2)}, u32[]{:S(2)}) %collective-permute-start.10) | collective-permute-done | bytes 720928 | tf_op jit(solution)/shard_map/ppermute | solution.py:29
  48.7 1.2 collective-permute-done.9.refs_1_
  51.5 1.0 collective-permute-start.15
  52.5 1.0 collective-permute-done.18.theirs
  54.7 7.3 %collective-permute-done.14.refs_3_ = bf16[128,1408]{1,0:T(8,128)(2,1)S(1)} collective-permute-done((bf16[128,1408]{1,0:T(8,128)(2,1)S(1)}, bf16[128,1408]{1,0:T(8,128)(2,1)S(1)}, u32[]{:S(2)}, u32[]{:S(2)}) %collective-permute-start.14) | collective-permute-done | bytes 360480 | tf_op jit(solution)/shard_map/ppermute | solution.py:29
  63.7 1.7 %collective-permute-start.24 = (bf16[512,512]{1,0:T(8,128)(2,1)S(1)}, bf16[512,512]{1,0:T(8,128)(2,1)S(1)}, u32[]{:S(2)}, u32[]{:S(2)}) collective-permute-start(bf16[512,512]{1,0:T(8,128)(2,1)S(1)} %merge_z.1.refs_0_), channel_id=1, source_target_pairs={{0,8},{4,12},{8,0},{12,4},{16,24},{20,28},{24,16},{28,20},{1,9},{5... | collective-permute-start | bytes 1572872 | tf_op jit(solution)/shard_map/ppermute | solution.py:29
  66.0 6.5 %front_0.1 = (bf16[512,512]{1,0:T(8,128)(2,1)S(1)}, bf16[512,256]{1,0:T(8,128)(2,1)S(1)}, f32[512,128]{1,0:T(8,128)S(1)}, f32[512,128]{1,0:T(8,128)S(1)}, bf16[2...) custom-call(s32[27]{0:T(128)S(1)} %concatenate.18.ints.ints_ref, f32[48]{0:T(128)S(1)} %pad_maximum_fusion.1.floats, ...), custom_call_target="tpu_custom_call" | custom-call | bytes 1000000 | tf_op jit(solution)/shard_map/front_0/pallas_call | solution.py:714
  72.5 0.8 collective-permute-start.22
  73.3 1.2 collective-permute-start.23
  74.5 5.7 %front_1.1 = (bf16[512,512]{1,0:T(8,128)(2,1)S(1)}, bf16[512,256]{1,0:T(8,128)(2,1)S(1)}, f32[512,128]{1,0:T(8,128)S(1)}, f32[512,128]{1,0:T(8,128)S(1)}, bf16[2,544,128]{2,1,0:T(8,128)(2,1)S(1)}) custom-call(s32[27]{0:T(128)S(1)} %concatenate.18.ints.ints_ref, f32[48]{0:T(128)S(1)} %pad_maximum_fusion.1.floats, f32[16,1024]{1,0:T(8,128)S(1)} %concatenate.21.vecs, ...), custom_call_target="tpu_custom_call" | custom-call | bytes 1000000 | tf_op jit(solution)/shard_map/front_1/pallas_call | solution.py:714
  80.3 3.4 %collective-permute-done.22.refs_2_ = bf16[2,544,128]{2,1,0:T(8,128)(2,1)S(1)} collective-permute-done((bf16[2,544,128]{2,1,0:T(8,128)(2,1)S(1)}, bf16[2,544,128]{2,1,0:T(8,128)(2,1)S(1)}, u32[]{:S(2)}, u32[]{:S(2)}) %collective-permute-start.22) | collective-permute-done | bytes 278560 | tf_op jit(solution)/shard_map/ppermute | solution.py:29
  83.7 1.4 collective-permute-done.23.refs_4_
  85.1 0.8 collective-permute-start.31
  86.5 1.3 collective-permute-start.35
  87.8 1.5 collective-permute-start.36
  89.3 2.4 %mid_0.1 = (f32[512,512]{1,0:T(8,128)S(1)}, f32[512,512]{1,0:T(8,128)S(1)}) custom-call(s32[27]{0:T(128)S(1)} %concatenate.18.ints.ints_ref, f32[48]{0:T(128)S(1)} %pad_maximum_fusion.1.floats, bf16[512,512]{1,0:T(8,128)(2,1)S(1)} %get-tuple-element.172.xs_ref, bf16[512,256]{1,0:T(8,128)(2,1)S(1)} %get-tuple-element.209.bc_ref.refs_11_.refs_3_, ...), custom_call_target="tpu_custom_call" | custom-call | flops 134217728 | bytes 1000000 | tf_op jit(solution)/shard_map/mid_0/pallas_call | solution.py:747
  91.7 0.9 collective-permute-start.33
  92.6 2.1 %collective-permute-done.31.refs_3_ = bf16[2,544,128]{2,1,0:T(8,128)(2,1)S(1)} collective-permute-done((bf16[2,544,128]{2,1,0:T(8,128)(2,1)S(1)}, bf16[2,544,128]{2,1,0:T(8,128)(2,1)S(1)}, u32[]{:S(2)}, u32[]{:S(2)}) %collective-permute-start.31) | collective-permute-done | bytes 278560 | tf_op jit(solution)/shard_map/ppermute | solution.py:29
  94.7 0.8 collective-permute-done.32.refs_5_
  96.0 2.4 %mid_1.1 = (f32[512,512]{1,0:T(8,128)S(1)}, f32[512,512]{1,0:T(8,128)S(1)}) custom-call(s32[27]{0:T(128)S(1)} %concatenate.18.ints.ints_ref, f32[48]{0:T(128)S(1)} %pad_maximum_fusion.1.floats, bf16[512,512]{1,0:T(8,128)(2,1)S(1)} %get-tuple-element.191.xs_ref, bf16[512,256]{1,0:T(8,128)(2,1)S(1)} %get-tuple-element.213.bc_ref.refs_15_.refs_7_, ...), custom_call_target="tpu_custom_call" | custom-call | flops 134217728 | bytes 1000000 | tf_op jit(solution)/shard_map/mid_1/pallas_call | solution.py:747
  98.5 2.9 %gate_0.1 = (f32[512,512]{1,0:T(8,128)S(1)}, f32[512,512]{1,0:T(8,128)S(1)}) custom-call(s32[27]{0:T(128)S(1)} %concatenate.18.ints.ints_ref, bf16[1040,2048]{1,0:T(8,128)(2,1)S(1)} %pad_maximum_fusion.tok_ref, bf16[512,512]{1,0:T(8,128)(2,1)S(1)} %merge_z.1.refs_0_, bf16[512,512]{1,0:T(8,128)(2,1)S(1)} %collective-permute-done.24.refs_1_, ...), custom_call_target="tpu_custom_call" | custom-call | flops 268435456 | bytes 1000000 | tf_op jit(solution)/shard_map/gate_0/pallas_call | solution.py:772
  101.4 2.2 %gate_1.1 = (f32[512,512]{1,0:T(8,128)S(1)}, f32[512,512]{1,0:T(8,128)S(1)}) custom-call(s32[27]{0:T(128)S(1)} %concatenate.18.ints.ints_ref, bf16[1040,2048]{1,0:T(8,128)(2,1)S(1)} %pad_maximum_fusion.tok_ref, bf16[256,512]{1,0:T(8,128)(2,1)S(1)} %collective-permute-done.35.refs_0_, bf16[256,512]{1,0:T(8,128)(2,1)S(1)} %collective-permute-done.36.refs_1_, ...), custom_call_target="tpu_custom_call" | custom-call | flops 268435456 | bytes 1000000 | tf_op jit(solution)/shard_map/gate_1/pallas_call | solution.py:772
  103.6 0.6 collective-permute-done.33.refs_6_
  104.2 0.8 collective-permute-done.34.refs_7_
  105.0 2.2 %back.1 = (bf16[512,640]{1,0:T(8,128)(2,1)S(1)}, bf16[4,512,128]{2,1,0:T(8,128)(2,1)S(1)}, bf16[2,512,128]{2,1,0:T(8,128)(2,1)S(1)}, f32[2,512,128]{2,1,0:T(8,128)S(1)}) custom-call(s32[27]{0:T(128)S(1)} %concatenate.18.ints.ints_ref, f32[16,1024]{1,0:T(8,128)S(1)} %concatenate.21.vecs, bf16[2,544,128]{2,1,0:T(8,128)(2,1)S(1)} %get-tuple-element.198.refs_0_, ...), custom_call_target="tpu_custom_call" | custom-call | flops 134217728 | bytes 8000000 | tf_op jit(solution)/shard_map/back/pallas_call | solution.py:785
  107.3 1.1 back_own.1.mine
  108.4 1.0 collective-permute-done.37.theirs
  109.4 2.0 %out_1.1 = (bf16[128,1024]{1,0:T(8,128)(2,1)S(1)}, bf16[128,1152]{1,0:T(8,128)(2,1)S(1)}, bf16[1024,2048]{1,0:T(8,128)(2,1)S(1)}) custom-call(s32[27]{0:T(128)S(1)} %concatenate.18.ints.ints_ref, bf16[512,640]{1,0:T(8,128)(2,1)S(1)} %back_own.1.mine, bf16[512,640]{1,0:T(8,128)(2,1)S(1)} %collective-permute-done.37.theirs, ...), custom_call_target="tpu_custom_call" | custom-call | flops 268435456 | bytes 1000000 | tf_op jit(solution)/shard_map/out_1/pallas_call | solution.py:829
  111.4 1.3 collective-permute-start.39
  112.7 0.7 collective-permute-start.38
  113.5 2.5 %out_3.1 = (bf16[128,1024]{1,0:T(8,128)(2,1)S(1)}, bf16[128,1152]{1,0:T(8,128)(2,1)S(1)}, bf16[128,2176]{1,0:T(8,128)(2,1)S(1)}, f32[128,1024]{1,0:T(8,128)S(1)}, f32[128,1152]{1,0:T(8,128)S(1)}) custom-call(s32[27]{0:T(128)S(1)} %concatenate.18.ints.ints_ref, bf16[512,640]{1,0:T(8,128)(2,1)S(1)} %back_own.1.mine, ...), custom_call_target="tpu_custom_call" | custom-call | flops 671088640 | bytes 1000000 | tf_op jit(solution)/shard_map/out_3/pallas_call | solution.py:829
  116.0 0.7 collective-permute-start.42
  116.7 6.0 %collective-permute-start.43 = (bf16[128,2176]{1,0:T(8,128)(2,1)S(1)}, bf16[128,2176]{1,0:T(8,128)(2,1)S(1)}, u32[]{:S(2)}, u32[]{:S(2)}) collective-permute-start(bf16[128,2176]{1,0:T(8,128)(2,1)S(1)} %get-tuple-element.235), channel_id=1, source_target_pairs={{0,1},{3,2},{4,5},{7,6},{8,9},{11,10},{12,13},{15,14},{16,17},{19,... | collective-permute-start | bytes 1671176 | tf_op jit(solution)/shard_map/ppermute | solution.py:547
  122.7 3.4 %collective-permute-done.38.got.refs_2_ = bf16[128,1024]{1,0:T(8,128)(2,1)S(1)} collective-permute-done((bf16[128,1024]{1,0:T(8,128)(2,1)S(1)}, bf16[128,1024]{1,0:T(8,128)(2,1)S(1)}, u32[]{:S(2)}, u32[]{:S(2)}) %collective-permute-start.38) | collective-permute-done | bytes 262176 | tf_op jit(solution)/shard_map/ppermute | solution.py:547
  126.1 0.7 add_far.3
  126.9 3.2 %collective-permute-start.41 = (bf16[128,1152]{1,0:T(8,128)(2,1)S(1)}, bf16[128,1152]{1,0:T(8,128)(2,1)S(1)}, u32[]{:S(2)}, u32[]{:S(2)}) collective-permute-start(bf16[128,1152]{1,0:T(8,128)(2,1)S(1)} %add_far.3), channel_id=1, source_target_pairs={{0,2},{1,3},{2,0},{3,1},{4,6},{5,7},{6,4},{7,5},{8,10},{9,11},{10,... | collective-permute-start | bytes 884744 | tf_op jit(solution)/shard_map/ppermute | solution.py:34
  130.0 0.6 add_far.2
  130.8 1.1 maximum_select_fusion
  131.9 5.8 %collective-permute-done.43.refs_7_ = bf16[128,2176]{1,0:T(8,128)(2,1)S(1)} collective-permute-done((bf16[128,2176]{1,0:T(8,128)(2,1)S(1)}, bf16[128,2176]{1,0:T(8,128)(2,1)S(1)}, u32[]{:S(2)}, u32[]{:S(2)}) %collective-permute-start.43) | collective-permute-done | bytes 557088 | tf_op jit(solution)/shard_map/ppermute | solution.py:547
  137.7 18.9 %collective-permute-done.40.refs_4_ = bf16[128,1024]{1,0:T(8,128)(2,1)S(1)} collective-permute-done((bf16[128,1024]{1,0:T(8,128)(2,1)S(1)}, bf16[128,1024]{1,0:T(8,128)(2,1)S(1)}, u32[]{:S(2)}, u32[]{:S(2)}) %collective-permute-start.40) | collective-permute-done | bytes 262176 | tf_op jit(solution)/shard_map/ppermute | solution.py:34
  156.6 1.9 %final.1 = bf16[128,2048]{1,0:T(8,128)(2,1)} custom-call(s32[27]{0:T(128)S(1)} %concatenate.18.ints.ints_ref, f32[128,1024]{1,0:T(8,128)S(1)} %get-tuple-element.229.refs_0_, f32[128,1152]{1,0:T(8,128)S(1)} %get-tuple-element.230.refs_1_, bf16[128,1024]{1,0:T(8,128)(2,1)S(1)} %collective-permute-done.38.got.refs_2_, ...), custom_call_target="tpu_custom_call" | custom-call | tf_op jit(solution)/shard_map/final/pallas_call | solution.py:849
  (86 shorter events, 9.1 us)
Async XLA Ops:
  0.6 15.0 %copy-start.7 = (f32[4,256]{1,0:T(4,128)S(1)}, f32[4,256]{1,0:T(4,128)}, u32[]{:S(2)}) copy-start(f32[4,256]{1,0:T(4,128)} %param.21) | copy-start | bytes 12292
  0.6 15.0 %copy-start.8 = (f32[256]{0:T(256)S(1)}, f32[256]{0:T(256)}, u32[]{:S(2)}) copy-start(f32[256]{0:T(256)} %param.22) | copy-start | bytes 3076
  0.7 15.0 %copy-start.5 = (f32[1024]{0:T(1024)S(1)}, f32[1024]{0:T(1024)}, u32[]{:S(2)}) copy-start(f32[1024]{0:T(1024)} %param.20) | copy-start | bytes 12292
  0.7 15.0 %copy-start.6 = (f32[1024]{0:T(1024)S(1)}, f32[1024]{0:T(1024)}, u32[]{:S(2)}) copy-start(f32[1024]{0:T(1024)} %param.26) | copy-start | bytes 12292
  0.7 15.0 %copy-start.4 = (f32[4,1024]{1,0:T(4,128)S(1)}, f32[4,1024]{1,0:T(4,128)}, u32[]{:S(2)}) copy-start(f32[4,1024]{1,0:T(4,128)} %param.19) | copy-start | bytes 49156
  0.7 15.0 %collective-permute-start.5 = (bf16[512,2048]{1,0:T(8,128)(2,1)}, bf16[512,2048]{1,0:T(8,128)(2,1)}, u32[]{:S(2)}, u32[]{:S(2)}) collective-permute-start(bf16[512,2048]{1,0:T(8,128)(2,1)} %param.15), channel_id=1, source_target_pairs={{0,4},{4,0},{8,12},{12,8},{16,20},{20,16},{24,28},{28,24},{1,5},{5... | collective-permute-start | bytes 6291464 | tf_op jit(solution)/shard_map/ppermute | solution.py:29
  2.5 17.2 %collective-permute-start.3 = (bf16[1024,256]{1,0:T(8,128)(2,1)S(1)}, bf16[1024,256]{1,0:T(8,128)(2,1)S(1)}, u32[]{:S(2)}, u32[]{:S(2)}) collective-permute-start(bf16[1024,256]{1,0:T(8,128)(2,1)S(1)} %convert_element_type.10.refs_0_), channel_id=1, source_target_pairs={{0,8},{4,12},{8,0},{12,4},{16,24},{20,28},{24,16},{28,20},{1,9},{5... | collective-permute-start | bytes 1572872 | tf_op jit(solution)/shard_map/ppermute | solution.py:29
  5.0 14.6 %collective-permute-start.4 = (bf16[1024,256]{1,0:T(8,128)(2,1)S(1)}, bf16[1024,256]{1,0:T(8,128)(2,1)S(1)}, u32[]{:S(2)}, u32[]{:S(2)}) collective-permute-start(bf16[1024,256]{1,0:T(8,128)(2,1)S(1)} %convert_element_type.10.refs_0_), channel_id=1, source_target_pairs={{0,16},{4,20},{8,24},{12,28},{16,0},{20,4},{24,8},{28,12},{1,17},{... | collective-permute-start | bytes 1572872 | tf_op jit(solution)/shard_map/ppermute | solution.py:29
  7.3 1.6 %copy-start = (f32[64,8192]{1,0:T(8,128)S(1)}, f32[64,8192]{1,0:T(8,128)}, u32[]{:S(2)}) copy-start(f32[64,8192]{1,0:T(8,128)} %w_ref.3) | copy-start | bytes 6291460
  8.9 0.8 copy-start.2
  9.8 0.8 copy-start.3
  11.4 17.4 %collective-permute-start = (bf16[64,1408]{1,0:T(8,128)(2,1)S(1)}, bf16[64,1408]{1,0:T(8,128)(2,1)S(1)}, u32[]{:S(2)}, u32[]{:S(2)}) collective-permute-start(bf16[64,1408]{1,0:T(8,128)(2,1)S(1)} %get-tuple-element.121), channel_id=1, source_target_pairs={{0,1},{1,2},{2,3},{3,0},{4,5},{5,6},{6,7},{7,4},{8,9},{9,10},{10,1... | collective-permute-start | bytes 540680 | tf_op jit(solution)/shard_map/ppermute | solution.py:34
  13.0 15.8 %collective-permute-start.1 = (bf16[64,1408]{1,0:T(8,128)(2,1)S(1)}, bf16[64,1408]{1,0:T(8,128)(2,1)S(1)}, u32[]{:S(2)}, u32[]{:S(2)}) collective-permute-start(bf16[64,1408]{1,0:T(8,128)(2,1)S(1)} %get-tuple-element.122), channel_id=1, source_target_pairs={{0,2},{1,3},{2,0},{3,1},{4,6},{5,7},{6,4},{7,5},{8,10},{9,11},{10,... | collective-permute-start | bytes 540680 | tf_op jit(solution)/shard_map/ppermute | solution.py:34
  15.7 6.4 %copy-start.9 = (f32[16]{0:T(128)S(1)}, f32[16]{0:T(128)}, u32[]{:S(2)}) copy-start(f32[16]{0:T(128)} %param.25) | copy-start | bytes 196
  15.7 6.4 %copy-start.10 = (f32[16]{0:T(128)S(1)}, f32[16]{0:T(128)}, u32[]{:S(2)}) copy-start(f32[16]{0:T(128)} %param.24) | copy-start | bytes 196
  15.8 6.4 %copy-start.11 = (f32[16]{0:T(128)S(1)}, f32[16]{0:T(128)}, u32[]{:S(2)}) copy-start(f32[16]{0:T(128)} %param.23) | copy-start | bytes 196
  15.8 13.1 %collective-permute-start.2 = (bf16[64,1408]{1,0:T(8,128)(2,1)S(1)}, bf16[64,1408]{1,0:T(8,128)(2,1)S(1)}, u32[]{:S(2)}, u32[]{:S(2)}) collective-permute-start(bf16[64,1408]{1,0:T(8,128)(2,1)S(1)} %get-tuple-element.123), channel_id=1, source_target_pairs={{0,3},{1,0},{2,1},{3,2},{4,7},{5,4},{6,5},{7,6},{8,11},{9,8},{10,9... | collective-permute-start | bytes 540680 | tf_op jit(solution)/shard_map/ppermute | solution.py:34
  19.7 4.7 %collective-permute-start.8 = (bf16[16,2048]{1,0:T(8,128)(2,1)S(1)}, bf16[16,2048]{1,0:T(8,128)(2,1)S(1)}, u32[]{:S(2)}, u32[]{:S(2)}) collective-permute-start(bf16[16,2048]{1,0:T(8,128)(2,1)S(1)} %slice.23), channel_id=1, source_target_pairs={{0,8},{4,12},{8,16},{12,20},{16,24},{20,28},{1,9},{5,13},{9,17},{1... | collective-permute-start | bytes 196616 | tf_op jit(solution)/shard_map/ppermute | solution.py:669
  22.3 8.7 %collective-permute-start.6 = (bf16[512,256]{1,0:T(8,128)(2,1)S(1)}, bf16[512,256]{1,0:T(8,128)(2,1)S(1)}, u32[]{:S(2)}, u32[]{:S(2)}) collective-permute-start(bf16[512,256]{1,0:T(8,128)(2,1)S(1)} %slice.21), channel_id=1, source_target_pairs={{0,8},{4,12},{8,0},{12,4},{16,24},{20,28},{24,16},{28,20},{1,9},{5... | collective-permute-start | bytes 786440 | tf_op jit(solution)/shard_map/ppermute | solution.py:29
  24.2 11.3 %copy-start.1 = (f32[64,8192]{1,0:T(8,128)S(1)}, f32[64,8192]{1,0:T(8,128)}, u32[]{:S(2)}) copy-start(f32[64,8192]{1,0:T(8,128)} %w_ref.3) | copy-start | bytes 6291460
  24.4 8.4 %collective-permute-start.7 = (bf16[512,256]{1,0:T(8,128)(2,1)S(1)}, bf16[512,256]{1,0:T(8,128)(2,1)S(1)}, u32[]{:S(2)}, u32[]{:S(2)}) collective-permute-start(bf16[512,256]{1,0:T(8,128)(2,1)S(1)} %slice.22), channel_id=1, source_target_pairs={{0,16},{4,20},{8,24},{12,28},{16,0},{20,4},{24,8},{28,12},{1,17},{... | collective-permute-start | bytes 786440 | tf_op jit(solution)/shard_map/ppermute | solution.py:29
  33.4 15.3 %collective-permute-start.10 = (bf16[256,1408]{1,0:T(8,128)(2,1)S(1)}, bf16[256,1408]{1,0:T(8,128)(2,1)S(1)}, u32[]{:S(2)}, u32[]{:S(2)}) collective-permute-start(bf16[256,1408]{1,0:T(8,128)(2,1)S(1)} %assemble_x.1.refs_0_), channel_id=1, source_target_pairs={{0,16},{4,20},{8,24},{12,28},{16,0},{20,4},{24,8},{28,12},{1,17},{... | collective-permute-start | bytes 2162696 | tf_op jit(solution)/shard_map/ppermute | solution.py:29
  35.5 14.3 %collective-permute-start.9 = (bf16[256,1408]{1,0:T(8,128)(2,1)S(1)}, bf16[256,1408]{1,0:T(8,128)(2,1)S(1)}, u32[]{:S(2)}, u32[]{:S(2)}) collective-permute-start(bf16[256,1408]{1,0:T(8,128)(2,1)S(1)} %assemble_x.1.refs_0_), channel_id=1, source_target_pairs={{0,8},{4,12},{8,0},{12,4},{16,24},{20,28},{24,16},{28,20},{1,9},{5... | collective-permute-start | bytes 2162696 | tf_op jit(solution)/shard_map/ppermute | solution.py:29
  36.1 6.9 %collective-permute-start.11 = (bf16[64,1024]{1,0:T(8,128)(2,1)S(1)}, bf16[64,1024]{1,0:T(8,128)(2,1)S(1)}, u32[]{:S(2)}, u32[]{:S(2)}) collective-permute-start(bf16[64,1024]{1,0:T(8,128)(2,1)S(1)} %get-tuple-element.139), channel_id=1, source_target_pairs={{0,1},{1,2},{2,3},{3,0},{4,5},{5,6},{6,7},{7,4},{8,9},{9,10},{10,1... | collective-permute-start | bytes 393224 | tf_op jit(solution)/shard_map/ppermute | solution.py:34
  38.1 8.7 %collective-permute-start.12 = (bf16[64,1024]{1,0:T(8,128)(2,1)S(1)}, bf16[64,1024]{1,0:T(8,128)(2,1)S(1)}, u32[]{:S(2)}, u32[]{:S(2)}) collective-permute-start(bf16[64,1024]{1,0:T(8,128)(2,1)S(1)} %get-tuple-element.140), channel_id=1, source_target_pairs={{0,2},{1,3},{2,0},{3,1},{4,6},{5,7},{6,4},{7,5},{8,10},{9,11},{10,... | collective-permute-start | bytes 393224 | tf_op jit(solution)/shard_map/ppermute | solution.py:34
  40.6 6.2 %collective-permute-start.13 = (bf16[64,1024]{1,0:T(8,128)(2,1)S(1)}, bf16[64,1024]{1,0:T(8,128)(2,1)S(1)}, u32[]{:S(2)}, u32[]{:S(2)}) collective-permute-start(bf16[64,1024]{1,0:T(8,128)(2,1)S(1)} %get-tuple-element.141), channel_id=1, source_target_pairs={{0,3},{1,0},{2,1},{3,2},{4,7},{5,4},{6,5},{7,6},{8,11},{9,8},{10,9... | collective-permute-start | bytes 393224 | tf_op jit(solution)/shard_map/ppermute | solution.py:34
  49.9 3.7 %collective-permute-start.16 = (bf16[256,1408]{1,0:T(8,128)(2,1)S(1)}, bf16[256,1408]{1,0:T(8,128)(2,1)S(1)}, u32[]{:S(2)}, u32[]{:S(2)}) collective-permute-start(bf16[256,1408]{1,0:T(8,128)(2,1)S(1)} %collective-permute-done.9.refs_1_), channel_id=1, source_target_pairs={{0,4},{4,0},{8,12},{12,8},{16,20},{20,16},{24,28},{28,24},{1,5},{5... | collective-permute-start | bytes 2162696 | tf_op jit(solution)/shard_map/ppermute | solution.py:29
  49.9 4.1 %collective-permute-start.17 = (bf16[256,1408]{1,0:T(8,128)(2,1)S(1)}, bf16[256,1408]{1,0:T(8,128)(2,1)S(1)}, u32[]{:S(2)}, u32[]{:S(2)}) collective-permute-start(bf16[256,1408]{1,0:T(8,128)(2,1)S(1)} %collective-permute-done.10.refs_2_), channel_id=1, source_target_pairs={{0,4},{4,0},{8,12},{12,8},{16,20},{20,16},{24,28},{28,24},{1,5},{5... | collective-permute-start | bytes 2162696 | tf_op jit(solution)/shard_map/ppermute | solution.py:29
  51.0 2.5 %collective-permute-start.18 = (bf16[256,512]{1,0:T(8,128)(2,1)S(1)}, bf16[256,512]{1,0:T(8,128)(2,1)S(1)}, u32[]{:S(2)}, u32[]{:S(2)}) collective-permute-start(bf16[256,512]{1,0:T(8,128)(2,1)S(1)} %get-tuple-element.149), channel_id=1, source_target_pairs={{0,4},{4,0},{8,12},{12,8},{16,20},{20,16},{24,28},{28,24},{1,5},{5... | collective-permute-start | bytes 786440 | tf_op jit(solution)/shard_map/ppermute | solution.py:29
  51.1 10.9 %collective-permute-start.14 = (bf16[128,1408]{1,0:T(8,128)(2,1)S(1)}, bf16[128,1408]{1,0:T(8,128)(2,1)S(1)}, u32[]{:S(2)}, u32[]{:S(2)}) collective-permute-start(bf16[128,1408]{1,0:T(8,128)(2,1)S(1)} %slice.24), channel_id=1, source_target_pairs={{0,8},{4,12},{8,0},{12,4},{16,24},{20,28},{24,16},{28,20},{1,9},{5... | collective-permute-start | bytes 1081352 | tf_op jit(solution)/shard_map/ppermute | solution.py:29
  51.5 10.6 %collective-permute-start.15 = (bf16[128,1408]{1,0:T(8,128)(2,1)S(1)}, bf16[128,1408]{1,0:T(8,128)(2,1)S(1)}, u32[]{:S(2)}, u32[]{:S(2)}) collective-permute-start(bf16[128,1408]{1,0:T(8,128)(2,1)S(1)} %slice.25), channel_id=1, source_target_pairs={{0,16},{4,20},{8,24},{12,28},{16,0},{20,4},{24,8},{28,12},{1,17},{... | collective-permute-start | bytes 1081352 | tf_op jit(solution)/shard_map/ppermute | solution.py:29
  53.5 9.6 %collective-permute-start.19 = (bf16[256,1408]{1,0:T(8,128)(2,1)S(1)}, bf16[256,1408]{1,0:T(8,128)(2,1)S(1)}, u32[]{:S(2)}, u32[]{:S(2)}) collective-permute-start(bf16[256,1408]{1,0:T(8,128)(2,1)S(1)} %assemble_x.1.refs_0_), channel_id=1, source_target_pairs={{0,4},{4,0},{8,12},{12,8},{16,20},{20,16},{24,28},{28,24},{1,5},{5... | collective-permute-start | bytes 2162696 | tf_op jit(solution)/shard_map/ppermute | solution.py:29
  53.6 9.0 %collective-permute-start.29 = (bf16[512,256]{1,0:T(8,128)(2,1)S(1)}, bf16[512,256]{1,0:T(8,128)(2,1)S(1)}, u32[]{:S(2)}, u32[]{:S(2)}) collective-permute-start(bf16[512,256]{1,0:T(8,128)(2,1)S(1)} %collective-permute-done.6.refs_3_), channel_id=1, source_target_pairs={{0,4},{4,0},{8,12},{12,8},{16,20},{20,16},{24,28},{28,24},{1,5},{5... | collective-permute-start | bytes 786440 | tf_op jit(solution)/shard_map/ppermute | solution.py:29
  54.0 8.6 %collective-permute-start.30 = (bf16[512,256]{1,0:T(8,128)(2,1)S(1)}, bf16[512,256]{1,0:T(8,128)(2,1)S(1)}, u32[]{:S(2)}, u32[]{:S(2)}) collective-permute-start(bf16[512,256]{1,0:T(8,128)(2,1)S(1)} %collective-permute-done.7.refs_4_), channel_id=1, source_target_pairs={{0,4},{4,0},{8,12},{12,8},{16,20},{20,16},{24,28},{28,24},{1,5},{5... | collective-permute-start | bytes 786440 | tf_op jit(solution)/shard_map/ppermute | solution.py:29
  62.1 1.7 %collective-permute-start.20 = (bf16[128,1408]{1,0:T(8,128)(2,1)S(1)}, bf16[128,1408]{1,0:T(8,128)(2,1)S(1)}, u32[]{:S(2)}, u32[]{:S(2)}) collective-permute-start(bf16[128,1408]{1,0:T(8,128)(2,1)S(1)} %collective-permute-done.14.refs_3_), channel_id=1, source_target_pairs={{0,4},{4,0},{8,12},{12,8},{16,20},{20,16},{24,28},{28,24},{1,5},{5... | collective-permute-start | bytes 1081352 | tf_op jit(solution)/shard_map/ppermute | solution.py:29
  62.1 3.3 %collective-permute-start.21 = (bf16[128,1408]{1,0:T(8,128)(2,1)S(1)}, bf16[128,1408]{1,0:T(8,128)(2,1)S(1)}, u32[]{:S(2)}, u32[]{:S(2)}) collective-permute-start(bf16[128,1408]{1,0:T(8,128)(2,1)S(1)} %collective-permute-done.15.refs_4_), channel_id=1, source_target_pairs={{0,4},{4,0},{8,12},{12,8},{16,20},{20,16},{24,28},{28,24},{1,5},{5... | collective-permute-start | bytes 1081352 | tf_op jit(solution)/shard_map/ppermute | solution.py:29
  62.6 9.9 %collective-permute-start.26 = (bf16[1024,256]{1,0:T(8,128)(2,1)S(1)}, bf16[1024,256]{1,0:T(8,128)(2,1)S(1)}, u32[]{:S(2)}, u32[]{:S(2)}) collective-permute-start(bf16[1024,256]{1,0:T(8,128)(2,1)S(1)} %convert_element_type.10.refs_0_), channel_id=1, source_target_pairs={{0,4},{4,0},{8,12},{12,8},{16,20},{20,16},{24,28},{28,24},{1,5},{5... | collective-permute-start | bytes 1572872 | tf_op jit(solution)/shard_map/ppermute | solution.py:29
  62.6 10.7 %collective-permute-start.27 = (bf16[1024,256]{1,0:T(8,128)(2,1)S(1)}, bf16[1024,256]{1,0:T(8,128)(2,1)S(1)}, u32[]{:S(2)}, u32[]{:S(2)}) collective-permute-start(bf16[1024,256]{1,0:T(8,128)(2,1)S(1)} %collective-permute-done.3.refs_1_), channel_id=1, source_target_pairs={{0,4},{4,0},{8,12},{12,8},{16,20},{20,16},{24,28},{28,24},{1,5},{5... | collective-permute-start | bytes 1572872 | tf_op jit(solution)/shard_map/ppermute | solution.py:29
  63.1 17.1 %collective-permute-start.28 = (bf16[1024,256]{1,0:T(8,128)(2,1)S(1)}, bf16[1024,256]{1,0:T(8,128)(2,1)S(1)}, u32[]{:S(2)}, u32[]{:S(2)}) collective-permute-start(bf16[1024,256]{1,0:T(8,128)(2,1)S(1)} %collective-permute-done.4.refs_2_), channel_id=1, source_target_pairs={{0,4},{4,0},{8,12},{12,8},{16,20},{20,16},{24,28},{28,24},{1,5},{5... | collective-permute-start | bytes 1572872 | tf_op jit(solution)/shard_map/ppermute | solution.py:29
  63.7 16.5 %collective-permute-start.24 = (bf16[512,512]{1,0:T(8,128)(2,1)S(1)}, bf16[512,512]{1,0:T(8,128)(2,1)S(1)}, u32[]{:S(2)}, u32[]{:S(2)}) collective-permute-start(bf16[512,512]{1,0:T(8,128)(2,1)S(1)} %merge_z.1.refs_0_), channel_id=1, source_target_pairs={{0,8},{4,12},{8,0},{12,4},{16,24},{20,28},{24,16},{28,20},{1,9},{5... | collective-permute-start | bytes 1572872 | tf_op jit(solution)/shard_map/ppermute | solution.py:29
  65.4 14.8 %collective-permute-start.25 = (bf16[512,512]{1,0:T(8,128)(2,1)S(1)}, bf16[512,512]{1,0:T(8,128)(2,1)S(1)}, u32[]{:S(2)}, u32[]{:S(2)}) collective-permute-start(bf16[512,512]{1,0:T(8,128)(2,1)S(1)} %merge_z.1.refs_0_), channel_id=1, source_target_pairs={{0,16},{4,20},{8,24},{12,28},{16,0},{20,4},{24,8},{28,12},{1,17},{... | collective-permute-start | bytes 1572872 | tf_op jit(solution)/shard_map/ppermute | solution.py:29
  72.5 11.2 %collective-permute-start.22 = (bf16[2,544,128]{2,1,0:T(8,128)(2,1)S(1)}, bf16[2,544,128]{2,1,0:T(8,128)(2,1)S(1)}, u32[]{:S(2)}, u32[]{:S(2)}) collective-permute-start(bf16[2,544,128]{2,1,0:T(8,128)(2,1)S(1)} %get-tuple-element.198.refs_0_), channel_id=1, source_target_pairs={{0,8},{4,12},{8,0},{12,4},{16,24},{20,28},{24,16},{28,20},{1,9},{5... | collective-permute-start | bytes 835592 | tf_op jit(solution)/shard_map/ppermute | solution.py:29
  73.3 11.8 %collective-permute-start.23 = (bf16[2,544,128]{2,1,0:T(8,128)(2,1)S(1)}, bf16[2,544,128]{2,1,0:T(8,128)(2,1)S(1)}, u32[]{:S(2)}, u32[]{:S(2)}) collective-permute-start(bf16[2,544,128]{2,1,0:T(8,128)(2,1)S(1)} %get-tuple-element.198.refs_0_), channel_id=1, source_target_pairs={{0,16},{4,20},{8,24},{12,28},{16,0},{20,4},{24,8},{28,12},{1,17},{... | collective-permute-start | bytes 835592 | tf_op jit(solution)/shard_map/ppermute | solution.py:29
  85.1 9.6 %collective-permute-start.31 = (bf16[2,544,128]{2,1,0:T(8,128)(2,1)S(1)}, bf16[2,544,128]{2,1,0:T(8,128)(2,1)S(1)}, u32[]{:S(2)}, u32[]{:S(2)}) collective-permute-start(bf16[2,544,128]{2,1,0:T(8,128)(2,1)S(1)} %get-tuple-element.199.refs_1_), channel_id=1, source_target_pairs={{0,8},{4,12},{8,0},{12,4},{16,24},{20,28},{24,16},{28,20},{1,9},{5... | collective-permute-start | bytes 835592 | tf_op jit(solution)/shard_map/ppermute | solution.py:29
  85.9 9.6 %collective-permute-start.32 = (bf16[2,544,128]{2,1,0:T(8,128)(2,1)S(1)}, bf16[2,544,128]{2,1,0:T(8,128)(2,1)S(1)}, u32[]{:S(2)}, u32[]{:S(2)}) collective-permute-start(bf16[2,544,128]{2,1,0:T(8,128)(2,1)S(1)} %get-tuple-element.199.refs_1_), channel_id=1, source_target_pairs={{0,16},{4,20},{8,24},{12,28},{16,0},{20,4},{24,8},{28,12},{1,17},{... | collective-permute-start | bytes 835592 | tf_op jit(solution)/shard_map/ppermute | solution.py:29
  86.5 14.9 %collective-permute-start.35 = (bf16[256,512]{1,0:T(8,128)(2,1)S(1)}, bf16[256,512]{1,0:T(8,128)(2,1)S(1)}, u32[]{:S(2)}, u32[]{:S(2)}) collective-permute-start(bf16[256,512]{1,0:T(8,128)(2,1)S(1)} %slice.26), channel_id=1, source_target_pairs={{0,8},{4,12},{8,0},{12,4},{16,24},{20,28},{24,16},{28,20},{1,9},{5... | collective-permute-start | bytes 786440 | tf_op jit(solution)/shard_map/ppermute | solution.py:29
  87.8 13.6 %collective-permute-start.36 = (bf16[256,512]{1,0:T(8,128)(2,1)S(1)}, bf16[256,512]{1,0:T(8,128)(2,1)S(1)}, u32[]{:S(2)}, u32[]{:S(2)}) collective-permute-start(bf16[256,512]{1,0:T(8,128)(2,1)S(1)} %slice.27), channel_id=1, source_target_pairs={{0,16},{4,20},{8,24},{12,28},{16,0},{20,4},{24,8},{28,12},{1,17},{... | collective-permute-start | bytes 786440 | tf_op jit(solution)/shard_map/ppermute | solution.py:29
  91.7 12.5 %collective-permute-start.33 = (bf16[2,544,128]{2,1,0:T(8,128)(2,1)S(1)}, bf16[2,544,128]{2,1,0:T(8,128)(2,1)S(1)}, u32[]{:S(2)}, u32[]{:S(2)}) collective-permute-start(bf16[2,544,128]{2,1,0:T(8,128)(2,1)S(1)} %collective-permute-done.23.refs_4_), channel_id=1, source_target_pairs={{0,8},{4,12},{8,0},{12,4},{16,24},{20,28},{24,16},{28,20},{1,9},{5... | collective-permute-start | bytes 835592 | tf_op jit(solution)/shard_map/ppermute | solution.py:29
  95.5 9.6 %collective-permute-start.34 = (bf16[2,544,128]{2,1,0:T(8,128)(2,1)S(1)}, bf16[2,544,128]{2,1,0:T(8,128)(2,1)S(1)}, u32[]{:S(2)}, u32[]{:S(2)}) collective-permute-start(bf16[2,544,128]{2,1,0:T(8,128)(2,1)S(1)} %collective-permute-done.31.refs_3_), channel_id=1, source_target_pairs={{0,16},{4,20},{8,24},{12,28},{16,0},{20,4},{24,8},{28,12},{1,17},{... | collective-permute-start | bytes 835592 | tf_op jit(solution)/shard_map/ppermute | solution.py:29
  107.2 2.2 %collective-permute-start.37 = (bf16[512,640]{1,0:T(8,128)(2,1)S(1)}, bf16[512,640]{1,0:T(8,128)(2,1)S(1)}, u32[]{:S(2)}, u32[]{:S(2)}) collective-permute-start(bf16[512,640]{1,0:T(8,128)(2,1)S(1)} %get-tuple-element.215), channel_id=1, source_target_pairs={{0,4},{4,0},{8,12},{12,8},{16,20},{20,16},{24,28},{28,24},{1,5},{5... | collective-permute-start | bytes 1966088 | tf_op jit(solution)/shard_map/ppermute | solution.py:29
  111.4 14.7 %collective-permute-start.39 = (bf16[128,1152]{1,0:T(8,128)(2,1)S(1)}, bf16[128,1152]{1,0:T(8,128)(2,1)S(1)}, u32[]{:S(2)}, u32[]{:S(2)}) collective-permute-start(bf16[128,1152]{1,0:T(8,128)(2,1)S(1)} %get-tuple-element.222), channel_id=1, source_target_pairs={{0,1},{1,0},{2,3},{3,2},{4,5},{5,4},{6,7},{7,6},{8,9},{9,8},{10,11... | collective-permute-start | bytes 884744 | tf_op jit(solution)/shard_map/ppermute | solution.py:547
  112.7 13.4 %collective-permute-start.38 = (bf16[128,1024]{1,0:T(8,128)(2,1)S(1)}, bf16[128,1024]{1,0:T(8,128)(2,1)S(1)}, u32[]{:S(2)}, u32[]{:S(2)}) collective-permute-start(bf16[128,1024]{1,0:T(8,128)(2,1)S(1)} %get-tuple-element.221), channel_id=1, source_target_pairs={{0,1},{1,0},{2,3},{3,2},{4,5},{5,4},{6,7},{7,6},{8,9},{9,8},{10,11... | collective-permute-start | bytes 786440 | tf_op jit(solution)/shard_map/ppermute | solution.py:547
  116.0 15.9 %collective-permute-start.42 = (bf16[128,2176]{1,0:T(8,128)(2,1)S(1)}, bf16[128,2176]{1,0:T(8,128)(2,1)S(1)}, u32[]{:S(2)}, u32[]{:S(2)}) collective-permute-start(bf16[128,2176]{1,0:T(8,128)(2,1)S(1)} %get-tuple-element.235), channel_id=1, source_target_pairs={{1,2},{2,1},{0,0},{3,3},{5,6},{6,5},{4,4},{7,7},{9,10},{10,9},{8,8... | collective-permute-start | bytes 1671176 | tf_op jit(solution)/shard_map/ppermute | solution.py:547
  116.7 21.0 %collective-permute-start.43 = (bf16[128,2176]{1,0:T(8,128)(2,1)S(1)}, bf16[128,2176]{1,0:T(8,128)(2,1)S(1)}, u32[]{:S(2)}, u32[]{:S(2)}) collective-permute-start(bf16[128,2176]{1,0:T(8,128)(2,1)S(1)} %get-tuple-element.235), channel_id=1, source_target_pairs={{0,1},{3,2},{4,5},{7,6},{8,9},{11,10},{12,13},{15,14},{16,17},{19,... | collective-permute-start | bytes 1671176 | tf_op jit(solution)/shard_map/ppermute | solution.py:547
  126.1 4.6 %collective-permute-start.44 = (bf16[2,512,128]{2,1,0:T(8,128)(2,1)S(1)}, bf16[2,512,128]{2,1,0:T(8,128)(2,1)S(1)}, u32[]{:S(2)}, u32[]{:S(2)}) collective-permute-start(bf16[2,512,128]{2,1,0:T(8,128)(2,1)S(1)} %get-tuple-element.237), channel_id=1, source_target_pairs={{0,4},{4,0},{8,12},{12,8},{16,20},{20,16},{24,28},{28,24},{1,5},{5... | collective-permute-start | bytes 786440 | tf_op jit(solution)/shard_map/ppermute | solution.py:29
  126.9 29.7 %collective-permute-start.41 = (bf16[128,1152]{1,0:T(8,128)(2,1)S(1)}, bf16[128,1152]{1,0:T(8,128)(2,1)S(1)}, u32[]{:S(2)}, u32[]{:S(2)}) collective-permute-start(bf16[128,1152]{1,0:T(8,128)(2,1)S(1)} %add_far.3), channel_id=1, source_target_pairs={{0,2},{1,3},{2,0},{3,1},{4,6},{5,7},{6,4},{7,5},{8,10},{9,11},{10,... | collective-permute-start | bytes 884744 | tf_op jit(solution)/shard_map/ppermute | solution.py:34
  130.7 25.9 %collective-permute-start.40 = (bf16[128,1024]{1,0:T(8,128)(2,1)S(1)}, bf16[128,1024]{1,0:T(8,128)(2,1)S(1)}, u32[]{:S(2)}, u32[]{:S(2)}) collective-permute-start(bf16[128,1024]{1,0:T(8,128)(2,1)S(1)} %add_far.2), channel_id=1, source_target_pairs={{0,2},{1,3},{2,0},{3,1},{4,6},{5,7},{6,4},{7,5},{8,10},{9,11},{10,... | collective-permute-start | bytes 786440 | tf_op jit(solution)/shard_map/ppermute | solution.py:34

commit v2 on v0

--- a/solution.py
+++ b/solution.py
@@ -440,16 +440,13 @@
             gating(sizes, ints_ref, low_states, vecs, side, *sides[side], mine)
 
 
-def is_inner(t):
-    return (t == 1) | (t == 2)
-
-
-def block_places(t, tp_count):
-    if tp_count == 4:
-        inside = is_inner(t)
-        first = jnp.where(inside, t ^ 1, 3 - t)
-        return [first, lax.rem(t + 2, 4), jnp.where(inside, 3 - t, t ^ 1), t]
-    return [lax.rem(t + j, tp_count) for j in range(1, tp_count)] + [t]
+def block_order(tp_count):
+    far = tp_count // 2
+    return [far] + [j for j in range(1, tp_count) if j != far] + [0]
+
+
+def in_halves(by, tp_count):
+    return by not in (0, tp_count // 2)
 
 
 def out_kernel(sizes, ints, mine, theirs, *refs):
@@ -457,8 +454,8 @@
     t, p, c = ints[0], ints[1], ints[2]
     if where:
         pieces = refs[: len(where)]
-        outs = refs[len(where) : len(where) + 2 * len(chosen)]
-        weights, sems = refs[len(where) + 2 * len(chosen) :]
+        outs = refs[len(where) : len(where) + len(chosen)]
+        weights, sems = refs[len(where) + len(chosen) :]
         copies = []
         for i, (piece, (k, other, first)) in enumerate(zip(pieces, where)):
             rows, columns = piece.shape
@@ -476,76 +473,45 @@
     piece_rows = mine.shape[0] // tp_count
     own_rows = rows_at(c * inner, inner)
     other_rows = rows_at((1 - c) * inner, inner)
-    for i, low, high in zip(chosen, outs[::2], outs[1::2]):
-        rows = rows_at(block_places(t, tp_count)[i] * piece_rows, piece_rows)
+    outs = list(outs)
+    for by in chosen:
+        sides = [(outs.pop(0), 0)]
+        if in_halves(by, tp_count):
+            sides.append((outs.pop(0), width // 2))
+        rows = rows_at(lax.rem(t + by, tp_count) * piece_rows, piece_rows)
         sums = jnp.sum(
             mine[rows, inner:].astype(F32) + theirs[rows, inner:].astype(F32), axis=1, keepdims=True
         )
-        sums = spread_terms(jnp.broadcast_to(sums, (piece_rows, LANES)))
-        high[:, width // 2 :] = sums.astype(high.dtype)
+        out, start = sides[-1]
+        terms = spread_terms(jnp.broadcast_to(sums, (piece_rows, LANES)))
+        out[:, width - start :] = terms.astype(out.dtype)
         for at in range(0, width, width // 4):
             lanes = slice(at, at + width // 4)
             value = jnp.dot(mine[rows, :inner], weights[own_rows, lanes], preferred_element_type=F32)
             value = value + jnp.dot(
                 theirs[rows, :inner], weights[other_rows, lanes], preferred_element_type=F32
             )
-            out, first = (low, at) if at < width // 2 else (high, at - width // 2)
-            out[:, first : first + width // 4] = value.astype(out.dtype)
-
-
-def add_kernel(width, ints, got, own, out):
-    inside = is_inner(ints[0])
-    came = jnp.where(inside, got[:, :width].astype(F32), 0.0)
-    out[:, :width] = (came + own[:, :width].astype(F32)).astype(MM)
-    if out.shape[1] > width:
-        came = jnp.where(inside, added_terms(got, width), 0.0)
-        out[:, width:] = spread_terms(came + added_terms(own, width)).astype(MM)
-
-
-def final_kernel(channels, takers, ints, *refs):
-    own, received, out = refs[:2], refs[2:-1], refs[-1]
-    half = out.shape[1] // 2
-    inside = is_inner(ints[0])
-
-    def taken(value, inner):
-        if inner is None:
-            return value
-        return jnp.where(inside, value, 0.0) if inner else jnp.where(inside, 0.0, value)
-
-    squares = added_terms(own[1], half)
-    for got, inner in zip(received[1::2], takers):
-        squares = squares + taken(added_terms(got, half), inner)
+            out, start = sides[at * len(sides) // width]
+            out[:, at - start : at - start + width // 4] = value.astype(out.dtype)
+
+
+def final_kernel(channels, sizes, own, *refs):
+    refs, out = list(refs[:-1]), refs[-1]
+    width = out.shape[1]
+    received = []
+    for size in sizes:
+        low = refs.pop(0)
+        received.append(((low, 0), (refs.pop(0), width // 2)) if size == 2 else ((low, 0),) * 2)
+    squares = added_terms(own, width)
+    for _, (high, start) in received:
+        squares = squares + added_terms(high, width - start)
     factor = lax.rsqrt(squares[:, :1] / channels + epsilon)
-    for side in range(2):
-        total = own[side][:, :half]
-        for got, inner in zip(received[side::2], takers):
-            total = total + taken(got[:, :half].astype(F32), inner)
-        out[:, side * half : (side + 1) * half] = (total * factor).astype(out.dtype)
-
-
-def sum_over_tp(ints, blocks, own):
-    tp_count = lax.axis_size("tp")
-    if tp_count != 4:
-        received = [[shift(x, j + 1) for x in block] for j, block in enumerate(blocks)]
-        return own, received, (None,) * (tp_count - 1)
-
-    def send(block, pairs):
-        return [lax.ppermute(x, "tp", pairs) for x in block]
-
-    def add(got, x, name):
-        kernel = functools.partial(add_kernel, own[0].shape[1])
-        specs = [SMEM, VMEM, VMEM]
-        return call(kernel, [sds(x.shape, MM)], specs, moved=100_000, name=name)(ints, got, x)[0]
-
-    first, second, third = blocks
-    beside = send(first, [(0, 1), (1, 0), (2, 3), (3, 2)])
-    to_middle = send(third, [(1, 2), (2, 1), (0, 0), (3, 3)])
-    to_inner = send(third, [(0, 1), (3, 2)])
-    joined = lax.optimization_barrier((*beside, *second, *own))
-    beside, second, own = list(joined[:2]), joined[2:4], list(joined[4:])
-    second = [add(got, x, "add_far") for got, x in zip(beside, second)]
-    across = [shift(x, 2) for x in second]
-    return own, [beside, across, to_middle, to_inner], (False, None, True, True)
+    for at in range(0, width, width // 4):
+        total = own[:, at : at + width // 4]
+        for sides in received:
+            got, start = sides[at * 2 // width]
+            total = total + got[:, at - start : at - start + width // 4].astype(F32)
+        out[:, at : at + width // 4] = (total * factor).astype(out.dtype)
 
 
 def on_device(
@@ -797,18 +763,20 @@
 
     out_width = seq_count * w_out.shape[1]
     piece = tok_dev // tp_count
-    ahead = 1 if tp_count == 4 else tp_count - 2
-
-    def project_out(chosen, outs, where, operands):
+
+    def project_out(chosen, where, operands):
         scratch, extra = [], []
-        outs = [
-            sds((piece, out_width // 2 + side * LANES), kind) for kind in outs for side in range(2)
-        ]
+        outs = []
+        for by in chosen:
+            if in_halves(by, tp_count):
+                outs += [sds((piece, out_width // 2 + side * LANES), MM) for side in range(2)]
+            else:
+                outs.append(sds((piece, out_width + LANES), MM if by else F32))
         if where:
             extra = [sds((2 * inner, out_width), MM)]
             scratch = [pltpu.SemaphoreType.DMA((len(where),))]
         return call(
-            functools.partial(out_kernel, (inner, tp_count, chosen, where)),
+            functools.partial(out_kernel, (inner, tp_count, tuple(chosen), where)),
             outs + extra,
             [SMEM, VMEM, VMEM] + ([ANY] * len(where) if where else [VMEM]),
             scratch,
@@ -817,21 +785,19 @@
             name="out_%d" % len(chosen),
         )(ints, mine, theirs, *operands)
 
-    *sent_first, out_weights = project_out(tuple(range(ahead)), [MM] * ahead, out_where, out_pieces)
-    *sent_next, own_low, own_high = project_out(
-        tuple(range(ahead, tp_count)), [MM] * (tp_count - 1 - ahead) + [F32], (), [out_weights]
-    )
-    halves = [*sent_first, *sent_next]
-    own, received, takers = sum_over_tp(
-        ints, [halves[i : i + 2] for i in range(0, len(halves), 2)], [own_low, own_high]
-    )
-    received = [half for block in received for half in block]
+    order = block_order(tp_count)
+    far_block, out_weights = project_out(order[:1], out_where, out_pieces)
+    received = [shift(far_block, order[0])]
+    *blocks, own = project_out(order[1:], (), [out_weights])
+    received += [shift(x, order[1 + i // 2]) for i, x in enumerate(blocks)]
+    sizes = (1,) + (2,) * (len(blocks) // 2)
+    own, asked = lax.optimization_barrier((own, asked))
     (mixed,) = call(
-        functools.partial(final_kernel, float(inner_all), takers),
+        functools.partial(final_kernel, float(inner_all), sizes),
         [sds((piece, out_width), MM)],
-        [SMEM] + [VMEM] * (2 + len(received)),
+        [VMEM] * (1 + len(received)),
         name="final",
-    )(ints, *own, *received)
+    )(own, *received)
 
     other_asked = flip(asked, 1).astype(F32)
     states = jnp.where(

time: 159 us -> 163 us (1.025)
  the two profiles are of different devices: /device:TPU:0 before, /device:TPU:17 now
where the time goes in v2:
time: 163 us
  waiting for transfers between devices  76.1 us (47%)
  starting transfers between devices  41.6 us (26%)
  Pallas kernels  34.2 us (21%)
  other arithmetic  5.37 us (3%)
  local copies, waits for them, and re-layouts  4.19 us (3%)
    ppermute x11, waiting for transfers between devices, shift(): return lax.ppermute(x, 'tp', [(i, (i + by) % count) for i in range(count)])  53.5 us
    ppermute x32, starting transfers between devices, flip(): return lax.ppermute(x, 'seq', [(i, i ^ bits) for i in range(count)])  29.9 us
    ppermute x32, waiting for transfers between devices, flip(): return lax.ppermute(x, 'seq', [(i, i ^ bits) for i in range(count)])  22.6 us
    pallas_call x2, Pallas kernels, front(): call(functools.partial(front_kernel, (inner, bc_width, heads, prompts, wh...  12.2 us
    ppermute x11, starting transfers between devices, shift(): return lax.ppermute(x, 'tp', [(i, (i + by) % count) for i in range(count)])  9.48 us
    pallas_call x2, Pallas kernels, on_device(): call(functools.partial(gate_kernel, chosen, 2 * depth, len(gate) > 0), [s...  5.07 us
    pallas_call x2, Pallas kernels, mid(): call(functools.partial(mid_kernel, (inner, heads, prompts, groups, side))...  4.89 us
    pallas_call x2, Pallas kernels, project_out(): call(functools.partial(out_kernel, (inner, tp_count, tuple(chosen), where...  4.41 us
  transfers between devices with their start and end apart: 44, of which 21 were waited for; matrix products, arithmetic and copies ran while one was open for 4% of the time, Pallas kernels for 17%

profile of v2, /device:TPU:17, one launch (start us, length us, event | category | flops | bytes accessed | tf_op | source)
XLA Modules:
  0.0 162.5 jit_solution(16185314641109920860)
XLA Ops:
  0.7 0.7 collective-permute-start.5
  1.4 1.3 convert_element_type.10.refs_0_
  2.7 1.3 collective-permute-start.3
  4.0 1.2 collective-permute-start.4
  5.2 0.7 concatenate.18.ints.ints_ref
  6.0 1.6 copy-done
  7.6 0.8 copy-done.2
  8.4 0.8 copy-done.3
  9.2 0.9 pack_x.1
  10.0 1.3 collective-permute-start
  11.6 1.3 collective-permute-start.2
  12.9 2.5 %broadcast_select_fusion = (bf16[512,2048]{1,0:T(8,128)(2,1)S(1)}, bf16[512,2048]{1,0:T(8,128)(2,1)S(1)}) fusion(bf16[512,2048]{1,0:T(8,128)(2,1)} %collective-permute-done.5, bf16[512,2048]{1,0:T(8,128)(2,1)} %param.15, pred[]{:T(512)S(6)} %eq.4), kind=kLoop, calls=%fused_computation.1 | loop fusion | flops 2097152 | bytes 8388609 | tf_op jit(solution)/shard_map/jit(_where)/select_n | solution.py:608
  15.4 0.9 collective-permute-done.3.refs_1_
  16.3 0.9 collective-permute-done.4.refs_2_
  17.2 2.2 %collective-permute-start.8 = (bf16[16,2048]{1,0:T(8,128)(2,1)S(1)}, bf16[16,2048]{1,0:T(8,128)(2,1)S(1)}, u32[]{:S(2)}, u32[]{:S(2)}) collective-permute-start(bf16[16,2048]{1,0:T(8,128)(2,1)S(1)} %slice.23), channel_id=1, source_target_pairs={{0,8},{4,12},{8,16},{12,20},{16,24},{20,28},{1,9},{5,13},{9,17},{1... | collective-permute-start | bytes 196616 | tf_op jit(solution)/shard_map/ppermute | solution.py:620
  19.6 2.2 %collective-permute-start.6 = (bf16[512,256]{1,0:T(8,128)(2,1)S(1)}, bf16[512,256]{1,0:T(8,128)(2,1)S(1)}, u32[]{:S(2)}, u32[]{:S(2)}) collective-permute-start(bf16[512,256]{1,0:T(8,128)(2,1)S(1)} %slice.21), channel_id=1, source_target_pairs={{0,8},{4,12},{8,0},{12,4},{16,24},{20,28},{24,16},{28,20},{1,9},{5... | collective-permute-start | bytes 786440 | tf_op jit(solution)/shard_map/ppermute | solution.py:29
  21.8 2.6 %collective-permute-start.7 = (bf16[512,256]{1,0:T(8,128)(2,1)S(1)}, bf16[512,256]{1,0:T(8,128)(2,1)S(1)}, u32[]{:S(2)}, u32[]{:S(2)}) collective-permute-start(bf16[512,256]{1,0:T(8,128)(2,1)S(1)} %slice.22), channel_id=1, source_target_pairs={{0,16},{4,20},{8,24},{12,28},{16,0},{20,4},{24,8},{28,12},{1,17},{... | collective-permute-start | bytes 786440 | tf_op jit(solution)/shard_map/ppermute | solution.py:29
  24.8 2.2 %collective-permute-done.2.refs_3_ = bf16[64,1408]{1,0:T(8,128)(2,1)S(1)} collective-permute-done((bf16[64,1408]{1,0:T(8,128)(2,1)S(1)}, bf16[64,1408]{1,0:T(8,128)(2,1)S(1)}, u32[]{:S(2)}, u32[]{:S(2)}) %collective-permute-start.2) | collective-permute-done | bytes 180256 | tf_op jit(solution)/shard_map/ppermute | solution.py:34
  26.9 1.2 collective-permute-done.6.refs_3_
  28.4 0.6 assemble_x.1.refs_0_
  29.0 1.2 collective-permute-start.10
  30.3 0.6 pack_z.1
  30.9 1.4 collective-permute-start.11
  32.3 1.3 collective-permute-start.13
  33.6 1.1 collective-permute-done.11.refs_1_
  34.7 2.3 %collective-permute-done.12.refs_2_ = bf16[64,1024]{1,0:T(8,128)(2,1)S(1)} collective-permute-done((bf16[64,1024]{1,0:T(8,128)(2,1)S(1)}, bf16[64,1024]{1,0:T(8,128)(2,1)S(1)}, u32[]{:S(2)}, u32[]{:S(2)}) %collective-permute-start.12) | collective-permute-done | bytes 131104 | tf_op jit(solution)/shard_map/ppermute | solution.py:34
  37.1 4.8 %collective-permute-done.13.refs_3_ = bf16[64,1024]{1,0:T(8,128)(2,1)S(1)} collective-permute-done((bf16[64,1024]{1,0:T(8,128)(2,1)S(1)}, bf16[64,1024]{1,0:T(8,128)(2,1)S(1)}, u32[]{:S(2)}, u32[]{:S(2)}) %collective-permute-start.13) | collective-permute-done | bytes 131104 | tf_op jit(solution)/shard_map/ppermute | solution.py:34
  41.9 0.8 collective-permute-done.10.refs_2_
  43.1 5.7 %collective-permute-start.16 = (bf16[256,1408]{1,0:T(8,128)(2,1)S(1)}, bf16[256,1408]{1,0:T(8,128)(2,1)S(1)}, u32[]{:S(2)}, u32[]{:S(2)}) collective-permute-start(bf16[256,1408]{1,0:T(8,128)(2,1)S(1)} %collective-permute-done.9.refs_1_), channel_id=1, source_target_pairs={{0,4},{4,0},{8,12},{12,8},{16,20},{20,16},{24,28},{28,24},{1,5},{5... | collective-permute-start | bytes 2162696 | tf_op jit(solution)/shard_map/ppermute | solution.py:29
  48.8 0.6 assemble_z.1
  50.6 1.4 collective-permute-done.18.theirs
  52.9 0.6 merge_z.1.refs_0_
  53.5 6.6 %collective-permute-done.14.refs_3_ = bf16[128,1408]{1,0:T(8,128)(2,1)S(1)} collective-permute-done((bf16[128,1408]{1,0:T(8,128)(2,1)S(1)}, bf16[128,1408]{1,0:T(8,128)(2,1)S(1)}, u32[]{:S(2)}, u32[]{:S(2)}) %collective-permute-start.14) | collective-permute-done | bytes 360480 | tf_op jit(solution)/shard_map/ppermute | solution.py:29
  60.1 0.9 collective-permute-start.20
  62.3 1.4 collective-permute-start.24
  64.1 6.5 %front_0.1 = (bf16[512,512]{1,0:T(8,128)(2,1)S(1)}, bf16[512,256]{1,0:T(8,128)(2,1)S(1)}, f32[512,128]{1,0:T(8,128)S(1)}, f32[512,128]{1,0:T(8,128)S(1)}, bf16[2...) custom-call(s32[27]{0:T(128)S(1)} %concatenate.18.ints.ints_ref, f32[48]{0:T(128)S(1)} %pad_maximum_fusion.1.floats, ...), custom_call_target="tpu_custom_call" | custom-call | bytes 1000000 | tf_op jit(solution)/shard_map/front_0/pallas_call | solution.py:665
  71.2 1.1 collective-permute-start.23
  72.2 5.7 %front_1.1 = (bf16[512,512]{1,0:T(8,128)(2,1)S(1)}, bf16[512,256]{1,0:T(8,128)(2,1)S(1)}, f32[512,128]{1,0:T(8,128)S(1)}, f32[512,128]{1,0:T(8,128)S(1)}, bf16[2,544,128]{2,1,0:T(8,128)(2,1)S(1)}) custom-call(s32[27]{0:T(128)S(1)} %concatenate.18.ints.ints_ref, f32[48]{0:T(128)S(1)} %pad_maximum_fusion.1.floats, f32[16,1024]{1,0:T(8,128)S(1)} %concatenate.21.vecs, ...), custom_call_target="tpu_custom_call" | custom-call | bytes 1000000 | tf_op jit(solution)/shard_map/front_1/pallas_call | solution.py:665
  78.0 3.4 %collective-permute-done.22.refs_2_ = bf16[2,544,128]{2,1,0:T(8,128)(2,1)S(1)} collective-permute-done((bf16[2,544,128]{2,1,0:T(8,128)(2,1)S(1)}, bf16[2,544,128]{2,1,0:T(8,128)(2,1)S(1)}, u32[]{:S(2)}, u32[]{:S(2)}) %collective-permute-start.22) | collective-permute-done | bytes 278560 | tf_op jit(solution)/shard_map/ppermute | solution.py:29
  81.4 1.1 collective-permute-done.23.refs_4_
  82.5 0.8 collective-permute-start.31
  83.7 0.7 collective-permute-start.35
  84.5 1.1 collective-permute-start.36
  85.6 2.4 %mid_0.1 = (f32[512,512]{1,0:T(8,128)S(1)}, f32[512,512]{1,0:T(8,128)S(1)}) custom-call(s32[27]{0:T(128)S(1)} %concatenate.18.ints.ints_ref, f32[48]{0:T(128)S(1)} %pad_maximum_fusion.1.floats, bf16[512,512]{1,0:T(8,128)(2,1)S(1)} %get-tuple-element.166.xs_ref, bf16[512,256]{1,0:T(8,128)(2,1)S(1)} %get-tuple-element.203.bc_ref.refs_11_.refs_3_, ...), custom_call_target="tpu_custom_call" | custom-call | flops 134217728 | bytes 1000000 | tf_op jit(solution)/shard_map/mid_0/pallas_call | solution.py:698
  88.0 0.9 collective-permute-start.33
  89.1 0.9 collective-permute-done.32.refs_5_
  90.4 2.4 %mid_1.1 = (f32[512,512]{1,0:T(8,128)S(1)}, f32[512,512]{1,0:T(8,128)S(1)}) custom-call(s32[27]{0:T(128)S(1)} %concatenate.18.ints.ints_ref, f32[48]{0:T(128)S(1)} %pad_maximum_fusion.1.floats, bf16[512,512]{1,0:T(8,128)(2,1)S(1)} %get-tuple-element.185.xs_ref, bf16[512,256]{1,0:T(8,128)(2,1)S(1)} %get-tuple-element.207.bc_ref.refs_15_.refs_7_, ...), custom_call_target="tpu_custom_call" | custom-call | flops 134217728 | bytes 1000000 | tf_op jit(solution)/shard_map/mid_1/pallas_call | solution.py:698
  92.8 2.9 %gate_0.1 = (f32[512,512]{1,0:T(8,128)S(1)}, f32[512,512]{1,0:T(8,128)S(1)}) custom-call(s32[27]{0:T(128)S(1)} %concatenate.18.ints.ints_ref, bf16[1040,2048]{1,0:T(8,128)(2,1)S(1)} %pad_maximum_fusion.tok_ref, bf16[512,512]{1,0:T(8,128)(2,1)S(1)} %merge_z.1.refs_0_, bf16[512,512]{1,0:T(8,128)(2,1)S(1)} %collective-permute-done.24.refs_1_, ...), custom_call_target="tpu_custom_call" | custom-call | flops 268435456 | bytes 1000000 | tf_op jit(solution)/shard_map/gate_0/pallas_call | solution.py:723
  95.7 2.2 %gate_1.1 = (f32[512,512]{1,0:T(8,128)S(1)}, f32[512,512]{1,0:T(8,128)S(1)}) custom-call(s32[27]{0:T(128)S(1)} %concatenate.18.ints.ints_ref, bf16[1040,2048]{1,0:T(8,128)(2,1)S(1)} %pad_maximum_fusion.tok_ref, bf16[256,512]{1,0:T(8,128)(2,1)S(1)} %collective-permute-done.35.refs_0_, bf16[256,512]{1,0:T(8,128)(2,1)S(1)} %collective-permute-done.36.refs_1_, ...), custom_call_target="tpu_custom_call" | custom-call | flops 268435456 | bytes 1000000 | tf_op jit(solution)/shard_map/gate_1/pallas_call | solution.py:723
  97.9 2.8 %collective-permute-done.33.refs_6_ = bf16[2,544,128]{2,1,0:T(8,128)(2,1)S(1)} collective-permute-done((bf16[2,544,128]{2,1,0:T(8,128)(2,1)S(1)}, bf16[2,544,128]{2,1,0:T(8,128)(2,1)S(1)}, u32[]{:S(2)}, u32[]{:S(2)}) %collective-permute-start.33) | collective-permute-done | bytes 278560 | tf_op jit(solution)/shard_map/ppermute | solution.py:29
  100.7 0.9 collective-permute-done.34.refs_7_
  101.6 2.2 %back.1 = (bf16[512,640]{1,0:T(8,128)(2,1)S(1)}, bf16[4,512,128]{2,1,0:T(8,128)(2,1)S(1)}, bf16[2,512,128]{2,1,0:T(8,128)(2,1)S(1)}, f32[2,512,128]{2,1,0:T(8,128)S(1)}) custom-call(s32[27]{0:T(128)S(1)} %concatenate.18.ints.ints_ref, f32[16,1024]{1,0:T(8,128)S(1)} %concatenate.21.vecs, bf16[2,544,128]{2,1,0:T(8,128)(2,1)S(1)} %get-tuple-element.192.refs_0_, ...), custom_call_target="tpu_custom_call" | custom-call | flops 134217728 | bytes 8000000 | tf_op jit(solution)/shard_map/back/pallas_call | solution.py:736
  103.8 2.5 %collective-permute-start.37 = (bf16[512,640]{1,0:T(8,128)(2,1)S(1)}, bf16[512,640]{1,0:T(8,128)(2,1)S(1)}, u32[]{:S(2)}, u32[]{:S(2)}) collective-permute-start(bf16[512,640]{1,0:T(8,128)(2,1)S(1)} %get-tuple-element.209), channel_id=1, source_target_pairs={{0,4},{4,0},{8,12},{12,8},{16,20},{20,16},{24,28},{28,24},{1,5},{5... | collective-permute-start | bytes 1966088 | tf_op jit(solution)/shard_map/ppermute | solution.py:29
  106.2 1.1 back_own.1.mine
  107.3 0.6 collective-permute-done.37.theirs
  107.9 2.0 %out_1.1 = (bf16[128,2176]{1,0:T(8,128)(2,1)S(1)}, bf16[1024,2048]{1,0:T(8,128)(2,1)S(1)}) custom-call(s32[27]{0:T(128)S(1)} %concatenate.18.ints.ints_ref, bf16[512,640]{1,0:T(8,128)(2,1)S(1)} %back_own.1.mine, bf16[512,640]{1,0:T(8,128)(2,1)S(1)} %collective-permute-done.37.theirs, bf16[1024,256]{1,0:T(8,128)(2,1)S(1)} %convert_element_type.10.refs_0_, ...), custom_call_target="tpu_custom_call" | custom-call | flops 134217728 | bytes 1000000 | tf_op jit(solution)/shard_map/out_1/pallas_call | solution.py:778
  110.3 2.4 %out_3.1 = (bf16[128,1024]{1,0:T(8,128)(2,1)S(1)}, bf16[128,1152]{1,0:T(8,128)(2,1)S(1)}, bf16[128,1024]{1,0:T(8,128)(2,1)S(1)}, bf16[128,1152]{1,0:T(8,128)(2,1)S(1)}, f32[128,2176]{1,0:T(8,128)S(1)}) custom-call(s32[27]{0:T(128)S(1)} %concatenate.18.ints.ints_ref, bf16[512,640]{1,0:T(8,128)(2,1)S(1)} %back_own.1.mine, ...), custom_call_target="tpu_custom_call" | custom-call | flops 671088640 | bytes 1000000 | tf_op jit(solution)/shard_map/out_3/pallas_call | solution.py:778
  112.8 0.7 collective-permute-start.43
  113.5 1.0 collective-permute-start.40
  114.5 1.2 collective-permute-start.42
  115.7 1.0 collective-permute-start.39
  117.2 1.1 maximum_select_fusion
  118.3 43.0 %collective-permute-done.39.refs_1_ = bf16[128,1024]{1,0:T(8,128)(2,1)S(1)} collective-permute-done((bf16[128,1024]{1,0:T(8,128)(2,1)S(1)}, bf16[128,1024]{1,0:T(8,128)(2,1)S(1)}, u32[]{:S(2)}, u32[]{:S(2)}) %collective-permute-start.39) | collective-permute-done | bytes 262176 | tf_op jit(solution)/shard_map/ppermute | solution.py:34
  161.3 1.2 final.1
  (82 shorter events, 7.7 us)
Async XLA Ops:
  0.6 10.8 %copy-start.7 = (f32[4,256]{1,0:T(4,128)S(1)}, f32[4,256]{1,0:T(4,128)}, u32[]{:S(2)}) copy-start(f32[4,256]{1,0:T(4,128)} %param.21) | copy-start | bytes 12292
  0.6 10.8 %copy-start.8 = (f32[256]{0:T(256)S(1)}, f32[256]{0:T(256)}, u32[]{:S(2)}) copy-start(f32[256]{0:T(256)} %param.22) | copy-start | bytes 3076
  0.7 10.8 %copy-start.5 = (f32[1024]{0:T(1024)S(1)}, f32[1024]{0:T(1024)}, u32[]{:S(2)}) copy-start(f32[1024]{0:T(1024)} %param.20) | copy-start | bytes 12292
  0.7 10.8 %copy-start.6 = (f32[1024]{0:T(1024)S(1)}, f32[1024]{0:T(1024)}, u32[]{:S(2)}) copy-start(f32[1024]{0:T(1024)} %param.26) | copy-start | bytes 12292
  0.7 10.8 %copy-start.4 = (f32[4,1024]{1,0:T(4,128)S(1)}, f32[4,1024]{1,0:T(4,128)}, u32[]{:S(2)}) copy-start(f32[4,1024]{1,0:T(4,128)} %param.19) | copy-start | bytes 49156
  0.7 10.9 %collective-permute-start.5 = (bf16[512,2048]{1,0:T(8,128)(2,1)}, bf16[512,2048]{1,0:T(8,128)(2,1)}, u32[]{:S(2)}, u32[]{:S(2)}) collective-permute-start(bf16[512,2048]{1,0:T(8,128)(2,1)} %param.15), channel_id=1, source_target_pairs={{0,4},{4,0},{8,12},{12,8},{16,20},{20,16},{24,28},{28,24},{1,5},{5... | collective-permute-start | bytes 6291464 | tf_op jit(solution)/shard_map/ppermute | solution.py:29
  2.7 13.6 %collective-permute-start.3 = (bf16[1024,256]{1,0:T(8,128)(2,1)S(1)}, bf16[1024,256]{1,0:T(8,128)(2,1)S(1)}, u32[]{:S(2)}, u32[]{:S(2)}) collective-permute-start(bf16[1024,256]{1,0:T(8,128)(2,1)S(1)} %convert_element_type.10.refs_0_), channel_id=1, source_target_pairs={{0,8},{4,12},{8,0},{12,4},{16,24},{20,28},{24,16},{28,20},{1,9},{5... | collective-permute-start | bytes 1572872 | tf_op jit(solution)/shard_map/ppermute | solution.py:29
  4.0 13.2 %collective-permute-start.4 = (bf16[1024,256]{1,0:T(8,128)(2,1)S(1)}, bf16[1024,256]{1,0:T(8,128)(2,1)S(1)}, u32[]{:S(2)}, u32[]{:S(2)}) collective-permute-start(bf16[1024,256]{1,0:T(8,128)(2,1)S(1)} %convert_element_type.10.refs_0_), channel_id=1, source_target_pairs={{0,16},{4,20},{8,24},{12,28},{16,0},{20,4},{24,8},{28,12},{1,17},{... | collective-permute-start | bytes 1572872 | tf_op jit(solution)/shard_map/ppermute | solution.py:29
  6.0 1.6 copy-start
  7.6 0.8 copy-start.2
  8.4 0.8 copy-start.3
  10.0 14.7 %collective-permute-start = (bf16[64,1408]{1,0:T(8,128)(2,1)S(1)}, bf16[64,1408]{1,0:T(8,128)(2,1)S(1)}, u32[]{:S(2)}, u32[]{:S(2)}) collective-permute-start(bf16[64,1408]{1,0:T(8,128)(2,1)S(1)} %get-tuple-element.115), channel_id=1, source_target_pairs={{0,1},{1,2},{2,3},{3,0},{4,5},{5,6},{6,7},{7,4},{8,9},{9,10},{10,1... | collective-permute-start | bytes 540680 | tf_op jit(solution)/shard_map/ppermute | solution.py:34
  11.4 13.4 %collective-permute-start.1 = (bf16[64,1408]{1,0:T(8,128)(2,1)S(1)}, bf16[64,1408]{1,0:T(8,128)(2,1)S(1)}, u32[]{:S(2)}, u32[]{:S(2)}) collective-permute-start(bf16[64,1408]{1,0:T(8,128)(2,1)S(1)} %get-tuple-element.116), channel_id=1, source_target_pairs={{0,2},{1,3},{2,0},{3,1},{4,6},{5,7},{6,4},{7,5},{8,10},{9,11},{10,... | collective-permute-start | bytes 540680 | tf_op jit(solution)/shard_map/ppermute | solution.py:34
  11.6 7.9 %copy-start.9 = (f32[16]{0:T(128)S(1)}, f32[16]{0:T(128)}, u32[]{:S(2)}) copy-start(f32[16]{0:T(128)} %param.25) | copy-start | bytes 196
  11.6 7.9 %copy-start.10 = (f32[16]{0:T(128)S(1)}, f32[16]{0:T(128)}, u32[]{:S(2)}) copy-start(f32[16]{0:T(128)} %param.24) | copy-start | bytes 196
  11.6 7.9 %copy-start.11 = (f32[16]{0:T(128)S(1)}, f32[16]{0:T(128)}, u32[]{:S(2)}) copy-start(f32[16]{0:T(128)} %param.23) | copy-start | bytes 196
  11.6 15.3 %collective-permute-start.2 = (bf16[64,1408]{1,0:T(8,128)(2,1)S(1)}, bf16[64,1408]{1,0:T(8,128)(2,1)S(1)}, u32[]{:S(2)}, u32[]{:S(2)}) collective-permute-start(bf16[64,1408]{1,0:T(8,128)(2,1)S(1)} %get-tuple-element.117), channel_id=1, source_target_pairs={{0,3},{1,0},{2,1},{3,2},{4,7},{5,4},{6,5},{7,6},{8,11},{9,8},{10,9... | collective-permute-start | bytes 540680 | tf_op jit(solution)/shard_map/ppermute | solution.py:34
  17.2 4.6 %collective-permute-start.8 = (bf16[16,2048]{1,0:T(8,128)(2,1)S(1)}, bf16[16,2048]{1,0:T(8,128)(2,1)S(1)}, u32[]{:S(2)}, u32[]{:S(2)}) collective-permute-start(bf16[16,2048]{1,0:T(8,128)(2,1)S(1)} %slice.23), channel_id=1, source_target_pairs={{0,8},{4,12},{8,16},{12,20},{16,24},{20,28},{1,9},{5,13},{9,17},{1... | collective-permute-start | bytes 196616 | tf_op jit(solution)/shard_map/ppermute | solution.py:620
  19.6 8.6 %collective-permute-start.6 = (bf16[512,256]{1,0:T(8,128)(2,1)S(1)}, bf16[512,256]{1,0:T(8,128)(2,1)S(1)}, u32[]{:S(2)}, u32[]{:S(2)}) collective-permute-start(bf16[512,256]{1,0:T(8,128)(2,1)S(1)} %slice.21), channel_id=1, source_target_pairs={{0,8},{4,12},{8,0},{12,4},{16,24},{20,28},{24,16},{28,20},{1,9},{5... | collective-permute-start | bytes 786440 | tf_op jit(solution)/shard_map/ppermute | solution.py:29
  21.7 8.5 %copy-start.1 = (f32[64,8192]{1,0:T(8,128)S(1)}, f32[64,8192]{1,0:T(8,128)}, u32[]{:S(2)}) copy-start(f32[64,8192]{1,0:T(8,128)} %w_ref.3) | copy-start | bytes 6291460
  21.8 6.6 %collective-permute-start.7 = (bf16[512,256]{1,0:T(8,128)(2,1)S(1)}, bf16[512,256]{1,0:T(8,128)(2,1)S(1)}, u32[]{:S(2)}, u32[]{:S(2)}) collective-permute-start(bf16[512,256]{1,0:T(8,128)(2,1)S(1)} %slice.22), channel_id=1, source_target_pairs={{0,16},{4,20},{8,24},{12,28},{16,0},{20,4},{24,8},{28,12},{1,17},{... | collective-permute-start | bytes 786440 | tf_op jit(solution)/shard_map/ppermute | solution.py:29
  29.0 13.8 %collective-permute-start.10 = (bf16[256,1408]{1,0:T(8,128)(2,1)S(1)}, bf16[256,1408]{1,0:T(8,128)(2,1)S(1)}, u32[]{:S(2)}, u32[]{:S(2)}) collective-permute-start(bf16[256,1408]{1,0:T(8,128)(2,1)S(1)} %assemble_x.1.refs_0_), channel_id=1, source_target_pairs={{0,16},{4,20},{8,24},{12,28},{16,0},{20,4},{24,8},{28,12},{1,17},{... | collective-permute-start | bytes 2162696 | tf_op jit(solution)/shard_map/ppermute | solution.py:29
  30.2 12.8 %collective-permute-start.9 = (bf16[256,1408]{1,0:T(8,128)(2,1)S(1)}, bf16[256,1408]{1,0:T(8,128)(2,1)S(1)}, u32[]{:S(2)}, u32[]{:S(2)}) collective-permute-start(bf16[256,1408]{1,0:T(8,128)(2,1)S(1)} %assemble_x.1.refs_0_), channel_id=1, source_target_pairs={{0,8},{4,12},{8,0},{12,4},{16,24},{20,28},{24,16},{28,20},{1,9},{5... | collective-permute-start | bytes 2162696 | tf_op jit(solution)/shard_map/ppermute | solution.py:29
  30.9 3.9 %collective-permute-start.11 = (bf16[64,1024]{1,0:T(8,128)(2,1)S(1)}, bf16[64,1024]{1,0:T(8,128)(2,1)S(1)}, u32[]{:S(2)}, u32[]{:S(2)}) collective-permute-start(bf16[64,1024]{1,0:T(8,128)(2,1)S(1)} %get-tuple-element.133), channel_id=1, source_target_pairs={{0,1},{1,2},{2,3},{3,0},{4,5},{5,6},{6,7},{7,4},{8,9},{9,10},{10,1... | collective-permute-start | bytes 393224 | tf_op jit(solution)/shard_map/ppermute | solution.py:34
  32.3 4.8 %collective-permute-start.12 = (bf16[64,1024]{1,0:T(8,128)(2,1)S(1)}, bf16[64,1024]{1,0:T(8,128)(2,1)S(1)}, u32[]{:S(2)}, u32[]{:S(2)}) collective-permute-start(bf16[64,1024]{1,0:T(8,128)(2,1)S(1)} %get-tuple-element.134), channel_id=1, source_target_pairs={{0,2},{1,3},{2,0},{3,1},{4,6},{5,7},{6,4},{7,5},{8,10},{9,11},{10,... | collective-permute-start | bytes 393224 | tf_op jit(solution)/shard_map/ppermute | solution.py:34
  32.3 9.6 %collective-permute-start.13 = (bf16[64,1024]{1,0:T(8,128)(2,1)S(1)}, bf16[64,1024]{1,0:T(8,128)(2,1)S(1)}, u32[]{:S(2)}, u32[]{:S(2)}) collective-permute-start(bf16[64,1024]{1,0:T(8,128)(2,1)S(1)} %get-tuple-element.135), channel_id=1, source_target_pairs={{0,3},{1,0},{2,1},{3,2},{4,7},{5,4},{6,5},{7,6},{8,11},{9,8},{10,9... | collective-permute-start | bytes 393224 | tf_op jit(solution)/shard_map/ppermute | solution.py:34
  43.1 9.3 %collective-permute-start.16 = (bf16[256,1408]{1,0:T(8,128)(2,1)S(1)}, bf16[256,1408]{1,0:T(8,128)(2,1)S(1)}, u32[]{:S(2)}, u32[]{:S(2)}) collective-permute-start(bf16[256,1408]{1,0:T(8,128)(2,1)S(1)} %collective-permute-done.9.refs_1_), channel_id=1, source_target_pairs={{0,4},{4,0},{8,12},{12,8},{16,20},{20,16},{24,28},{28,24},{1,5},{5... | collective-permute-start | bytes 2162696 | tf_op jit(solution)/shard_map/ppermute | solution.py:29
  48.8 3.7 %collective-permute-start.17 = (bf16[256,1408]{1,0:T(8,128)(2,1)S(1)}, bf16[256,1408]{1,0:T(8,128)(2,1)S(1)}, u32[]{:S(2)}, u32[]{:S(2)}) collective-permute-start(bf16[256,1408]{1,0:T(8,128)(2,1)S(1)} %collective-permute-done.10.refs_2_), channel_id=1, source_target_pairs={{0,4},{4,0},{8,12},{12,8},{16,20},{20,16},{24,28},{28,24},{1,5},{5... | collective-permute-start | bytes 2162696 | tf_op jit(solution)/shard_map/ppermute | solution.py:29
  49.4 2.6 %collective-permute-start.18 = (bf16[256,512]{1,0:T(8,128)(2,1)S(1)}, bf16[256,512]{1,0:T(8,128)(2,1)S(1)}, u32[]{:S(2)}, u32[]{:S(2)}) collective-permute-start(bf16[256,512]{1,0:T(8,128)(2,1)S(1)} %get-tuple-element.143), channel_id=1, source_target_pairs={{0,4},{4,0},{8,12},{12,8},{16,20},{20,16},{24,28},{28,24},{1,5},{5... | collective-permute-start | bytes 786440 | tf_op jit(solution)/shard_map/ppermute | solution.py:29
  50.0 10.1 %collective-permute-start.14 = (bf16[128,1408]{1,0:T(8,128)(2,1)S(1)}, bf16[128,1408]{1,0:T(8,128)(2,1)S(1)}, u32[]{:S(2)}, u32[]{:S(2)}) collective-permute-start(bf16[128,1408]{1,0:T(8,128)(2,1)S(1)} %slice.24), channel_id=1, source_target_pairs={{0,8},{4,12},{8,0},{12,4},{16,24},{20,28},{24,16},{28,20},{1,9},{5... | collective-permute-start | bytes 1081352 | tf_op jit(solution)/shard_map/ppermute | solution.py:29
  50.1 10.0 %collective-permute-start.15 = (bf16[128,1408]{1,0:T(8,128)(2,1)S(1)}, bf16[128,1408]{1,0:T(8,128)(2,1)S(1)}, u32[]{:S(2)}, u32[]{:S(2)}) collective-permute-start(bf16[128,1408]{1,0:T(8,128)(2,1)S(1)} %slice.25), channel_id=1, source_target_pairs={{0,16},{4,20},{8,24},{12,28},{16,0},{20,4},{24,8},{28,12},{1,17},{... | collective-permute-start | bytes 1081352 | tf_op jit(solution)/shard_map/ppermute | solution.py:29
  52.0 9.6 %collective-permute-start.19 = (bf16[256,1408]{1,0:T(8,128)(2,1)S(1)}, bf16[256,1408]{1,0:T(8,128)(2,1)S(1)}, u32[]{:S(2)}, u32[]{:S(2)}) collective-permute-start(bf16[256,1408]{1,0:T(8,128)(2,1)S(1)} %assemble_x.1.refs_0_), channel_id=1, source_target_pairs={{0,4},{4,0},{8,12},{12,8},{16,20},{20,16},{24,28},{28,24},{1,5},{5... | collective-permute-start | bytes 2162696 | tf_op jit(solution)/shard_map/ppermute | solution.py:29
  52.4 8.6 %collective-permute-start.29 = (bf16[512,256]{1,0:T(8,128)(2,1)S(1)}, bf16[512,256]{1,0:T(8,128)(2,1)S(1)}, u32[]{:S(2)}, u32[]{:S(2)}) collective-permute-start(bf16[512,256]{1,0:T(8,128)(2,1)S(1)} %collective-permute-done.6.refs_3_), channel_id=1, source_target_pairs={{0,4},{4,0},{8,12},{12,8},{16,20},{20,16},{24,28},{28,24},{1,5},{5... | collective-permute-start | bytes 786440 | tf_op jit(solution)/shard_map/ppermute | solution.py:29
  52.5 9.0 %collective-permute-start.30 = (bf16[512,256]{1,0:T(8,128)(2,1)S(1)}, bf16[512,256]{1,0:T(8,128)(2,1)S(1)}, u32[]{:S(2)}, u32[]{:S(2)}) collective-permute-start(bf16[512,256]{1,0:T(8,128)(2,1)S(1)} %collective-permute-done.7.refs_4_), channel_id=1, source_target_pairs={{0,4},{4,0},{8,12},{12,8},{16,20},{20,16},{24,28},{28,24},{1,5},{5... | collective-permute-start | bytes 786440 | tf_op jit(solution)/shard_map/ppermute | solution.py:29
  60.1 2.2 %collective-permute-start.20 = (bf16[128,1408]{1,0:T(8,128)(2,1)S(1)}, bf16[128,1408]{1,0:T(8,128)(2,1)S(1)}, u32[]{:S(2)}, u32[]{:S(2)}) collective-permute-start(bf16[128,1408]{1,0:T(8,128)(2,1)S(1)} %collective-permute-done.14.refs_3_), channel_id=1, source_target_pairs={{0,4},{4,0},{8,12},{12,8},{16,20},{20,16},{24,28},{28,24},{1,5},{5... | collective-permute-start | bytes 1081352 | tf_op jit(solution)/shard_map/ppermute | solution.py:29
  61.0 2.7 %collective-permute-start.21 = (bf16[128,1408]{1,0:T(8,128)(2,1)S(1)}, bf16[128,1408]{1,0:T(8,128)(2,1)S(1)}, u32[]{:S(2)}, u32[]{:S(2)}) collective-permute-start(bf16[128,1408]{1,0:T(8,128)(2,1)S(1)} %collective-permute-done.15.refs_4_), channel_id=1, source_target_pairs={{0,4},{4,0},{8,12},{12,8},{16,20},{20,16},{24,28},{28,24},{1,5},{5... | collective-permute-start | bytes 1081352 | tf_op jit(solution)/shard_map/ppermute | solution.py:29
  61.0 9.6 %collective-permute-start.26 = (bf16[1024,256]{1,0:T(8,128)(2,1)S(1)}, bf16[1024,256]{1,0:T(8,128)(2,1)S(1)}, u32[]{:S(2)}, u32[]{:S(2)}) collective-permute-start(bf16[1024,256]{1,0:T(8,128)(2,1)S(1)} %convert_element_type.10.refs_0_), channel_id=1, source_target_pairs={{0,4},{4,0},{8,12},{12,8},{16,20},{20,16},{24,28},{28,24},{1,5},{5... | collective-permute-start | bytes 1572872 | tf_op jit(solution)/shard_map/ppermute | solution.py:29
  61.5 9.7 %collective-permute-start.27 = (bf16[1024,256]{1,0:T(8,128)(2,1)S(1)}, bf16[1024,256]{1,0:T(8,128)(2,1)S(1)}, u32[]{:S(2)}, u32[]{:S(2)}) collective-permute-start(bf16[1024,256]{1,0:T(8,128)(2,1)S(1)} %collective-permute-done.3.refs_1_), channel_id=1, source_target_pairs={{0,4},{4,0},{8,12},{12,8},{16,20},{20,16},{24,28},{28,24},{1,5},{5... | collective-permute-start | bytes 1572872 | tf_op jit(solution)/shard_map/ppermute | solution.py:29
  61.6 16.4 %collective-permute-start.28 = (bf16[1024,256]{1,0:T(8,128)(2,1)S(1)}, bf16[1024,256]{1,0:T(8,128)(2,1)S(1)}, u32[]{:S(2)}, u32[]{:S(2)}) collective-permute-start(bf16[1024,256]{1,0:T(8,128)(2,1)S(1)} %collective-permute-done.4.refs_2_), channel_id=1, source_target_pairs={{0,4},{4,0},{8,12},{12,8},{16,20},{20,16},{24,28},{28,24},{1,5},{5... | collective-permute-start | bytes 1572872 | tf_op jit(solution)/shard_map/ppermute | solution.py:29
  62.3 15.7 %collective-permute-start.24 = (bf16[512,512]{1,0:T(8,128)(2,1)S(1)}, bf16[512,512]{1,0:T(8,128)(2,1)S(1)}, u32[]{:S(2)}, u32[]{:S(2)}) collective-permute-start(bf16[512,512]{1,0:T(8,128)(2,1)S(1)} %merge_z.1.refs_0_), channel_id=1, source_target_pairs={{0,8},{4,12},{8,0},{12,4},{16,24},{20,28},{24,16},{28,20},{1,9},{5... | collective-permute-start | bytes 1572872 | tf_op jit(solution)/shard_map/ppermute | solution.py:29
  63.7 14.3 %collective-permute-start.25 = (bf16[512,512]{1,0:T(8,128)(2,1)S(1)}, bf16[512,512]{1,0:T(8,128)(2,1)S(1)}, u32[]{:S(2)}, u32[]{:S(2)}) collective-permute-start(bf16[512,512]{1,0:T(8,128)(2,1)S(1)} %merge_z.1.refs_0_), channel_id=1, source_target_pairs={{0,16},{4,20},{8,24},{12,28},{16,0},{20,4},{24,8},{28,12},{1,17},{... | collective-permute-start | bytes 1572872 | tf_op jit(solution)/shard_map/ppermute | solution.py:29
  70.6 10.8 %collective-permute-start.22 = (bf16[2,544,128]{2,1,0:T(8,128)(2,1)S(1)}, bf16[2,544,128]{2,1,0:T(8,128)(2,1)S(1)}, u32[]{:S(2)}, u32[]{:S(2)}) collective-permute-start(bf16[2,544,128]{2,1,0:T(8,128)(2,1)S(1)} %get-tuple-element.192.refs_0_), channel_id=1, source_target_pairs={{0,8},{4,12},{8,0},{12,4},{16,24},{20,28},{24,16},{28,20},{1,9},{5... | collective-permute-start | bytes 835592 | tf_op jit(solution)/shard_map/ppermute | solution.py:29
  71.2 11.3 %collective-permute-start.23 = (bf16[2,544,128]{2,1,0:T(8,128)(2,1)S(1)}, bf16[2,544,128]{2,1,0:T(8,128)(2,1)S(1)}, u32[]{:S(2)}, u32[]{:S(2)}) collective-permute-start(bf16[2,544,128]{2,1,0:T(8,128)(2,1)S(1)} %get-tuple-element.192.refs_0_), channel_id=1, source_target_pairs={{0,16},{4,20},{8,24},{12,28},{16,0},{20,4},{24,8},{28,12},{1,17},{... | collective-permute-start | bytes 835592 | tf_op jit(solution)/shard_map/ppermute | solution.py:29
  82.5 6.6 %collective-permute-start.31 = (bf16[2,544,128]{2,1,0:T(8,128)(2,1)S(1)}, bf16[2,544,128]{2,1,0:T(8,128)(2,1)S(1)}, u32[]{:S(2)}, u32[]{:S(2)}) collective-permute-start(bf16[2,544,128]{2,1,0:T(8,128)(2,1)S(1)} %get-tuple-element.193.refs_1_), channel_id=1, source_target_pairs={{0,8},{4,12},{8,0},{12,4},{16,24},{20,28},{24,16},{28,20},{1,9},{5... | collective-permute-start | bytes 835592 | tf_op jit(solution)/shard_map/ppermute | solution.py:29
  83.3 6.7 %collective-permute-start.32 = (bf16[2,544,128]{2,1,0:T(8,128)(2,1)S(1)}, bf16[2,544,128]{2,1,0:T(8,128)(2,1)S(1)}, u32[]{:S(2)}, u32[]{:S(2)}) collective-permute-start(bf16[2,544,128]{2,1,0:T(8,128)(2,1)S(1)} %get-tuple-element.193.refs_1_), channel_id=1, source_target_pairs={{0,16},{4,20},{8,24},{12,28},{16,0},{20,4},{24,8},{28,12},{1,17},{... | collective-permute-start | bytes 835592 | tf_op jit(solution)/shard_map/ppermute | solution.py:29
  83.7 12.0 %collective-permute-start.35 = (bf16[256,512]{1,0:T(8,128)(2,1)S(1)}, bf16[256,512]{1,0:T(8,128)(2,1)S(1)}, u32[]{:S(2)}, u32[]{:S(2)}) collective-permute-start(bf16[256,512]{1,0:T(8,128)(2,1)S(1)} %slice.26), channel_id=1, source_target_pairs={{0,8},{4,12},{8,0},{12,4},{16,24},{20,28},{24,16},{28,20},{1,9},{5... | collective-permute-start | bytes 786440 | tf_op jit(solution)/shard_map/ppermute | solution.py:29
  84.5 11.3 %collective-permute-start.36 = (bf16[256,512]{1,0:T(8,128)(2,1)S(1)}, bf16[256,512]{1,0:T(8,128)(2,1)S(1)}, u32[]{:S(2)}, u32[]{:S(2)}) collective-permute-start(bf16[256,512]{1,0:T(8,128)(2,1)S(1)} %slice.27), channel_id=1, source_target_pairs={{0,16},{4,20},{8,24},{12,28},{16,0},{20,4},{24,8},{28,12},{1,17},{... | collective-permute-start | bytes 786440 | tf_op jit(solution)/shard_map/ppermute | solution.py:29
  88.0 12.7 %collective-permute-start.33 = (bf16[2,544,128]{2,1,0:T(8,128)(2,1)S(1)}, bf16[2,544,128]{2,1,0:T(8,128)(2,1)S(1)}, u32[]{:S(2)}, u32[]{:S(2)}) collective-permute-start(bf16[2,544,128]{2,1,0:T(8,128)(2,1)S(1)} %collective-permute-done.23.refs_4_), channel_id=1, source_target_pairs={{0,8},{4,12},{8,0},{12,4},{16,24},{20,28},{24,16},{28,20},{1,9},{5... | collective-permute-start | bytes 835592 | tf_op jit(solution)/shard_map/ppermute | solution.py:29
  90.0 11.6 %collective-permute-start.34 = (bf16[2,544,128]{2,1,0:T(8,128)(2,1)S(1)}, bf16[2,544,128]{2,1,0:T(8,128)(2,1)S(1)}, u32[]{:S(2)}, u32[]{:S(2)}) collective-permute-start(bf16[2,544,128]{2,1,0:T(8,128)(2,1)S(1)} %collective-permute-done.31.refs_3_), channel_id=1, source_target_pairs={{0,16},{4,20},{8,24},{12,28},{16,0},{20,4},{24,8},{28,12},{1,17},{... | collective-permute-start | bytes 835592 | tf_op jit(solution)/shard_map/ppermute | solution.py:29
  103.8 4.2 %collective-permute-start.37 = (bf16[512,640]{1,0:T(8,128)(2,1)S(1)}, bf16[512,640]{1,0:T(8,128)(2,1)S(1)}, u32[]{:S(2)}, u32[]{:S(2)}) collective-permute-start(bf16[512,640]{1,0:T(8,128)(2,1)S(1)} %get-tuple-element.209), channel_id=1, source_target_pairs={{0,4},{4,0},{8,12},{12,8},{16,20},{20,16},{24,28},{28,24},{1,5},{5... | collective-permute-start | bytes 1966088 | tf_op jit(solution)/shard_map/ppermute | solution.py:29
  109.9 51.4 %collective-permute-start.38 = (bf16[128,2176]{1,0:T(8,128)(2,1)S(1)}, bf16[128,2176]{1,0:T(8,128)(2,1)S(1)}, u32[]{:S(2)}, u32[]{:S(2)}) collective-permute-start(bf16[128,2176]{1,0:T(8,128)(2,1)S(1)} %get-tuple-element.219), channel_id=1, source_target_pairs={{0,2},{1,3},{2,0},{3,1},{4,6},{5,7},{6,4},{7,5},{8,10},{9,11},{10,... | collective-permute-start | bytes 1671176 | tf_op jit(solution)/shard_map/ppermute | solution.py:34
  112.8 3.9 %collective-permute-start.43 = (bf16[2,512,128]{2,1,0:T(8,128)(2,1)S(1)}, bf16[2,512,128]{2,1,0:T(8,128)(2,1)S(1)}, u32[]{:S(2)}, u32[]{:S(2)}) collective-permute-start(bf16[2,512,128]{2,1,0:T(8,128)(2,1)S(1)} %get-tuple-element.225), channel_id=1, source_target_pairs={{0,4},{4,0},{8,12},{12,8},{16,20},{20,16},{24,28},{28,24},{1,5},{5... | collective-permute-start | bytes 786440 | tf_op jit(solution)/shard_map/ppermute | solution.py:29
  113.5 47.8 %collective-permute-start.40 = (bf16[128,1152]{1,0:T(8,128)(2,1)S(1)}, bf16[128,1152]{1,0:T(8,128)(2,1)S(1)}, u32[]{:S(2)}, u32[]{:S(2)}) collective-permute-start(bf16[128,1152]{1,0:T(8,128)(2,1)S(1)} %get-tuple-element.221), channel_id=1, source_target_pairs={{0,1},{1,2},{2,3},{3,0},{4,5},{5,6},{6,7},{7,4},{8,9},{9,10},{10,1... | collective-permute-start | bytes 884744 | tf_op jit(solution)/shard_map/ppermute | solution.py:34
  114.5 46.8 %collective-permute-start.42 = (bf16[128,1152]{1,0:T(8,128)(2,1)S(1)}, bf16[128,1152]{1,0:T(8,128)(2,1)S(1)}, u32[]{:S(2)}, u32[]{:S(2)}) collective-permute-start(bf16[128,1152]{1,0:T(8,128)(2,1)S(1)} %get-tuple-element.223), channel_id=1, source_target_pairs={{0,3},{1,0},{2,1},{3,2},{4,7},{5,4},{6,5},{7,6},{8,11},{9,8},{10,9... | collective-permute-start | bytes 884744 | tf_op jit(solution)/shard_map/ppermute | solution.py:34
  115.7 45.6 %collective-permute-start.39 = (bf16[128,1024]{1,0:T(8,128)(2,1)S(1)}, bf16[128,1024]{1,0:T(8,128)(2,1)S(1)}, u32[]{:S(2)}, u32[]{:S(2)}) collective-permute-start(bf16[128,1024]{1,0:T(8,128)(2,1)S(1)} %get-tuple-element.220), channel_id=1, source_target_pairs={{0,1},{1,2},{2,3},{3,0},{4,5},{5,6},{6,7},{7,4},{8,9},{9,10},{10,1... | collective-permute-start | bytes 786440 | tf_op jit(solution)/shard_map/ppermute | solution.py:34
  116.7 44.6 %collective-permute-start.41 = (bf16[128,1024]{1,0:T(8,128)(2,1)S(1)}, bf16[128,1024]{1,0:T(8,128)(2,1)S(1)}, u32[]{:S(2)}, u32[]{:S(2)}) collective-permute-start(bf16[128,1024]{1,0:T(8,128)(2,1)S(1)} %get-tuple-element.222), channel_id=1, source_target_pairs={{0,3},{1,0},{2,1},{3,2},{4,7},{5,4},{6,5},{7,6},{8,11},{9,8},{10,9... | collective-permute-start | bytes 786440 | tf_op jit(solution)/shard_map/ppermute | solution.py:34
